TPU v7x, 32 devices: a whole 2x2x4 slice. The times are simulated.
32 devices in a mesh: row: 8 (over z, core), col: 4 (over y, x).
Axes of the slice: x: 2, y: 2, z: 4, core: 2. Of those that a mesh axis runs over, the one named last changes fastest.
Arguments:
- tokens: bfloat16 [2048, 8192], P('row', 'col'), may hold values from -6 to 6
- out_grad: bfloat16 [2048, 8192], P('row', 'col'), may hold values from -1.5 to 1.5
- gate_weight: bfloat16 [112, 1024, 128], P('col', 'row'), may hold values from -0.1875 to 0.1875
- up_weight: bfloat16 [112, 1024, 128], P('col', 'row'), may hold values from -0.1875 to 0.1875
- down_weight: bfloat16 [112, 1024, 128], P('col', 'row'), may hold values from -0.125 to 0.125
- gate_rows: int32 [112, 8], P('col'), may hold values from 0 to 63, all different within a row
- up_rows: int32 [112, 8], P('col'), may hold values from 0 to 63, all different within a row
- down_columns: int32 [112, 8], P('col'), may hold values from 0 to 63, all different within a row
Outputs:
- output: bfloat16 [2048, 8192], P('row', 'col')
- input_grad: bfloat16 [2048, 8192], P('row', 'col')
- gate_weight_grad: bfloat16 [112, 1024, 128], P('col', 'row')
- up_weight_grad: bfloat16 [112, 1024, 128], P('col', 'row')
- down_weight_grad: bfloat16 [112, 1024, 128], P('col', 'row')
Inputs may be any that keep to these rules, and one draw needn't show every extreme that they name: `gate_rows`: each row names 8 different block-rows; every block-row is named in some row. `up_rows`: each row names 8 different block-rows; every block-row is named in some row. `down_columns`: each row names 8 different output block-columns; every block-column is named in some row.
All inputs are finite; a program needn't handle non-finite values.
Results may differ from a plain program's by a relative error of at most 0.018.
Values may be sent and summed in bfloat16 or wider, within the bound.
No kernel may reach another device: no remote copies, remote signals or barrier semaphores. Data moves between devices by JAX's collectives and lax.ppermute only.
A program may use at most 192 MiB of HBM per device.

v0:
```python
import jax
import jax.numpy as jnp
from jax import lax
from jax.sharding import PartitionSpec as P

D = 8192
BS = 128
KG = 8
KH = 8
DB = 64


def spread(contrib, block_lists):
    rows_here = contrib.shape[0]
    zero_block = jnp.zeros((rows_here, DB, BS), jnp.float32)
    placed = zero_block.at[:, block_lists.reshape(-1)].add(contrib.reshape(rows_here, -1, BS))
    return placed.reshape(rows_here, D)


def shards(tokens, out_grad, gate_weight, up_weight, down_weight, gate_rows, up_rows, down_columns):
    panel_in, panel_grad = (
        lax.all_gather(tokens, "col", axis=1, tiled=True),
        lax.all_gather(out_grad, "col", axis=1, tiled=True),
    )
    rows_here = panel_in.shape[0]
    gate_tiles, up_tiles, down_tiles = (
        lax.all_gather(gate_weight, "row", axis=1, tiled=True),
        lax.all_gather(up_weight, "row", axis=1, tiled=True),
        lax.all_gather(down_weight, "row", axis=1, tiled=True),
    )
    owned_slots = gate_tiles.shape[0]
    gate_four = gate_tiles.reshape(owned_slots, KG, BS, BS)
    up_four = up_tiles.reshape(owned_slots, KG, BS, BS)
    blocks_in = panel_in.reshape(rows_here, DB, BS)
    picked_gate = jnp.take(blocks_in, gate_rows.reshape(-1), axis=1).reshape(
        rows_here, owned_slots, KG, BS
    )
    picked_up = jnp.take(blocks_in, up_rows.reshape(-1), axis=1).reshape(
        rows_here, owned_slots, KG, BS
    )
    gate_value = jnp.einsum(
        "tfkr,fkri->tfi", picked_gate, gate_four, preferred_element_type=jnp.float32
    )
    up_value = jnp.einsum("tfkr,fkri->tfi", picked_up, up_four, preferred_element_type=jnp.float32)
    sigmoid_gate = jax.nn.sigmoid(gate_value)
    silu_gate = gate_value * sigmoid_gate
    hidden = (silu_gate * up_value).astype(jnp.bfloat16)
    down_four = down_tiles.reshape(owned_slots, KH, BS, BS)
    out_part = jnp.einsum("tfi,fkji->tfkj", hidden, down_four, preferred_element_type=jnp.float32)
    partial_out = spread(out_part, down_columns)
    out_sum = lax.psum_scatter(
        partial_out.astype(jnp.bfloat16), "col", scatter_dimension=1, tiled=True
    )
    blocks_grad = panel_grad.reshape(rows_here, DB, BS)
    picked_grad = jnp.take(blocks_grad, down_columns.reshape(-1), axis=1).reshape(
        rows_here, owned_slots, KH, BS
    )
    hidden_grad = jnp.einsum(
        "tfkj,fkji->tfi", picked_grad, down_four, preferred_element_type=jnp.float32
    )
    gate_grad = (
        hidden_grad * up_value * sigmoid_gate * (1.0 + gate_value * (1.0 - sigmoid_gate))
    ).astype(jnp.bfloat16)
    up_grad = (hidden_grad * silu_gate).astype(jnp.bfloat16)
    from_gate = jnp.einsum(
        "tfi,fkri->tfkr", gate_grad, gate_four, preferred_element_type=jnp.float32
    )
    from_up = jnp.einsum("tfi,fkri->tfkr", up_grad, up_four, preferred_element_type=jnp.float32)
    partial_in = spread(from_gate, gate_rows) + spread(from_up, up_rows)
    gate_partial = jnp.einsum(
        "tfkr,tfi->fkri", picked_gate, gate_grad, preferred_element_type=jnp.float32
    ).reshape(owned_slots, KG * BS, BS)
    up_partial = jnp.einsum(
        "tfkr,tfi->fkri", picked_up, up_grad, preferred_element_type=jnp.float32
    ).reshape(owned_slots, KG * BS, BS)
    down_partial = jnp.einsum(
        "tfkj,tfi->fkji", picked_grad, hidden, preferred_element_type=jnp.float32
    ).reshape(owned_slots, KH * BS, BS)
    gate_sum, up_sum, down_sum = (
        lax.psum_scatter(
            gate_partial.astype(jnp.bfloat16), "row", scatter_dimension=1, tiled=True
        ).astype(jnp.float32),
        lax.psum_scatter(
            up_partial.astype(jnp.bfloat16), "row", scatter_dimension=1, tiled=True
        ).astype(jnp.float32),
        lax.psum_scatter(
            down_partial.astype(jnp.bfloat16), "row", scatter_dimension=1, tiled=True
        ).astype(jnp.float32),
    )
    in_sum = lax.psum_scatter(
        partial_in.astype(jnp.bfloat16), "col", scatter_dimension=1, tiled=True
    )
    return (
        out_sum,
        in_sum,
        gate_sum.astype(jnp.bfloat16),
        up_sum.astype(jnp.bfloat16),
        down_sum.astype(jnp.bfloat16),
    )


def solution(mesh):
    in_specs = (
        P("row", "col"),
        P("row", "col"),
        P("col", "row", None),
        P("col", "row", None),
        P("col", "row", None),
        P("col", None),
        P("col", None),
        P("col", None),
    )
    out_specs = (
        P("row", "col"),
        P("row", "col"),
        P("col", "row", None),
        P("col", "row", None),
        P("col", "row", None),
    )
    return jax.shard_map(shards, mesh=mesh, in_specs=in_specs, out_specs=out_specs, check_vma=False)
```

profile of v0, /device:TPU:0, one launch (start us, length us, event | category | flops | bytes accessed | tf_op | source)
XLA Modules:
  0.0 954.4 jit_solution(2175223832987647120)
XLA Ops:
  15.2 50.6 %all-gather.6.cloned.1.call-done = bf16[256,8192]{0,1:T(8,128)(2,1)} async-done(((bf16[256,2048]{0,1:T(8,128)(2,1)}), bf16[256,8192]{0,1:T(8,128)(2,1)}) %all-gather.6.cloned.1.call-update) | async-done | bytes 4194320 | tf_op jit(solution)/shard_map/all_gather | solution.py:22
  65.9 6.4 copy.35
  72.3 48.8 %all-gather.14.cloned.1.call-done = bf16[256,8192]{0,1:T(8,128)(2,1)} async-done(((bf16[256,2048]{0,1:T(8,128)(2,1)}), bf16[256,8192]{0,1:T(8,128)(2,1)}) %all-gather.14.cloned.1.call-update) | async-done | bytes 4194320 | tf_op jit(solution)/shard_map/all_gather | solution.py:23
  121.0 6.4 copy.42
  127.4 11.5 %gather_fusion.1 = bf16[224,256,128]{2,1,0:T(8,128)(2,1)} fusion(bf16[256,64,128]{2,0,1:T(8,128)(2,1)} %copy.35, s32[1024]{0:T(1024)S(1)} %pad_clamp_fusion.1), kind=kCustom, calls=%fused_computation.1.clone | custom fusion | bytes 29361024 | tf_op jit(solution)/shard_map/jit(_take)/gather | solution.py:38
  138.9 11.4 %gather_fusion = bf16[224,256,128]{2,1,0:T(8,128)(2,1)} fusion(bf16[256,64,128]{2,0,1:T(8,128)(2,1)} %copy.35, s32[1024]{0:T(1024)S(1)} %pad_clamp_fusion.2), kind=kCustom, calls=%fused_computation.clone | custom fusion | bytes 29361024 | tf_op jit(solution)/shard_map/jit(_take)/gather | solution.py:35
  150.4 11.5 %gather_fusion.2 = bf16[224,256,128]{2,1,0:T(8,128)(2,1)} fusion(bf16[256,64,128]{2,0,1:T(8,128)(2,1)} %copy.42, s32[1024]{0:T(1024)S(1)} %pad_clamp_fusion), kind=kCustom, calls=%fused_computation.2.clone | custom fusion | bytes 29361024 | tf_op jit(solution)/shard_map/jit(_take)/gather | solution.py:55
  161.8 14.9 %broadcast_select_fusion = bf16[224,256,128]{2,1,0:T(8,128)(2,1)} fusion(bf16[224,256,128]{2,1,0:T(8,128)(2,1)} %gather_fusion.2, pred[224]{0:T(512)(128)(4,1)S(1)} %compare_and_fusion), kind=kLoop, calls=%fused_computation.6 | loop fusion | flops 7340032 | bytes 29360352 | tf_op jit(solution)/shard_map/jit(_take)/select_n | solution.py:55
  176.7 14.6 %broadcast_select_fusion.1 = bf16[224,256,128]{2,1,0:T(8,128)(2,1)} fusion(bf16[224,256,128]{2,1,0:T(8,128)(2,1)} %gather_fusion.1, pred[224]{0:T(512)(128)(4,1)S(1)} %compare_and_fusion.1), kind=kLoop, calls=%fused_computation.7 | loop fusion | flops 7340032 | bytes 29360352 | tf_op jit(solution)/shard_map/jit(_take)/select_n | solution.py:38
  191.3 6.7 broadcast_select_fusion.2
  198.1 14.1 %fusion.15 = f32[28,256,128,1]{2,1,3,0:T(8,128)} fusion(bf16[256,28,8,128]{3,0,2,1:T(8,128)(2,1)} %bitcast.122, bf16[28,8,128,128]{3,2,1,0:T(8,128)(2,1)} %bitcast.135), kind=kOutput, calls=%fused_computation.46 | convolution fusion | flops 1879048192 | bytes 25690112 | tf_op jit(solution)/shard_map/tfkr,fkri->tfi/dot_general | solution.py:44
  212.2 57.4 %all-gather.8.cloned.1.call-done = bf16[28,1024,128]{2,1,0:T(8,128)(2,1)} async-done(((bf16[28,128,128]{2,1,0:T(8,128)(2,1)}), bf16[28,1024,128]{2,1,0:T(8,128)(2,1)}) %all-gather.8.cloned.1.call-update) | async-done | bytes 7340048 | tf_op jit(solution)/shard_map/all_gather | solution.py:27
  269.6 13.2 %fusion.14 = f32[28,256,128,1]{2,1,3,0:T(8,128)} fusion(bf16[256,28,8,128]{3,0,2,1:T(8,128)(2,1)} %bitcast.124, bf16[28,8,128,128]{3,2,1,0:T(8,128)(2,1)} %bitcast.137), kind=kOutput, calls=%fused_computation.45 | convolution fusion | flops 1879048192 | bytes 25690112 | tf_op jit(solution)/shard_map/tfkr,fkri->tfi/dot_general | solution.py:41
  282.8 60.2 %all-gather.12.cloned.1.call-done = bf16[28,1024,128]{2,1,0:T(8,128)(2,1)} async-done(((bf16[28,128,128]{2,1,0:T(8,128)(2,1)}), bf16[28,1024,128]{2,1,0:T(8,128)(2,1)}) %all-gather.12.cloned.1.call-update) | async-done | bytes 7340048 | tf_op jit(solution)/shard_map/all_gather | solution.py:29
  343.0 15.5 %fusion.10 = (bf16[256,28,128,1]{2,0,3,1:T(8,128)(2,1)S(1)}, bf16[256,28,128]{2,0,1:T(8,128)(2,1)}, bf16[256,28,128,1]{2,0,3,1:T(8,128)(2,1)}) fusion(f32[28,256,128,1]{2,1,3,0:T(8,128)} %fusion.14, f32[28,256,128,1]{2,1,3,0:T(8,128)} %fusion.15, bf16[256,28,8,128]{3,0,2,1:T(8,128)(2,1)} %bitcast.126, bf16[28,8,128,128]{3,2,1,0:T(8,128)(2,1)} %bitcast.133), kind=kOutput, calls=%fused_computation.29 | convolution fusion | flops 1892810752 | bytes 34865152 | tf_op jit(solution)/shard_map/tfkj,fkji->tfi/dot_general | solution.py:58
  358.5 15.3 %fusion.17 = f32[28,256,8,128]{3,1,2,0:T(8,128)} fusion(bf16[256,28,128,1]{2,0,3,1:T(8,128)(2,1)S(1)} %get-tuple-element.16, bf16[28,8,128,128]{3,2,1,0:T(8,128)(2,1)} %bitcast.136), kind=kOutput, calls=%fused_computation.48 | convolution fusion | flops 1879048192 | bytes 38535168 | tf_op jit(solution)/shard_map/tfi,fkri->tfkr/dot_general | solution.py:68
  373.8 17.3 %fusion.12 = f32[28,256,8,128]{3,1,2,0:T(8,128)} fusion(bf16[28,8,128,128]{3,2,1,0:T(8,128)(2,1)} %bitcast.138, bf16[256,28,128]{2,0,1:T(8,128)(2,1)} %get-tuple-element.17), kind=kOutput, calls=%fused_computation.31 | convolution fusion | flops 1879048192 | bytes 38535168 | tf_op jit(solution)/shard_map/tfi,fkri->tfkr/dot_general | solution.py:65
  395.5 66.9 %scatter_fusion.2 = f32[256,64,128]{2,0,1:T(8,128)} fusion(f32[256,64,128]{2,0,1:T(8,128)} %broadcast.57.clone.2, s32[224]{0:T(256)S(1)} %bitcast.144, f32[224,256,128]{2,1,0:T(8,128)} %bitcast.120), kind=kCustom, calls=%fused_computation.5 | custom fusion | flops 7340032 | bytes 88081280 | tf_op jit(solution)/shard_map/scatter-add | solution.py:16
  466.8 67.3 %scatter_fusion.1 = f32[256,64,128]{2,0,1:T(8,128)} fusion(f32[256,64,128]{2,0,1:T(8,128)} %broadcast.57.clone.1, s32[224]{0:T(256)S(1)} %bitcast.143, f32[224,256,128]{2,1,0:T(8,128)} %bitcast.119), kind=kCustom, calls=%fused_computation.4 | custom fusion | flops 7340032 | bytes 88081280 | tf_op jit(solution)/shard_map/scatter-add | solution.py:16
  534.2 9.8 %add_convert_fusion = bf16[256,64,128]{2,0,1:T(8,128)(2,1)} fusion(f32[256,64,128]{2,0,1:T(8,128)} %scatter_fusion.1, f32[256,64,128]{2,0,1:T(8,128)} %scatter_fusion.2), kind=kLoop, calls=%fused_computation.9 | loop fusion | flops 4194304 | bytes 20971520 | tf_op jit(solution)/shard_map/convert_element_type | solution.py:91
  544.0 6.9 copy.44
  551.1 15.2 %fusion.16 = f32[28,256,8,128]{3,1,2,0:T(8,128)} fusion(bf16[256,28,128,1]{2,0,3,1:T(8,128)(2,1)S(1)} %copy-done.3, bf16[28,8,128,128]{3,2,1,0:T(8,128)(2,1)} %bitcast.134), kind=kOutput, calls=%fused_computation.47 | convolution fusion | flops 1879048192 | bytes 38535168 | tf_op jit(solution)/shard_map/tfi,fkji->tfkj/dot_general | solution.py:49
  570.8 67.4 %scatter_fusion = f32[256,64,128]{2,0,1:T(8,128)} fusion(f32[256,64,128]{2,0,1:T(8,128)} %broadcast.57.clone, s32[224]{0:T(256)S(1)} %bitcast.145, f32[224,256,128]{2,1,0:T(8,128)} %bitcast.121), kind=kCustom, calls=%fused_computation.3 | custom fusion | flops 7340032 | bytes 88081280 | tf_op jit(solution)/shard_map/scatter-add | solution.py:16
  638.2 6.1 convert_element_type.46
  644.3 6.4 copy.38
  650.8 9.5 convolution_convert_fusion
  661.8 9.9 %convolution_convert_fusion.2 = bf16[28,8,128,128]{3,2,1,0:T(8,128)(2,1)} fusion(bf16[256,28,8,128]{3,0,2,1:T(8,128)(2,1)} %bitcast.125, bf16[256,28,128]{2,0,1:T(8,128)(2,1)S(1)} %copy-done.2), kind=kOutput, calls=%fused_computation.12 | convolution fusion | flops 1882718208 | bytes 23855104 | tf_op jit(solution)/shard_map/tfkr,tfi->fkri/dot_general | solution.py:70
  673.2 9.8 %convolution_convert_fusion.1 = bf16[28,8,128,128]{3,2,1,0:T(8,128)(2,1)} fusion(bf16[256,28,8,128]{3,0,2,1:T(8,128)(2,1)} %bitcast.123, bf16[256,28,128,1]{2,0,3,1:T(8,128)(2,1)S(1)} %copy-done.1), kind=kOutput, calls=%fused_computation.11 | convolution fusion | flops 1882718208 | bytes 23855104 | tf_op jit(solution)/shard_map/tfkr,tfi->fkri/dot_general | solution.py:73
  685.4 17.6 %reduce-scatter.6.cloned.1.call-done = bf16[256,2048]{0,1:T(8,128)(2,1)} async-done(((bf16[256,8192]{0,1:T(8,128)(2,1)}), bf16[256,2048]{0,1:T(8,128)(2,1)}) %reduce-scatter.6.cloned.1.call-update) | async-done | bytes 1048592 | tf_op jit(solution)/shard_map/reduce_scatter | solution.py:51
  705.2 80.4 %reduce-scatter.14.cloned.1.call-done = bf16[28,128,128]{2,1,0:T(8,128)(2,1)} async-done(((bf16[28,1024,128]{2,1,0:T(8,128)(2,1)}), bf16[28,128,128]{2,1,0:T(8,128)(2,1)}) %reduce-scatter.14.cloned.1.call-update) | async-done | bytes 917520 | tf_op jit(solution)/shard_map/reduce_scatter | solution.py:86
  785.6 81.0 %reduce-scatter.10.cloned.1.call-done = bf16[28,128,128]{2,1,0:T(8,128)(2,1)} async-done(((bf16[28,1024,128]{2,1,0:T(8,128)(2,1)}), bf16[28,128,128]{2,1,0:T(8,128)(2,1)}) %reduce-scatter.10.cloned.1.call-update) | async-done | bytes 917520 | tf_op jit(solution)/shard_map/reduce_scatter | solution.py:80
  866.6 80.8 %reduce-scatter.12.cloned.1.call-done = bf16[28,128,128]{2,1,0:T(8,128)(2,1)} async-done(((bf16[28,1024,128]{2,1,0:T(8,128)(2,1)}), bf16[28,128,128]{2,1,0:T(8,128)(2,1)}) %reduce-scatter.12.cloned.1.call-update) | async-done | bytes 917520 | tf_op jit(solution)/shard_map/reduce_scatter | solution.py:83
  (79 shorter events, 28.9 us)
Async XLA Ops:
  7.2 6.7 copy-start.7
  7.2 6.9 copy-start.8
  7.2 7.2 copy-start.9
  7.2 58.7 %all-gather.6.cloned.1.call-start = ((), (), s32[]{:S(2)}) async-start(), calls=%async_computation.5 | async-start | bytes 5242880 | tf_op jit(solution)/shard_map/all_gather | solution.py:22
  9.5 111.5 %all-gather.14.cloned.1.call-start = ((), (), s32[]{:S(2)}) async-start(), calls=%async_computation.10 | async-start | bytes 5242880 | tf_op jit(solution)/shard_map/all_gather | solution.py:23
  11.9 186.2 %all-gather.10.cloned.1.call-start = ((), (), s32[]{:S(2)}) async-start(), calls=%async_computation.7 | async-start | bytes 8257536 | tf_op jit(solution)/shard_map/all_gather | solution.py:28
  12.6 256.9 %all-gather.8.cloned.1.call-start = ((), (), s32[]{:S(2)}) async-start(), calls=%async_computation.6 | async-start | bytes 8257536 | tf_op jit(solution)/shard_map/all_gather | solution.py:27
  13.2 329.9 %all-gather.12.cloned.1.call-start = ((), (), s32[]{:S(2)}) async-start(), calls=%async_computation.8 | async-start | bytes 8257536 | tf_op jit(solution)/shard_map/all_gather | solution.py:29
  13.8 669.3 %reduce-scatter.8.cloned.1.call-start = ((), (), s32[]{:S(2)}) async-start(), calls=%async_computation.11 | async-start | bytes 5242880 | tf_op jit(solution)/shard_map/reduce_scatter | solution.py:90
  14.5 112.9 %copy-start.4 = (s32[28,8]{1,0:T(8,128)}, s32[28,8]{1,0:T(8,128)S(1)}, u32[]{:S(2)}) copy-start(s32[28,8]{1,0:T(8,128)S(1)} %copy.32) | copy-start | bytes 2692
  161.8 29.5 %slice-start = ((s8[14680064]{0:T(1024)(128)(4,1)}), s8[4194304]{0:T(1024)(128)(4,1)S(1)}, s32[]{:S(2)}) async-start(s8[14680064]{0:T(1024)(128)(4,1)} %bitcast.128), calls=%async_computation.15 | async-start | bytes 8388608
  161.8 29.5 %slice-start.1 = ((s8[14680064]{0:T(1024)(128)(4,1)}), s8[4194304]{0:T(1024)(128)(4,1)S(1)}, s32[]{:S(2)}) async-start(s8[14680064]{0:T(1024)(128)(4,1)} %bitcast.128), calls=%async_computation.16 | async-start | bytes 8388608
  176.7 14.6 %slice-start.2 = ((s8[14680064]{0:T(1024)(128)(4,1)}), s8[4194304]{0:T(1024)(128)(4,1)S(1)}, s32[]{:S(2)}) async-start(s8[14680064]{0:T(1024)(128)(4,1)} %bitcast.128), calls=%async_computation.17 | async-start | bytes 8388608
  176.7 14.6 %slice-start.3 = ((s8[14680064]{0:T(1024)(128)(4,1)}), s8[2097152]{0:T(1024)(128)(4,1)S(1)}, s32[]{:S(2)}) async-start(s8[14680064]{0:T(1024)(128)(4,1)} %bitcast.128), calls=%async_computation.18 | async-start | bytes 4194304
  358.5 15.3 %copy-start = (bf16[256,28,128,1]{2,0,3,1:T(8,128)(2,1)}, bf16[256,28,128,1]{2,0,3,1:T(8,128)(2,1)S(1)}, u32[]{:S(2)}) copy-start(bf16[256,28,128,1]{2,0,3,1:T(8,128)(2,1)S(1)} %get-tuple-element.16) | copy-start | bytes 5505028
  462.4 4.4 copy-start.6
  544.0 7.0 copy-start.5
  544.0 7.1 copy-start.3
  551.0 152.0 %reduce-scatter.6.cloned.1.call-start = ((), (), s32[]{:S(2)}) async-start(), calls=%async_computation.9 | async-start | bytes 5242880 | tf_op jit(solution)/shard_map/reduce_scatter | solution.py:51
  650.7 134.9 %reduce-scatter.14.cloned.1.call-start = ((), (), s32[]{:S(2)}) async-start(), calls=%async_computation.14 | async-start | bytes 8257536 | tf_op jit(solution)/shard_map/reduce_scatter | solution.py:86
  660.3 1.5 copy-start.2
  660.3 206.3 %reduce-scatter.10.cloned.1.call-start = ((), (), s32[]{:S(2)}) async-start(), calls=%async_computation.12 | async-start | bytes 8257536 | tf_op jit(solution)/shard_map/reduce_scatter | solution.py:80
  671.7 1.5 copy-start.1
  671.7 275.7 %reduce-scatter.12.cloned.1.call-start = ((), (), s32[]{:S(2)}) async-start(), calls=%async_computation.13 | async-start | bytes 8257536 | tf_op jit(solution)/shard_map/reduce_scatter | solution.py:83
Sparse Core Ops, SparseCore 0:
  10.4 55.3 all-gather.5
  68.3 52.6 all-gather.13
  122.7 73.3 all-gather.9
  197.5 71.9 all-gather.7
  271.0 71.9 all-gather.11
  551.1 51.6 reduce-scatter.7
  650.8 52.1 reduce-scatter.5
  705.8 79.6 reduce-scatter.13
  788.5 78.0 reduce-scatter.9
  869.3 78.0 reduce-scatter.11
where the time goes:
time: 961 us; the launch traced here: 954 us
  waiting for transfers between devices  479 us (50%)
  other arithmetic  254 us (26%)
  matrix products  120 us (12%)
  local copies, waits for them, and re-layouts  86.5 us (9%)
  between operations  14.6 us (2%)
    scatter-add x3, other arithmetic, spread(): zero_block.at[:, block_lists.reshape(-1)]  202 us
    reduce_scatter x1, waiting for transfers between devices, shards(): lax.psum_scatter(gate_partial.astype(jnp.bfloat16), 'row', scatter_dimens...  81 us
    reduce_scatter x1, waiting for transfers between devices, shards(): lax.psum_scatter(up_partial.astype(jnp.bfloat16), 'row', scatter_dimensio...  80.8 us
    reduce_scatter x1, waiting for transfers between devices, shards(): lax.psum_scatter(down_partial.astype(jnp.bfloat16), 'row', scatter_dimens...  80.4 us
    all_gather x1, waiting for transfers between devices, shards(): lax.all_gather(down_weight, 'row', axis=1, tiled=True)  60.2 us
    all_gather x1, waiting for transfers between devices, shards(): lax.all_gather(gate_weight, 'row', axis=1, tiled=True)  57.4 us
    all_gather x1, waiting for transfers between devices, shards(): lax.all_gather(tokens, 'col', axis=1, tiled=True)  50.6 us
    all_gather x1, waiting for transfers between devices, shards(): lax.all_gather(out_grad, 'col', axis=1, tiled=True)  48.8 us
  transfers between devices with their start and end apart: 10, of which 8 were waited for; matrix products, arithmetic and copies ran while one was open for 26% of the time, Pallas kernels for 0%

commit v1 on v0

v1 whole, which is shorter than its diff:
```python
import functools

import jax
import jax.numpy as jnp
from jax import lax
from jax.experimental import pallas as pl
from jax.experimental.pallas import tpu as pltpu
from jax.sharding import PartitionSpec as P

BS = 128
BF = jnp.bfloat16
F32 = jnp.float32


def contract(a, b, da, db):
    return lax.dot_general(a, b, (((da,), (db,)), ((), ())), preferred_element_type=F32)


def chunk_kernel(scal, *refs, n_col, slots, kg, f_total, f_first, blocks, first, last):
    refs = list(refs)

    def take(count):
        got = refs[:count]
        del refs[:count]
        return got

    x_hbm, y_hbm = take(n_col), take(n_col)
    acc_in = [] if first else take(2)
    tiles = take(slots)
    tile_grads = take(slots)
    results = take(2 * n_col) if last else take(2)
    x_all, y_all, acc_out, acc_x, load_sem, acc_sem, store_sem = refs

    step = pl.program_id(0)
    steps = pl.num_programs(0)
    tokens = x_all.shape[1]
    order = 3 * f_total * kg
    me = scal[order + kg]

    x_loads = [pltpu.make_async_copy(x_hbm[s], x_all.at[s], load_sem.at[0, s]) for s in range(n_col)]
    y_loads = [pltpu.make_async_copy(y_hbm[s], y_all.at[s], load_sem.at[1, s]) for s in range(n_col)]
    totals = (acc_out, acc_x)
    acc_loads = [pltpu.make_async_copy(src, dst, acc_sem.at[i]) for i, (src, dst) in enumerate(zip(acc_in, totals))]

    @pl.when(step == 0)
    def _():
        for copy in x_loads + y_loads + acc_loads:
            copy.start()
        if first:
            for total in totals:
                total[...] = jnp.zeros_like(total)
        for copy in x_loads:
            copy.wait()

    def places(table):
        found = []
        for s in range(kg):
            block = scal[table * f_total * kg + (f_first + step) * kg + scal[order + s]]
            slot = (block // blocks) ^ me
            found.append((slot, pl.multiple_of(lax.rem(block, blocks) * BS, BS)))
        return found

    def picked(source, where):
        return jnp.concatenate([source[slot, :, pl.ds(at, BS)] for slot, at in where], axis=1)

    def stacked(kind):
        return jnp.concatenate([tile[kind, 0] for tile in tiles], axis=0)

    def put(kind, grads):
        for s, ref in enumerate(tile_grads):
            ref[kind, 0] = grads[s * BS : (s + 1) * BS].astype(BF)

    def scatter(total, where, left, right):
        for s in range(0, kg, 2):
            two = contract(left, right[s * BS : (s + 2) * BS], 1, 1)
            for i in range(2):
                slot, at = where[s + i]
                total[slot, :, pl.ds(at, BS)] += two[:, i * BS : (i + 1) * BS]

    gate_at, up_at, down_at = places(0), places(1), places(2)
    gate_w, up_w, down_w = stacked(0), stacked(1), stacked(2)
    x_gate, x_up = picked(x_all, gate_at), picked(x_all, up_at)
    gate = contract(x_gate, gate_w, 1, 0)
    up = contract(x_up, up_w, 1, 0)
    sig = jax.nn.sigmoid(gate)
    silu = gate * sig
    hidden = (silu * up).astype(BF)

    @pl.when(step == 0)
    def _():
        for copy in y_loads:
            copy.wait()

    y_down = picked(y_all, down_at)
    hidden_grad = contract(y_down, down_w, 1, 0)
    gate_grad = (hidden_grad * up * sig * (1.0 + gate * (1.0 - sig))).astype(BF)
    up_grad = (hidden_grad * silu).astype(BF)
    put(2, contract(y_down, hidden, 0, 0))
    put(0, contract(x_gate, gate_grad, 0, 0))
    put(1, contract(x_up, up_grad, 0, 0))

    @pl.when(step == 0)
    def _():
        for copy in acc_loads:
            copy.wait()

    scatter(acc_out, down_at, hidden, down_w)
    scatter(acc_x, gate_at, gate_grad, gate_w)
    scatter(acc_x, up_at, up_grad, up_w)

    @pl.when(step == steps - 1)
    def _():
        if not last:
            stores = [pltpu.make_async_copy(src, dst, acc_sem.at[i]) for i, (src, dst) in enumerate(zip(totals, results))]
            for copy in stores:
                copy.start()
        else:
            stores = []
            for i, (total, rounded) in enumerate(zip(totals, (x_all, y_all))):
                for s in range(n_col):
                    for t in range(0, tokens, 32):
                        rounded[s, t : t + 32] = total[s, t : t + 32].astype(BF)
                    copy = pltpu.make_async_copy(rounded.at[s], results[i * n_col + s], store_sem.at[i, s])
                    copy.start()
                    stores.append(copy)
        for copy in stores:
            copy.wait()


def run_chunk(scal, xs, ys, accs, tiles, *, f_total, f_first, last):
    n_col, slots = len(xs), len(tiles)
    tokens, width = xs[0].shape
    f_here = tiles[0].shape[1]
    kg = slots
    first = accs is None
    anywhere = pl.BlockSpec(memory_space=pl.ANY)
    tile_spec = pl.BlockSpec((3, 1, BS, BS), lambda f, scal: (0, f, 0, 0))
    tile_shape = jax.ShapeDtypeStruct((3, f_here, BS, BS), BF)
    acc_shape = jax.ShapeDtypeStruct((n_col, tokens, width), F32)
    slice_shape = jax.ShapeDtypeStruct((tokens, width), BF)
    results = [slice_shape] * (2 * n_col) if last else [acc_shape] * 2
    kernel = functools.partial(
        chunk_kernel,
        n_col=n_col,
        slots=slots,
        kg=kg,
        f_total=f_total,
        f_first=f_first,
        blocks=width // BS,
        first=first,
        last=last,
    )
    flops = 9 * 2 * tokens * f_here * kg * BS * BS
    out = pl.pallas_call(
        kernel,
        grid_spec=pltpu.PrefetchScalarGridSpec(
            num_scalar_prefetch=1,
            grid=(f_here,),
            in_specs=[anywhere] * (2 * n_col + (0 if first else 2)) + [tile_spec] * slots,
            out_specs=[tile_spec] * slots + [anywhere] * len(results),
            scratch_shapes=[
                pltpu.VMEM((n_col, tokens, width), BF),
                pltpu.VMEM((n_col, tokens, width), BF),
                pltpu.VMEM((n_col, tokens, width), F32),
                pltpu.VMEM((n_col, tokens, width), F32),
                pltpu.SemaphoreType.DMA((2, n_col)),
                pltpu.SemaphoreType.DMA((2,)),
                pltpu.SemaphoreType.DMA((2, n_col)),
            ],
        ),
        out_shape=[tile_shape] * slots + results,
        compiler_params=pltpu.CompilerParams(vmem_limit_bytes=48 * 1024 * 1024),
        cost_estimate=pl.CostEstimate(flops=flops, bytes_accessed=40 * 1024 * 1024, transcendentals=0),
        name="ffn_chunk",
    )(scal, *xs, *ys, *([] if first else accs), *tiles)
    return out[:slots], out[slots:]


def total_of(*terms):
    value = terms[0].astype(F32)
    for term in terms[1:]:
        value = value + term.astype(F32)
    return value.astype(BF)


def make_shards(n_row, n_col):
    nz = n_row // 2

    def right(first, stop):
        return [(2 * z + c, 2 * z + 2 + c) for z in range(first, stop) for c in (0, 1)]

    def left(first, stop):
        return [(2 * z + c, 2 * z - 2 + c) for z in range(first, stop) for c in (0, 1)]

    across = [(r, r ^ 1) for r in range(n_row)]

    def from_columns(piece):
        return [piece] + [lax.ppermute(piece, "col", [(i, i ^ o) for i in range(n_col)]) for o in range(1, n_col)]

    def gather_chain(own, after):
        z = lax.axis_index("row") // 2
        own, _ = lax.optimization_barrier((own, after))
        rights, lefts = [own], [own]
        for s in range(1, nz):
            rights.append(lax.ppermute(rights[-1], "row", right(s - 1, nz - 1)))
            lefts.append(lax.ppermute(lefts[-1], "row", left(1, nz - s + 1)))
        slots = [own] + [jnp.where(z >= o, rights[o], lefts[nz - o]) for o in range(1, nz)]
        marker = (rights[min(2, nz - 1)], lefts[min(2, nz - 1)])
        return slots, marker

    def reduce_chain(own, sent):
        got = [lax.ppermute(part, "row", across) for part in sent]
        from_left = from_right = ()
        for s in range(1, nz):
            to_right = total_of(own[s], got[s], *from_left)
            to_left = total_of(own[nz - s], got[nz - s], *from_right)
            from_left = (lax.ppermute(to_right, "row", right(0, s)),)
            from_right = (lax.ppermute(to_left, "row", left(nz - s, nz)),)
        return total_of(own[0], got[0], *from_left, *from_right)

    def sum_columns(parts):
        return total_of(*[parts[0]] + [lax.ppermute(parts[o], "col", [(i, i ^ o) for i in range(n_col)]) for o in range(1, n_col)])

    def shards(tokens, out_grad, gate_weight, up_weight, down_weight, gate_rows, up_rows, down_columns):
        f_total, part = gate_weight.shape[:2]
        kg = gate_rows.shape[1]
        row = lax.axis_index("row")
        z, core = row // 2, row % 2
        whole_tiles = part == BS
        spots = (z - jnp.arange(nz, dtype=jnp.int32)) % nz
        order = jnp.concatenate([2 * spots + core, 2 * spots + 1 - core]) if whole_tiles else spots
        scal = jnp.concatenate(
            [t.reshape(-1) for t in (gate_rows, up_rows, down_columns)]
            + [order.astype(jnp.int32), lax.axis_index("col").astype(jnp.int32).reshape(1)]
        )
        xs, ys = from_columns(tokens), from_columns(out_grad)

        pieces = 4 if f_total % 4 == 0 else 1
        size = f_total // pieces
        after = ()
        accs, grads = None, []
        for piece in range(pieces):
            f_first = piece * size
            own = jnp.stack([w[f_first : f_first + size] for w in (gate_weight, up_weight, down_weight)])
            mine, after = gather_chain(own, after)
            other = [lax.ppermute(m, "row", across) for m in mine]
            if whole_tiles:
                tiles = mine + other
            else:
                tiles = [
                    jnp.where(core == 0, jnp.concatenate([a, b], 2), jnp.concatenate([b, a], 2))
                    for a, b in zip(mine, other)
                ]
            tile_grads, accs = run_chunk(
                scal, xs, ys, accs, tiles, f_total=f_total, f_first=f_first, last=piece == pieces - 1
            )
            if whole_tiles:
                keep, give = tile_grads[:nz], tile_grads[nz:]
            else:
                keep = [lax.dynamic_slice_in_dim(g, core * part, part, 2) for g in tile_grads]
                give = [lax.dynamic_slice_in_dim(g, (1 - core) * part, part, 2) for g in tile_grads]
            grads.append(reduce_chain(keep, give))

        output, input_grad = sum_columns(accs[:n_col]), sum_columns(accs[n_col:])
        weight_grads = [jnp.concatenate([g[kind] for g in grads], axis=0) for kind in range(3)]
        return (output, input_grad, *weight_grads)

    return shards


def solution(mesh):
    in_specs = (
        P("row", "col"),
        P("row", "col"),
        P("col", "row", None),
        P("col", "row", None),
        P("col", "row", None),
        P("col", None),
        P("col", None),
        P("col", None),
    )
    out_specs = in_specs[:5]
    shards = make_shards(mesh.shape["row"], mesh.shape["col"])
    return jax.shard_map(shards, mesh=mesh, in_specs=in_specs, out_specs=out_specs, check_vma=False)
```

time: 961 us -> 570 us (0.59)
  waiting for transfers between devices: 479 us -> 251 us
  other arithmetic: 254 us -> 34.2 us
  starting transfers between devices: 0.4 us -> 140 us
  Pallas kernels: 0 us -> 122 us
  matrix products: 120 us -> 0 us
  local copies, waits for them, and re-layouts: 86.5 us -> 11.4 us
  between operations: 14.6 us -> 2.16 us
    reduce_scatter x5 -> x0, waiting for transfers between devices: 260 us -> none  [the longest x1 81 us: shards(): lax.psum_scatter(gate_partial.astype(jnp.bfloat16), 'row', scatter_dimens...]
    ppermute x0 -> x92, waiting for transfers between devices: none -> 251 us  [the longest x12 60 us: reduce_chain(): from_left = (lax.ppermute(to_right, 'row', right(0, s)),)]
    all_gather x5 -> x0, waiting for transfers between devices: 217 us -> none  [the longest x1 60.2 us: shards(): lax.all_gather(down_weight, 'row', axis=1, tiled=True)]
    scatter-add x3 -> x0, other arithmetic: 202 us -> none  [spread(): zero_block.at[:, block_lists.reshape(-1)]]
    ppermute x0 -> x92, starting transfers between devices: none -> 140 us  [the longest x12 65 us: reduce_chain(): from_left = (lax.ppermute(to_right, 'row', right(0, s)),)]
    pallas_call x0 -> x4, Pallas kernels: none -> 122 us  [run_chunk(): pl.pallas_call(kernel, grid_spec=pltpu.PrefetchScalarGridSpec(num_scalar_...]
    dot_general x9 -> x0, matrix products: 120 us -> none  [the longest x1 17.3 us: shards(): jnp.einsum('tfi,fkri->tfkr', gate_grad, gate_four, preferred_element_type...]
    gather x3 -> x0, local copies, waits for them, and re-layouts: 34.4 us -> none  [the longest x1 11.5 us: shards(): jnp.take(blocks_in, up_rows.reshape(-1), axis=1)]
  transfers between devices with their start and end apart: 10 -> 92, of which waited for: 8 -> 26; matrix products, arithmetic and copies ran while one was open for 26% -> 6% of each run, Pallas kernels for 0% -> 22%
where the time goes in v1:
time: 570 us; the launch traced here: 562 us
  waiting for transfers between devices  251 us (44%)
  starting transfers between devices  140 us (25%)
  Pallas kernels  122 us (21%)
  other arithmetic  34.2 us (6%)
  local copies, waits for them, and re-layouts  11.4 us (2%)
    pallas_call x4, Pallas kernels, run_chunk(): pl.pallas_call(kernel, grid_spec=pltpu.PrefetchScalarGridSpec(num_scalar_...  122 us
    ppermute x12, starting transfers between devices, reduce_chain(): from_left = (lax.ppermute(to_right, 'row', right(0, s)),)  65 us
    ppermute x12, waiting for transfers between devices, reduce_chain(): from_left = (lax.ppermute(to_right, 'row', right(0, s)),)  60 us
    ppermute x12, waiting for transfers between devices, gather_chain(): lefts.append(lax.ppermute(lefts[-1], 'row', left(1, nz - s + 1)))  54.9 us
    ppermute x6, waiting for transfers between devices, from_columns(): lax.ppermute(piece, 'col', [(i, i ^ o) for i in range(n_col)])  47.4 us
    ppermute x6, waiting for transfers between devices, sum_columns(): lax.ppermute(parts[o], 'col', [(i, i ^ o) for i in range(n_col)])  46.7 us
    ppermute x12, waiting for transfers between devices, gather_chain(): rights.append(lax.ppermute(rights[-1], 'row', right(s - 1, nz - 1)))  28.7 us
    ppermute x12, starting transfers between devices, gather_chain(): rights.append(lax.ppermute(rights[-1], 'row', right(s - 1, nz - 1)))  23.7 us
  transfers between devices with their start and end apart: 92, of which 26 were waited for; matrix products, arithmetic and copies ran while one was open for 6% of the time, Pallas kernels for 22%

profile of v1, /device:TPU:0, one launch (start us, length us, event | category | flops | bytes accessed | tf_op | source)
XLA Modules:
  0.0 561.7 jit_solution(1613704298305464536)
XLA Ops:
  4.0 5.1 collective-permute-start.6
  10.5 13.3 %collective-permute-done.6 = bf16[3,7,128,128]{3,2,1,0:T(8,128)(2,1)S(1)} collective-permute-done((bf16[3,7,128,128]{3,2,1,0:T(8,128)(2,1)S(1)}, bf16[3,7,128,128]{3,2,1,0:T(8,128)(2,1)S(1)}, u32[]{:S(2)}, u32[]{:S(2)}) %collective-permute-start.6) | collective-permute-done | bytes 688160 | tf_op jit(solution)/shard_map/ppermute | solution.py:205
  33.4 12.6 %collective-permute-done.8 = bf16[3,7,128,128]{3,2,1,0:T(8,128)(2,1)} collective-permute-done((bf16[3,7,128,128]{3,2,1,0:T(8,128)(2,1)S(1)}, bf16[3,7,128,128]{3,2,1,0:T(8,128)(2,1)}, u32[]{:S(2)}, u32[]{:S(2)}) %collective-permute-start.8) | collective-permute-done | bytes 688160 | tf_op jit(solution)/shard_map/ppermute | solution.py:206
  47.3 8.0 %collective-permute-done.refs_1_ = bf16[256,2048]{1,0:T(8,128)(2,1)S(1)} collective-permute-done((bf16[256,2048]{1,0:T(8,128)(2,1)S(1)}, bf16[256,2048]{1,0:T(8,128)(2,1)S(1)}, u32[]{:S(2)}, u32[]{:S(2)}) %collective-permute-start) | collective-permute-done | bytes 1048608 | tf_op jit(solution)/shard_map/ppermute | solution.py:198
  56.8 19.6 %collective-permute-done.1.refs_2_ = bf16[256,2048]{1,0:T(8,128)(2,1)S(1)} collective-permute-done((bf16[256,2048]{1,0:T(8,128)(2,1)S(1)}, bf16[256,2048]{1,0:T(8,128)(2,1)S(1)}, u32[]{:S(2)}, u32[]{:S(2)}) %collective-permute-start.1) | collective-permute-done | bytes 1048608 | tf_op jit(solution)/shard_map/ppermute | solution.py:198
  82.6 6.2 %collective-permute-start.16 = (bf16[3,7,128,128]{3,2,1,0:T(8,128)(2,1)S(1)}, bf16[3,7,128,128]{3,2,1,0:T(8,128)(2,1)}, u32[]{:S(2)}, u32[]{:S(2)}) collective-permute-start(bf16[3,7,128,128]{3,2,1,0:T(8,128)(2,1)S(1)} %pad_maximum_fusion.4.refs_10_), channel_id=1, source_target_pairs={{0,8},{4,12},{8,16},{12,20},{16,24},{20,28},{1,9},{5,13},{9,17},{1... | collective-permute-start | bytes 2064392 | tf_op jit(solution)/shard_map/ppermute | solution.py:205
  91.8 5.2 collective-permute-done.17
  102.0 19.7 %collective-permute-done.4.refs_6_ = bf16[256,2048]{1,0:T(8,128)(2,1)} collective-permute-done((bf16[256,2048]{1,0:T(8,128)(2,1)S(1)}, bf16[256,2048]{1,0:T(8,128)(2,1)}, u32[]{:S(2)}, u32[]{:S(2)}) %collective-permute-start.4) | collective-permute-done | bytes 1048608 | tf_op jit(solution)/shard_map/ppermute | solution.py:198
  126.1 25.8 %ffn_chunk.4 = (bf16[3,7,128,128]{3,2,1,0:T(8,128)(2,1)S(1)}, bf16[3,7,128,128]{3,2,1,0:T(8,128)(2,1)S(1)}, bf16[3,7,128,128]{3,2,1,0:T(8,128)(2,1)S(1)}, bf16[3...) custom-call(s32[681]{0:T(1024)S(1)} %concatenate.12.scal, ...), custom_call_target="tpu_custom_call" | custom-call | flops 4227858432 | bytes 41943040 | tf_op jit(solution)/shard_map/ffn_chunk/pallas_call | solution.py:154
  162.5 9.5 %collective-permute-done.26 = bf16[3,7,128,128]{3,2,1,0:T(8,128)(2,1)S(1)} collective-permute-done((bf16[3,7,128,128]{3,2,1,0:T(8,128)(2,1)S(1)}, bf16[3,7,128,128]{3,2,1,0:T(8,128)(2,1)S(1)}, u32[]{:S(2)}, u32[]{:S(2)}) %collective-permute-start.26) | collective-permute-done | bytes 688160 | tf_op jit(solution)/shard_map/ppermute | solution.py:205
  172.6 5.3 collective-permute-done.27
  180.4 5.5 collective-permute-start.56
  186.7 32.7 %ffn_chunk.5 = (bf16[3,7,128,128]{3,2,1,0:T(8,128)(2,1)S(1)}, bf16[3,7,128,128]{3,2,1,0:T(8,128)(2,1)S(1)}, bf16[3,7,128,128]{3,2,1,0:T(8,128)(2,1)S(1)}, bf16[3...) custom-call(s32[681]{0:T(1024)S(1)} %concatenate.12.scal, ...), custom_call_target="tpu_custom_call" | custom-call | flops 4227858432 | bytes 41943040 | tf_op jit(solution)/shard_map/ffn_chunk/pallas_call | solution.py:154
  231.5 5.9 %collective-permute-done.36 = bf16[3,7,128,128]{3,2,1,0:T(8,128)(2,1)S(1)} collective-permute-done((bf16[3,7,128,128]{3,2,1,0:T(8,128)(2,1)S(1)}, bf16[3,7,128,128]{3,2,1,0:T(8,128)(2,1)S(1)}, u32[]{:S(2)}, u32[]{:S(2)}) %collective-permute-start.36) | collective-permute-done | bytes 688160 | tf_op jit(solution)/shard_map/ppermute | solution.py:205
  243.4 8.4 %collective-permute-done.57 = bf16[3,7,128,128]{3,2,1,0:T(8,128)(2,1)S(1)} collective-permute-done((bf16[3,7,128,128]{3,2,1,0:T(8,128)(2,1)S(1)}, bf16[3,7,128,128]{3,2,1,0:T(8,128)(2,1)S(1)}, u32[]{:S(2)}, u32[]{:S(2)}) %collective-permute-start.57) | collective-permute-done | bytes 688160 | tf_op jit(solution)/shard_map/ppermute | solution.py:217
  260.0 10.7 %collective-permute-done.38 = bf16[3,7,128,128]{3,2,1,0:T(8,128)(2,1)S(1)} collective-permute-done((bf16[3,7,128,128]{3,2,1,0:T(8,128)(2,1)S(1)}, bf16[3,7,128,128]{3,2,1,0:T(8,128)(2,1)S(1)}, u32[]{:S(2)}, u32[]{:S(2)}) %collective-permute-start.38) | collective-permute-done | bytes 688160 | tf_op jit(solution)/shard_map/ppermute | solution.py:206
  275.5 13.9 %collective-permute-done.39 = bf16[3,7,128,128]{3,2,1,0:T(8,128)(2,1)S(1)} collective-permute-done((bf16[3,7,128,128]{3,2,1,0:T(8,128)(2,1)S(1)}, bf16[3,7,128,128]{3,2,1,0:T(8,128)(2,1)S(1)}, u32[]{:S(2)}, u32[]{:S(2)}) %collective-permute-start.39) | collective-permute-done | bytes 688160 | tf_op jit(solution)/shard_map/ppermute | solution.py:206
  292.6 33.3 %ffn_chunk.6 = (bf16[3,7,128,128]{3,2,1,0:T(8,128)(2,1)S(1)}, bf16[3,7,128,128]{3,2,1,0:T(8,128)(2,1)S(1)}, bf16[3,7,128,128]{3,2,1,0:T(8,128)(2,1)S(1)}, bf16[3...) custom-call(s32[681]{0:T(1024)S(1)} %concatenate.12.scal, ...), custom_call_target="tpu_custom_call" | custom-call | flops 4227858432 | bytes 41943040 | tf_op jit(solution)/shard_map/ffn_chunk/pallas_call | solution.py:154
  331.8 30.7 %ffn_chunk.7 = (bf16[3,7,128,128]{3,2,1,0:T(8,128)(2,1)S(1)}, bf16[3,7,128,128]{3,2,1,0:T(8,128)(2,1)S(1)}, bf16[3,7,128,128]{3,2,1,0:T(8,128)(2,1)S(1)}, bf16[3...) custom-call(s32[681]{0:T(1024)S(1)} %concatenate.12.scal, ...), custom_call_target="tpu_custom_call" | custom-call | flops 4227858432 | bytes 41943040 | tf_op jit(solution)/shard_map/ffn_chunk/pallas_call | solution.py:154
  374.5 5.4 collective-permute-done.58
  385.1 9.4 %collective-permute-done.76 = bf16[3,7,128,128]{3,2,1,0:T(8,128)(2,1)S(1)} collective-permute-done((bf16[3,7,128,128]{3,2,1,0:T(8,128)(2,1)S(1)}, bf16[3,7,128,128]{3,2,1,0:T(8,128)(2,1)S(1)}, u32[]{:S(2)}, u32[]{:S(2)}) %collective-permute-start.76) | collective-permute-done | bytes 688160 | tf_op jit(solution)/shard_map/ppermute | solution.py:217
  395.6 5.0 collective-permute-start.77
  402.3 7.0 %collective-permute-done.86 = bf16[3,7,128,128]{3,2,1,0:T(8,128)(2,1)S(1)} collective-permute-done((bf16[3,7,128,128]{3,2,1,0:T(8,128)(2,1)S(1)}, bf16[3,7,128,128]{3,2,1,0:T(8,128)(2,1)S(1)}, u32[]{:S(2)}, u32[]{:S(2)}) %collective-permute-start.86) | collective-permute-done | bytes 688160 | tf_op jit(solution)/shard_map/ppermute | solution.py:217
  414.0 9.6 %collective-permute-done.77 = bf16[3,7,128,128]{3,2,1,0:T(8,128)(2,1)S(1)} collective-permute-done((bf16[3,7,128,128]{3,2,1,0:T(8,128)(2,1)S(1)}, bf16[3,7,128,128]{3,2,1,0:T(8,128)(2,1)S(1)}, u32[]{:S(2)}, u32[]{:S(2)}) %collective-permute-start.77) | collective-permute-done | bytes 688160 | tf_op jit(solution)/shard_map/ppermute | solution.py:217
  430.9 11.6 %collective-permute-done.87 = bf16[3,7,128,128]{3,2,1,0:T(8,128)(2,1)S(1)} collective-permute-done((bf16[3,7,128,128]{3,2,1,0:T(8,128)(2,1)S(1)}, bf16[3,7,128,128]{3,2,1,0:T(8,128)(2,1)S(1)}, u32[]{:S(2)}, u32[]{:S(2)}) %collective-permute-start.87) | collective-permute-done | bytes 688160 | tf_op jit(solution)/shard_map/ppermute | solution.py:217
  445.9 13.4 %collective-permute-done.50 = bf16[256,2048]{1,0:T(8,128)(2,1)S(1)} collective-permute-done((bf16[256,2048]{1,0:T(8,128)(2,1)S(1)}, bf16[256,2048]{1,0:T(8,128)(2,1)S(1)}, u32[]{:S(2)}, u32[]{:S(2)}) %collective-permute-start.50) | collective-permute-done | bytes 1048608 | tf_op jit(solution)/shard_map/ppermute | solution.py:222
  465.5 14.9 %collective-permute-done.46 = bf16[256,2048]{1,0:T(8,128)(2,1)S(1)} collective-permute-done((bf16[256,2048]{1,0:T(8,128)(2,1)S(1)}, bf16[256,2048]{1,0:T(8,128)(2,1)S(1)}, u32[]{:S(2)}, u32[]{:S(2)}) %collective-permute-start.46) | collective-permute-done | bytes 1048608 | tf_op jit(solution)/shard_map/ppermute | solution.py:222
  484.8 18.4 %collective-permute-done.47 = bf16[256,2048]{1,0:T(8,128)(2,1)S(1)} collective-permute-done((bf16[256,2048]{1,0:T(8,128)(2,1)S(1)}, bf16[256,2048]{1,0:T(8,128)(2,1)S(1)}, u32[]{:S(2)}, u32[]{:S(2)}) %collective-permute-start.47) | collective-permute-done | bytes 1048608 | tf_op jit(solution)/shard_map/ppermute | solution.py:222
  507.8 5.6 %collective-permute-start.78 = (bf16[3,7,128,128]{3,2,1,0:T(8,128)(2,1)S(1)}, bf16[3,7,128,128]{3,2,1,0:T(8,128)(2,1)S(1)}, u32[]{:S(2)}, u32[]{:S(2)}) collective-permute-start(bf16[3,7,128,128]{3,2,1,0:T(8,128)(2,1)S(1)} %get-tuple-element.107), channel_id=1, source_target_pairs={{0,8},{4,12},{8,16},{12,20},{16,24},{20,28},{1,9},{5,13},{9,17},{1... | collective-permute-start | bytes 2064392 | tf_op jit(solution)/shard_map/ppermute | solution.py:217
  513.5 8.7 %collective-permute-done.71 = bf16[3,7,128,128]{3,2,1,0:T(8,128)(2,1)S(1)} collective-permute-done((bf16[3,7,128,128]{3,2,1,0:T(8,128)(2,1)S(1)}, bf16[3,7,128,128]{3,2,1,0:T(8,128)(2,1)S(1)}, u32[]{:S(2)}, u32[]{:S(2)}) %collective-permute-start.71) | collective-permute-done | bytes 688160 | tf_op jit(solution)/shard_map/ppermute | solution.py:218
  524.0 18.7 %collective-permute-start.88 = (bf16[3,7,128,128]{3,2,1,0:T(8,128)(2,1)S(1)}, bf16[3,7,128,128]{3,2,1,0:T(8,128)(2,1)S(1)}, u32[]{:S(2)}, u32[]{:S(2)}) collective-permute-start(bf16[3,7,128,128]{3,2,1,0:T(8,128)(2,1)S(1)} %get-tuple-element.109), channel_id=1, source_target_pairs={{0,8},{4,12},{8,16},{12,20},{16,24},{20,28},{1,9},{5,13},{9,17},{1... | collective-permute-start | bytes 2064392 | tf_op jit(solution)/shard_map/ppermute | solution.py:217
  544.9 8.6 %collective-permute-done.88 = bf16[3,7,128,128]{3,2,1,0:T(8,128)(2,1)S(1)} collective-permute-done((bf16[3,7,128,128]{3,2,1,0:T(8,128)(2,1)S(1)}, bf16[3,7,128,128]{3,2,1,0:T(8,128)(2,1)S(1)}, u32[]{:S(2)}, u32[]{:S(2)}) %collective-permute-start.88) | collective-permute-done | bytes 688160 | tf_op jit(solution)/shard_map/ppermute | solution.py:217
  (323 shorter events, 151.9 us)
Async XLA Ops:
  30.7 45.7 %collective-permute-start.1 = (bf16[256,2048]{1,0:T(8,128)(2,1)S(1)}, bf16[256,2048]{1,0:T(8,128)(2,1)S(1)}, u32[]{:S(2)}, u32[]{:S(2)}) collective-permute-start(bf16[256,2048]{1,0:T(8,128)(2,1)S(1)} %copy-done.4), channel_id=1, source_target_pairs={{0,2},{1,3},{2,0},{3,1},{4,6},{5,7},{6,4},{7,5},{8,10},{9,11},{10,... | collective-permute-start | bytes 3145736 | tf_op jit(solution)/shard_map/ppermute | solution.py:198
  32.2 47.1 %collective-permute-start.2 = (bf16[256,2048]{1,0:T(8,128)(2,1)S(1)}, bf16[256,2048]{1,0:T(8,128)(2,1)S(1)}, u32[]{:S(2)}, u32[]{:S(2)}) collective-permute-start(bf16[256,2048]{1,0:T(8,128)(2,1)S(1)} %copy-done.4), channel_id=1, source_target_pairs={{0,3},{1,2},{2,1},{3,0},{4,7},{5,6},{6,5},{7,4},{8,11},{9,10},{10,... | collective-permute-start | bytes 3145736 | tf_op jit(solution)/shard_map/ppermute | solution.py:198
  32.7 47.7 %collective-permute-start.11 = (bf16[3,7,128,128]{3,2,1,0:T(8,128)(2,1)S(1)}, bf16[3,7,128,128]{3,2,1,0:T(8,128)(2,1)S(1)}, u32[]{:S(2)}, u32[]{:S(2)}) collective-permute-start(bf16[3,7,128,128]{3,2,1,0:T(8,128)(2,1)S(1)} %collective-permute-done.10), channel_id=1, source_target_pairs={{16,24},{20,28},{17,25},{21,29},{18,26},{22,30},{19,27},{23,31}} | collective-permute-start | bytes 2064392 | tf_op jit(solution)/shard_map/ppermute | solution.py:205
  46.0 36.6 %collective-permute-start.9 = (bf16[3,7,128,128]{3,2,1,0:T(8,128)(2,1)}, bf16[3,7,128,128]{3,2,1,0:T(8,128)(2,1)}, u32[]{:S(2)}, u32[]{:S(2)}) collective-permute-start(bf16[3,7,128,128]{3,2,1,0:T(8,128)(2,1)} %collective-permute-done.8), channel_id=1, source_target_pairs={{8,0},{12,4},{9,1},{13,5},{10,2},{14,6},{11,3},{15,7}} | collective-permute-start | bytes 2064392 | tf_op jit(solution)/shard_map/ppermute | solution.py:206
  55.3 45.1 %collective-permute-start.3 = (bf16[256,2048]{1,0:T(8,128)(2,1)S(1)}, bf16[256,2048]{1,0:T(8,128)(2,1)}, u32[]{:S(2)}, u32[]{:S(2)}) collective-permute-start(bf16[256,2048]{1,0:T(8,128)(2,1)S(1)} %copy-done.5), channel_id=1, source_target_pairs={{0,1},{1,0},{2,3},{3,2},{4,5},{5,4},{6,7},{7,6},{8,9},{9,8},{10,11... | collective-permute-start | bytes 3145736 | tf_op jit(solution)/shard_map/ppermute | solution.py:198
  76.4 45.3 %collective-permute-start.4 = (bf16[256,2048]{1,0:T(8,128)(2,1)S(1)}, bf16[256,2048]{1,0:T(8,128)(2,1)}, u32[]{:S(2)}, u32[]{:S(2)}) collective-permute-start(bf16[256,2048]{1,0:T(8,128)(2,1)S(1)} %copy-done.5), channel_id=1, source_target_pairs={{0,2},{1,3},{2,0},{3,1},{4,6},{5,7},{6,4},{7,5},{8,10},{9,11},{10,... | collective-permute-start | bytes 3145736 | tf_op jit(solution)/shard_map/ppermute | solution.py:198
  79.4 42.3 %collective-permute-start.5 = (bf16[256,2048]{1,0:T(8,128)(2,1)S(1)}, bf16[256,2048]{1,0:T(8,128)(2,1)}, u32[]{:S(2)}, u32[]{:S(2)}) collective-permute-start(bf16[256,2048]{1,0:T(8,128)(2,1)S(1)} %copy-done.5), channel_id=1, source_target_pairs={{0,3},{1,2},{2,1},{3,0},{4,7},{5,6},{6,5},{7,4},{8,11},{9,10},{10,... | collective-permute-start | bytes 3145736 | tf_op jit(solution)/shard_map/ppermute | solution.py:198
  123.3 35.0 %collective-permute-start.19 = (bf16[3,7,128,128]{3,2,1,0:T(8,128)(2,1)}, bf16[3,7,128,128]{3,2,1,0:T(8,128)(2,1)S(1)}, u32[]{:S(2)}, u32[]{:S(2)}) collective-permute-start(bf16[3,7,128,128]{3,2,1,0:T(8,128)(2,1)} %collective-permute-done.18), channel_id=1, source_target_pairs={{8,0},{12,4},{9,1},{13,5},{10,2},{14,6},{11,3},{15,7}} | collective-permute-start | bytes 2064392 | tf_op jit(solution)/shard_map/ppermute | solution.py:206
  171.9 47.5 %collective-permute-start.30 = (bf16[3,7,128,128]{3,2,1,0:T(8,128)(2,1)S(1)}, bf16[3,7,128,128]{3,2,1,0:T(8,128)(2,1)S(1)}, u32[]{:S(2)}, u32[]{:S(2)}) collective-permute-start(bf16[3,7,128,128]{3,2,1,0:T(8,128)(2,1)S(1)} %collective-permute-done.26), channel_id=1, source_target_pairs={{8,16},{12,20},{16,24},{20,28},{9,17},{13,21},{17,25},{21,29},{10,... | collective-permute-start | bytes 2064392 | tf_op jit(solution)/shard_map/ppermute | solution.py:205
  177.9 42.5 %collective-permute-start.28 = (bf16[3,7,128,128]{3,2,1,0:T(8,128)(2,1)S(1)}, bf16[3,7,128,128]{3,2,1,0:T(8,128)(2,1)S(1)}, u32[]{:S(2)}, u32[]{:S(2)}) collective-permute-start(bf16[3,7,128,128]{3,2,1,0:T(8,128)(2,1)S(1)} %collective-permute-done.27), channel_id=1, source_target_pairs={{8,0},{12,4},{16,8},{20,12},{9,1},{13,5},{17,9},{21,13},{10,2},{14... | collective-permute-start | bytes 2064392 | tf_op jit(solution)/shard_map/ppermute | solution.py:206
  180.3 41.4 %collective-permute-start.54 = (bf16[3,7,128,128]{3,2,1,0:T(8,128)(2,1)S(1)}, bf16[3,7,128,128]{3,2,1,0:T(8,128)(2,1)S(1)}, u32[]{:S(2)}, u32[]{:S(2)}) collective-permute-start(bf16[3,7,128,128]{3,2,1,0:T(8,128)(2,1)S(1)} %get-tuple-element.76), channel_id=1, source_target_pairs={{0,4},{4,0},{8,12},{12,8},{16,20},{20,16},{24,28},{28,24},{1,5},{5... | collective-permute-start | bytes 2064392 | tf_op jit(solution)/shard_map/ppermute | solution.py:212
  180.4 42.7 %collective-permute-start.56 = (bf16[3,7,128,128]{3,2,1,0:T(8,128)(2,1)}, bf16[3,7,128,128]{3,2,1,0:T(8,128)(2,1)}, u32[]{:S(2)}, u32[]{:S(2)}) collective-permute-start(bf16[3,7,128,128]{3,2,1,0:T(8,128)(2,1)} %fusion.1), channel_id=1, source_target_pairs={{0,8},{4,12},{1,9},{5,13},{2,10},{6,14},{3,11},{7,15}} | collective-permute-start | bytes 2064392 | tf_op jit(solution)/shard_map/ppermute | solution.py:217
  185.9 43.3 %collective-permute-start.53 = (bf16[3,7,128,128]{3,2,1,0:T(8,128)(2,1)S(1)}, bf16[3,7,128,128]{3,2,1,0:T(8,128)(2,1)}, u32[]{:S(2)}, u32[]{:S(2)}) collective-permute-start(bf16[3,7,128,128]{3,2,1,0:T(8,128)(2,1)S(1)} %get-tuple-element.74), channel_id=1, source_target_pairs={{0,4},{4,0},{8,12},{12,8},{16,20},{20,16},{24,28},{28,24},{1,5},{5... | collective-permute-start | bytes 2064392 | tf_op jit(solution)/shard_map/ppermute | solution.py:212
  275.0 50.9 %collective-permute-start.42 = (bf16[3,7,128,128]{3,2,1,0:T(8,128)(2,1)S(1)}, bf16[3,7,128,128]{3,2,1,0:T(8,128)(2,1)}, u32[]{:S(2)}, u32[]{:S(2)}) collective-permute-start(bf16[3,7,128,128]{3,2,1,0:T(8,128)(2,1)S(1)} %pad_maximum_fusion.6.refs_10_), channel_id=1, source_target_pairs={{0,4},{4,0},{8,12},{12,8},{16,20},{20,16},{24,28},{28,24},{1,5},{5... | collective-permute-start | bytes 2064392 | tf_op jit(solution)/shard_map/ppermute | solution.py:246
  289.3 36.8 %collective-permute-start.59 = (bf16[3,7,128,128]{3,2,1,0:T(8,128)(2,1)}, bf16[3,7,128,128]{3,2,1,0:T(8,128)(2,1)S(1)}, u32[]{:S(2)}, u32[]{:S(2)}) collective-permute-start(bf16[3,7,128,128]{3,2,1,0:T(8,128)(2,1)} %get-tuple-element.104), channel_id=1, source_target_pairs={{24,16},{28,20},{25,17},{29,21},{26,18},{30,22},{27,19},{31,23}} | collective-permute-start | bytes 2064392 | tf_op jit(solution)/shard_map/ppermute | solution.py:218
  291.1 38.6 %collective-permute-start.44 = (bf16[3,7,128,128]{3,2,1,0:T(8,128)(2,1)S(1)}, bf16[3,7,128,128]{3,2,1,0:T(8,128)(2,1)}, u32[]{:S(2)}, u32[]{:S(2)}) collective-permute-start(bf16[3,7,128,128]{3,2,1,0:T(8,128)(2,1)S(1)} %broadcast_select_fusion.4.refs_12_), channel_id=1, source_target_pairs={{0,4},{4,0},{8,12},{12,8},{16,20},{20,16},{24,28},{28,24},{1,5},{5... | collective-permute-start | bytes 2064392 | tf_op jit(solution)/shard_map/ppermute | solution.py:246
  291.2 38.7 %collective-permute-start.45 = (bf16[3,7,128,128]{3,2,1,0:T(8,128)(2,1)S(1)}, bf16[3,7,128,128]{3,2,1,0:T(8,128)(2,1)}, u32[]{:S(2)}, u32[]{:S(2)}) collective-permute-start(bf16[3,7,128,128]{3,2,1,0:T(8,128)(2,1)S(1)} %broadcast_select_fusion.refs_13_), channel_id=1, source_target_pairs={{0,4},{4,0},{8,12},{12,8},{16,20},{20,16},{24,28},{28,24},{1,5},{5... | collective-permute-start | bytes 2064392 | tf_op jit(solution)/shard_map/ppermute | solution.py:246
  291.7 39.7 %collective-permute-start.43 = (bf16[3,7,128,128]{3,2,1,0:T(8,128)(2,1)}, bf16[3,7,128,128]{3,2,1,0:T(8,128)(2,1)}, u32[]{:S(2)}, u32[]{:S(2)}) collective-permute-start(bf16[3,7,128,128]{3,2,1,0:T(8,128)(2,1)} %broadcast_select_fusion.8.refs_11_), channel_id=1, source_target_pairs={{0,4},{4,0},{8,12},{12,8},{16,20},{20,16},{24,28},{28,24},{1,5},{5... | collective-permute-start | bytes 2064392 | tf_op jit(solution)/shard_map/ppermute | solution.py:246
  325.9 36.6 %collective-permute-start.63 = (bf16[3,7,128,128]{3,2,1,0:T(8,128)(2,1)S(1)}, bf16[3,7,128,128]{3,2,1,0:T(8,128)(2,1)}, u32[]{:S(2)}, u32[]{:S(2)}) collective-permute-start(bf16[3,7,128,128]{3,2,1,0:T(8,128)(2,1)S(1)} %get-tuple-element.82), channel_id=1, source_target_pairs={{0,4},{4,0},{8,12},{12,8},{16,20},{20,16},{24,28},{28,24},{1,5},{5... | collective-permute-start | bytes 2064392 | tf_op jit(solution)/shard_map/ppermute | solution.py:212
  326.2 37.7 %collective-permute-start.67 = (bf16[3,7,128,128]{3,2,1,0:T(8,128)(2,1)}, bf16[3,7,128,128]{3,2,1,0:T(8,128)(2,1)}, u32[]{:S(2)}, u32[]{:S(2)}) collective-permute-start(bf16[3,7,128,128]{3,2,1,0:T(8,128)(2,1)} %add_convert_fusion.16), channel_id=1, source_target_pairs={{0,8},{4,12},{8,16},{12,20},{1,9},{5,13},{9,17},{13,21},{2,10},{6,... | collective-permute-start | bytes 2064392 | tf_op jit(solution)/shard_map/ppermute | solution.py:217
  329.7 37.2 %collective-permute-start.52 = (bf16[3,7,128,128]{3,2,1,0:T(8,128)(2,1)S(1)}, bf16[3,7,128,128]{3,2,1,0:T(8,128)(2,1)}, u32[]{:S(2)}, u32[]{:S(2)}) collective-permute-start(bf16[3,7,128,128]{3,2,1,0:T(8,128)(2,1)S(1)} %get-tuple-element.72), channel_id=1, source_target_pairs={{0,4},{4,0},{8,12},{12,8},{16,20},{20,16},{24,28},{28,24},{1,5},{5... | collective-permute-start | bytes 2064392 | tf_op jit(solution)/shard_map/ppermute | solution.py:212
  329.9 37.4 %collective-permute-start.60 = (bf16[3,7,128,128]{3,2,1,0:T(8,128)(2,1)}, bf16[3,7,128,128]{3,2,1,0:T(8,128)(2,1)}, u32[]{:S(2)}, u32[]{:S(2)}) collective-permute-start(bf16[3,7,128,128]{3,2,1,0:T(8,128)(2,1)} %add_convert_fusion.19), channel_id=1, source_target_pairs={{16,8},{20,12},{24,16},{28,20},{17,9},{21,13},{25,17},{29,21},{18,... | collective-permute-start | bytes 2064392 | tf_op jit(solution)/shard_map/ppermute | solution.py:218
  411.8 47.6 %collective-permute-start.50 = (bf16[256,2048]{1,0:T(8,128)(2,1)S(1)}, bf16[256,2048]{1,0:T(8,128)(2,1)S(1)}, u32[]{:S(2)}, u32[]{:S(2)}) collective-permute-start(bf16[256,2048]{1,0:T(8,128)(2,1)S(1)} %copy-done.52), channel_id=1, source_target_pairs={{0,2},{1,3},{2,0},{3,1},{4,6},{5,7},{6,4},{7,5},{8,10},{9,11},{10,... | collective-permute-start | bytes 3145736 | tf_op jit(solution)/shard_map/ppermute | solution.py:222
  412.8 48.8 %collective-permute-start.51 = (bf16[256,2048]{1,0:T(8,128)(2,1)S(1)}, bf16[256,2048]{1,0:T(8,128)(2,1)S(1)}, u32[]{:S(2)}, u32[]{:S(2)}) collective-permute-start(bf16[256,2048]{1,0:T(8,128)(2,1)S(1)} %copy-done.51), channel_id=1, source_target_pairs={{0,3},{1,2},{2,1},{3,0},{4,7},{5,6},{6,5},{7,4},{8,11},{9,10},{10,... | collective-permute-start | bytes 3145736 | tf_op jit(solution)/shard_map/ppermute | solution.py:222
  429.7 50.7 %collective-permute-start.46 = (bf16[256,2048]{1,0:T(8,128)(2,1)S(1)}, bf16[256,2048]{1,0:T(8,128)(2,1)S(1)}, u32[]{:S(2)}, u32[]{:S(2)}) collective-permute-start(bf16[256,2048]{1,0:T(8,128)(2,1)S(1)} %copy-done.50), channel_id=1, source_target_pairs={{0,1},{1,0},{2,3},{3,2},{4,5},{5,4},{6,7},{7,6},{8,9},{9,8},{10,11... | collective-permute-start | bytes 3145736 | tf_op jit(solution)/shard_map/ppermute | solution.py:222
  444.4 58.8 %collective-permute-start.47 = (bf16[256,2048]{1,0:T(8,128)(2,1)S(1)}, bf16[256,2048]{1,0:T(8,128)(2,1)S(1)}, u32[]{:S(2)}, u32[]{:S(2)}) collective-permute-start(bf16[256,2048]{1,0:T(8,128)(2,1)S(1)} %copy-done.49), channel_id=1, source_target_pairs={{0,2},{1,3},{2,0},{3,1},{4,6},{5,7},{6,4},{7,5},{8,10},{9,11},{10,... | collective-permute-start | bytes 3145736 | tf_op jit(solution)/shard_map/ppermute | solution.py:222
  459.4 45.1 %collective-permute-start.48 = (bf16[256,2048]{1,0:T(8,128)(2,1)S(1)}, bf16[256,2048]{1,0:T(8,128)(2,1)S(1)}, u32[]{:S(2)}, u32[]{:S(2)}) collective-permute-start(bf16[256,2048]{1,0:T(8,128)(2,1)S(1)} %copy-done.48), channel_id=1, source_target_pairs={{0,3},{1,2},{2,1},{3,0},{4,7},{5,6},{6,5},{7,4},{8,11},{9,10},{10,... | collective-permute-start | bytes 3145736 | tf_op jit(solution)/shard_map/ppermute | solution.py:222
  464.0 43.3 %collective-permute-start.62 = (bf16[3,7,128,128]{3,2,1,0:T(8,128)(2,1)S(1)}, bf16[3,7,128,128]{3,2,1,0:T(8,128)(2,1)S(1)}, u32[]{:S(2)}, u32[]{:S(2)}) collective-permute-start(bf16[3,7,128,128]{3,2,1,0:T(8,128)(2,1)S(1)} %get-tuple-element.80), channel_id=1, source_target_pairs={{0,4},{4,0},{8,12},{12,8},{16,20},{20,16},{24,28},{28,24},{1,5},{5... | collective-permute-start | bytes 2064392 | tf_op jit(solution)/shard_map/ppermute | solution.py:212
  464.3 42.6 %collective-permute-start.80 = (bf16[3,7,128,128]{3,2,1,0:T(8,128)(2,1)S(1)}, bf16[3,7,128,128]{3,2,1,0:T(8,128)(2,1)S(1)}, u32[]{:S(2)}, u32[]{:S(2)}) collective-permute-start(bf16[3,7,128,128]{3,2,1,0:T(8,128)(2,1)S(1)} %add_convert_fusion.9), channel_id=1, source_target_pairs={{16,8},{20,12},{24,16},{28,20},{17,9},{21,13},{25,17},{29,21},{18,... | collective-permute-start | bytes 2064392 | tf_op jit(solution)/shard_map/ppermute | solution.py:218
  506.9 36.1 %collective-permute-start.72 = (bf16[3,7,128,128]{3,2,1,0:T(8,128)(2,1)S(1)}, bf16[3,7,128,128]{3,2,1,0:T(8,128)(2,1)S(1)}, u32[]{:S(2)}, u32[]{:S(2)}) collective-permute-start(bf16[3,7,128,128]{3,2,1,0:T(8,128)(2,1)S(1)} %get-tuple-element.88), channel_id=1, source_target_pairs={{0,4},{4,0},{8,12},{12,8},{16,20},{20,16},{24,28},{28,24},{1,5},{5... | collective-permute-start | bytes 2064392 | tf_op jit(solution)/shard_map/ppermute | solution.py:212
  507.3 37.7 %collective-permute-start.82 = (bf16[3,7,128,128]{3,2,1,0:T(8,128)(2,1)S(1)}, bf16[3,7,128,128]{3,2,1,0:T(8,128)(2,1)S(1)}, u32[]{:S(2)}, u32[]{:S(2)}) collective-permute-start(bf16[3,7,128,128]{3,2,1,0:T(8,128)(2,1)S(1)} %get-tuple-element.96), channel_id=1, source_target_pairs={{0,4},{4,0},{8,12},{12,8},{16,20},{20,16},{24,28},{28,24},{1,5},{5... | collective-permute-start | bytes 2064392 | tf_op jit(solution)/shard_map/ppermute | solution.py:212
  507.8 36.5 %collective-permute-start.78 = (bf16[3,7,128,128]{3,2,1,0:T(8,128)(2,1)S(1)}, bf16[3,7,128,128]{3,2,1,0:T(8,128)(2,1)S(1)}, u32[]{:S(2)}, u32[]{:S(2)}) collective-permute-start(bf16[3,7,128,128]{3,2,1,0:T(8,128)(2,1)S(1)} %get-tuple-element.107), channel_id=1, source_target_pairs={{0,8},{4,12},{8,16},{12,20},{16,24},{20,28},{1,9},{5,13},{9,17},{1... | collective-permute-start | bytes 2064392 | tf_op jit(solution)/shard_map/ppermute | solution.py:217
  (114 other events, 2029.3 us)

commit v2 on v1

v2 whole, which is shorter than its diff:
```python
import functools

import jax
import jax.numpy as jnp
from jax import lax
from jax.experimental import pallas as pl
from jax.experimental.pallas import tpu as pltpu
from jax.sharding import PartitionSpec as P

BS = 128
BF = jnp.bfloat16
F32 = jnp.float32


def contract(a, b, da, db):
    return lax.dot_general(a, b, (((da,), (db,)), ((), ())), preferred_element_type=F32)


def chunk_kernel(scal, *refs, n_col, pieces, groups, waits, kg, f_total, f_first, blocks, first, last):
    refs = list(refs)

    def take(count):
        got = refs[:count]
        del refs[:count]
        return got

    (panels,) = take(1)
    take(waits)
    acc_in = [] if first else take(2)
    tiles = take(groups)
    tile_grads = take(groups)
    results = take(len(pieces)) if last else take(2)
    x_all, y_all, acc_out, acc_x, load_sem, acc_sem, store_sem = refs

    step = pl.program_id(0)
    steps = pl.num_programs(0)
    tokens = x_all.shape[1]
    order = 3 * f_total * kg
    me = scal[order + kg]
    both = (x_all, y_all)
    totals = (acc_out, acc_x)

    x_loads, y_loads = [
        [pltpu.make_async_copy(panels.at[slot, kind], both[kind].at[slot], load_sem.at[kind, slot]) for slot in range(n_col)]
        for kind in range(2)
    ]
    acc_loads = [pltpu.make_async_copy(src, dst, acc_sem.at[i]) for i, (src, dst) in enumerate(zip(acc_in, totals))]

    @pl.when(step == 0)
    def _():
        for copy in x_loads + y_loads + acc_loads:
            copy.start()
        if first:
            for total in totals:
                total[...] = jnp.zeros_like(total)
        for copy in x_loads:
            copy.wait()

    def places(table):
        found = []
        for s in range(kg):
            block = scal[table * f_total * kg + (f_first + step) * kg + scal[order + s]]
            found.append((block // blocks, pl.multiple_of(lax.rem(block, blocks) * BS, BS)))
        return found

    def picked(source, where):
        return jnp.concatenate([source[slot, :, pl.ds(at, BS)] for slot, at in where], axis=1)

    def stacked(kind):
        return jnp.concatenate([tile[i, kind, 0] for tile in tiles for i in range(tile.shape[0])], axis=0)

    def put(kind, grads):
        s = 0
        for ref in tile_grads:
            for i in range(ref.shape[0]):
                ref[i, kind, 0] = grads[:, s * BS : (s + 1) * BS].astype(BF)
                s += 1

    def scatter(total, where, left, right):
        for s in range(0, kg, 2):
            two = contract(left, right[s * BS : (s + 2) * BS], 1, 1)
            for i in range(2):
                slot, at = where[s + i]
                total[slot ^ me, :, pl.ds(at, BS)] += two[:, i * BS : (i + 1) * BS]

    gate_at, up_at, down_at = places(0), places(1), places(2)
    gate_w, up_w, down_w = stacked(0), stacked(1), stacked(2)
    x_gate, x_up = picked(x_all, gate_at), picked(x_all, up_at)
    gate = contract(x_gate, gate_w, 1, 0)
    up = contract(x_up, up_w, 1, 0)
    sig = jax.nn.sigmoid(gate)
    silu = gate * sig
    hidden = (silu * up).astype(BF)

    @pl.when(step == 0)
    def _():
        for copy in y_loads:
            copy.wait()

    y_down = picked(y_all, down_at)
    hidden_grad = contract(y_down, down_w, 1, 0)
    gate_grad = (hidden_grad * up * sig * (1.0 + gate * (1.0 - sig))).astype(BF)
    up_grad = (hidden_grad * silu).astype(BF)
    put(2, contract(hidden, y_down, 0, 0))
    put(0, contract(gate_grad, x_gate, 0, 0))
    put(1, contract(up_grad, x_up, 0, 0))

    @pl.when(step == 0)
    def _():
        for copy in acc_loads:
            copy.wait()

    scatter(acc_out, down_at, hidden, down_w)
    scatter(acc_x, gate_at, gate_grad, gate_w)
    scatter(acc_x, up_at, up_grad, up_w)

    @pl.when(step == steps - 1)
    def _():
        stores = []
        for kind, (total, rounded) in enumerate(zip(totals, both)):
            if last:
                for s in range(n_col):
                    for t in range(0, tokens, 32):
                        rounded[s, t : t + 32] = total[s, t : t + 32].astype(BF)
                here = [
                    pltpu.make_async_copy(
                        rounded.at[slot, pl.ds(at, rows)], results[p].at[kind], store_sem.at[kind, p]
                    )
                    for p, (slot, at, rows) in enumerate(pieces)
                ]
            else:
                here = [pltpu.make_async_copy(total, results[kind], acc_sem.at[kind])]
            for copy in here:
                copy.start()
            stores += here
        for copy in stores:
            copy.wait()


def run_chunk(scal, panels, after, pieces, accs, tiles, *, f_total, f_first, f_here, tile_first, last):
    n_col, _, tokens, width = panels.shape
    kg = sum(t.shape[0] for t in tiles)
    first = accs is None
    anywhere = pl.BlockSpec(memory_space=pl.ANY)
    tile_specs = [pl.BlockSpec((t.shape[0], 3, 1, BS, BS), lambda f, scal: (0, 0, f + tile_first, 0, 0)) for t in tiles]
    grad_specs = [pl.BlockSpec((t.shape[0], 3, 1, BS, BS), lambda f, scal: (0, 0, f, 0, 0)) for t in tiles]
    grad_shapes = [jax.ShapeDtypeStruct((t.shape[0], 3, f_here, BS, BS), BF) for t in tiles]
    if last:
        results = [jax.ShapeDtypeStruct((2, rows, width), BF) for _, _, rows in pieces]
    else:
        results = [jax.ShapeDtypeStruct((n_col, tokens, width), F32)] * 2
    kernel = functools.partial(
        chunk_kernel,
        n_col=n_col,
        pieces=pieces,
        groups=len(tiles),
        waits=len(after),
        kg=kg,
        f_total=f_total,
        f_first=f_first,
        blocks=width // BS,
        first=first,
        last=last,
    )
    flops = 9 * 2 * tokens * f_here * kg * BS * BS
    out = pl.pallas_call(
        kernel,
        grid_spec=pltpu.PrefetchScalarGridSpec(
            num_scalar_prefetch=1,
            grid=(f_here,),
            in_specs=[anywhere] * (1 + len(after) + (0 if first else 2)) + tile_specs,
            out_specs=grad_specs + [anywhere] * len(results),
            scratch_shapes=[
                pltpu.VMEM((n_col, tokens, width), BF),
                pltpu.VMEM((n_col, tokens, width), BF),
                pltpu.VMEM((n_col, tokens, width), F32),
                pltpu.VMEM((n_col, tokens, width), F32),
                pltpu.SemaphoreType.DMA((2, n_col)),
                pltpu.SemaphoreType.DMA((2,)),
                pltpu.SemaphoreType.DMA((2, len(pieces))),
            ],
        ),
        out_shape=grad_shapes + results,
        compiler_params=pltpu.CompilerParams(vmem_limit_bytes=48 * 1024 * 1024),
        cost_estimate=pl.CostEstimate(flops=flops, bytes_accessed=64 * 1024 * 1024, transcendentals=0),
        name="ffn_chunk",
    )(scal, panels, *after, *([] if first else accs), *tiles)
    return out[: len(tiles)], out[len(tiles) :]


def total_of(*terms):
    value = terms[0].astype(F32)
    for term in terms[1:]:
        value = value + term.astype(F32)
    return value.astype(BF)


def make_shards(n_row, n_col):
    nz = n_row // 2
    across = [(r, r ^ 1) for r in range(n_row)]
    two_phase = n_col == 4

    def right(first, stop):
        return [(2 * z + c, 2 * z + 2 + c) for z in range(first, stop) for c in (0, 1)]

    def left(first, stop):
        return [(2 * z + c, 2 * z - 2 + c) for z in range(first, stop) for c in (0, 1)]

    def over(value, offset):
        return lax.ppermute(value, "col", [(i, i ^ offset) for i in range(n_col)])

    def swap(value):
        return lax.ppermute(value, "row", across)

    def pieces_of(tokens):
        half = tokens // 2
        if two_phase:
            return ((0, 0, tokens), (1, 0, tokens), (2, 0, tokens), (3, 0, half), (3, half, half))
        return tuple((s, 0, tokens) for s in range(n_col))

    def sum_columns(parts):
        if two_phase:
            mine, beside, above, low, high = parts
            half = low.shape[1]
            low, high = over(low, 1), over(high, 2)
            above = jnp.concatenate([total_of(above[:, :half], low), above[:, half:]], axis=1)
            beside = jnp.concatenate([beside[:, :half], total_of(beside[:, half:], high)], axis=1)
            got = [over(beside, 1), over(above, 2)]
        else:
            mine = parts[0]
            got = [over(parts[o], o) for o in range(1, n_col)]
        return [total_of(mine[i], *[g[i] for g in got]) for i in range(2)]

    class Chain:
        def __init__(self, z, own=None, grads=None):
            self.z, self.own, self.grads = z, own, grads
            self.from_left, self.from_right = [], []
            self.tick = 0 if own is not None else 1

        def part(self, slot):
            return [g[slot // 2] for g in self.grads[slot % 2 :: 2]]

        def run(self, count):
            for _ in range(count):
                i = self.tick
                summing = self.grads is not None
                if i == 0:
                    to_right = to_left = self.own
                elif not summing:
                    to_right, to_left = self.from_left[-1], self.from_right[-1]
                else:
                    to_right = total_of(*self.part(i), *self.from_left[-1:])
                    to_left = total_of(*self.part(nz - i), *self.from_right[-1:])
                    if self.own is not None:
                        to_right = jnp.where(self.z >= i, self.from_left[-1], to_right)
                        to_left = jnp.where(nz - 1 - self.z >= i, self.from_right[-1], to_left)
                start = 0 if summing else i
                stop = nz - 1 if self.own is not None else i
                self.from_left.append(lax.ppermute(to_right, "row", right(start, stop)))
                self.from_right.append(lax.ppermute(to_left, "row", left(nz - stop, nz - start)))
                self.tick += 1
            return self

        def slots(self):
            found = [self.own]
            for o in range(1, nz):
                found.append(jnp.where(self.z >= o, self.from_left[o - 1], self.from_right[nz - o - 1]))
            return found

        def total(self):
            return total_of(*self.part(0), self.from_left[-1], self.from_right[-1])

    def shards(tokens, out_grad, gate_weight, up_weight, down_weight, gate_rows, up_rows, down_columns):
        f_total, part = gate_weight.shape[:2]
        kg = gate_rows.shape[1]
        row = lax.axis_index("row")
        z, core = row // 2, row % 2
        whole_tiles = part == BS
        slots = list(range(0, nz, 2)) + list(range(1, nz, 2))
        spots = (z - jnp.array(slots, dtype=jnp.int32)) % nz
        order = jnp.concatenate([2 * spots + core, 2 * spots + 1 - core]) if whole_tiles else spots
        scal = jnp.concatenate(
            [t.reshape(-1) for t in (gate_rows, up_rows, down_columns)]
            + [order.astype(jnp.int32), lax.axis_index("col").astype(jnp.int32).reshape(1)]
        )
        pieces = pieces_of(tokens.shape[0])
        panels = lax.all_gather(jnp.stack([tokens, out_grad]), "col")

        def own_tiles(start, stop):
            return jnp.stack([w[start:stop] for w in (gate_weight, up_weight, down_weight)])

        def all_tiles(mine):
            even, odd = jnp.stack(mine[0::2]), jnp.stack(mine[1::2])
            other_even, other_odd = swap(even), swap(odd)
            if whole_tiles:
                return [even, odd, other_even, other_odd]
            return [
                jnp.where(core == 0, jnp.concatenate([a, b], -2), jnp.concatenate([b, a], -2))
                for a, b in ((even, other_even), (odd, other_odd))
            ]

        def exchanged(tile_grads):
            if whole_tiles:
                keep, give = tile_grads[:2], tile_grads[2:]
            else:
                keep = [lax.dynamic_slice_in_dim(g, core * part, part, 4) for g in tile_grads]
                give = [lax.dynamic_slice_in_dim(g, (1 - core) * part, part, 4) for g in tile_grads]
            got_odd = swap(give[1])
            return [keep[0], keep[1], swap(give[0]), got_odd]

        if f_total % 4 == 0:
            sizes = [f_total // 4] * 4
        else:
            sizes = [f_total]
        starts = [sum(sizes[:i]) for i in range(len(sizes) + 1)]
        accs = None

        def compute(i, tiles, tile_first, accs, after=()):
            tile_grads, accs = run_chunk(
                scal,
                panels,
                after,
                pieces,
                accs,
                tiles,
                f_total=f_total,
                f_first=starts[i],
                f_here=sizes[i],
                tile_first=tile_first,
                last=i == len(sizes) - 1,
            )
            return exchanged(tile_grads), accs

        if len(sizes) == 1:
            gather = Chain(z, own_tiles(0, f_total)).run(nz - 1)
            grads, accs = compute(0, all_tiles(gather.slots()), 0, None)
            sums = [Chain(z, None, grads).run(nz - 1).total()]
        else:
            gather = Chain(z, own_tiles(0, starts[2])).run(nz - 1)
            tiles = all_tiles(gather.slots())
            one, two = Chain(z, own_tiles(starts[2], starts[3])), Chain(z, own_tiles(starts[3], starts[4]))
            one.run(1)
            two.run(1)
            one.grads, accs = compute(0, tiles, 0, None, (one.from_left[0], one.from_right[0]))
            one.run(1)
            after = (two.from_left[0], two.from_right[0], one.grads[3])
            two.grads, accs = compute(1, tiles, starts[1], accs, after)
            one.run(nz - 2)
            grads, accs = compute(2, all_tiles(one.slots()), 0, accs)
            three = Chain(z, None, grads)
            two.run(nz - 1)
            grads, accs = compute(3, all_tiles(two.slots()), 0, accs, (grads[3],))
            four = Chain(z, None, grads)
            sums = [one.total(), two.total(), three.run(nz - 1).total(), four.run(nz - 1).total()]

        output, input_grad = sum_columns(accs)
        weight_grads = [jnp.concatenate([jnp.swapaxes(g[kind], 1, 2) for g in sums], axis=0) for kind in range(3)]
        return (output, input_grad, *weight_grads)

    return shards


def solution(mesh):
    in_specs = (
        P("row", "col"),
        P("row", "col"),
        P("col", "row", None),
        P("col", "row", None),
        P("col", "row", None),
        P("col", None),
        P("col", None),
        P("col", None),
    )
    out_specs = in_specs[:5]
    shards = make_shards(mesh.shape["row"], mesh.shape["col"])
    return jax.shard_map(shards, mesh=mesh, in_specs=in_specs, out_specs=out_specs, check_vma=False)
```

time: 570 us -> 512 us (0.90); the launches traced: 562 us -> 510 us
  starting transfers between devices: 140 us -> 96.2 us
  waiting for transfers between devices: 251 us -> 219 us
  other arithmetic: 34.2 us -> 49.7 us
  between operations: 2.16 us -> 15.2 us
  Pallas kernels: 122 us -> 116 us
    ppermute x92 -> x52, starting transfers between devices: 140 us -> 96.2 us  [the longest x17 68.9 us: run(): self.from_left.append(lax.ppermute(to_right, 'row', right(start, stop)))]
    ppermute x92 -> x52, waiting for transfers between devices: 251 us -> 219 us  [the longest x17 115 us: run(): lax.ppermute(to_left, 'row', left(nz - stop, nz - start))]
    select_n x12 -> x6, other arithmetic: 8.83 us -> 22.5 us  [the longest x4 12.7 us: run(): to_left = jnp.where(nz - 1 - self.z >= i, self.from_right[-1], to_left)]
    another operation x4 -> x13, other arithmetic: 1.36 us -> 12.9 us  [the longest x12 9.89 us: all_tiles(): even, odd = (jnp.stack(mine[0::2]), jnp.stack(mine[1::2]))]
    convert_element_type x26 -> x13, other arithmetic: 20.9 us -> 13.4 us  [total_of(): return value.astype(BF)]
    pallas_call x4, Pallas kernels: 122 us -> 116 us  [run_chunk(): pl.pallas_call(kernel, grid_spec=pltpu.PrefetchScalarGridSpec(num_scalar_...]
    unnamed x111 -> x94, local copies, waits for them, and re-layouts: 7.62 us -> 13.3 us
  transfers between devices with their start and end apart: 92 -> 53, of which waited for: 26 -> 23; matrix products, arithmetic and copies ran while one was open for 6% -> 9% of each run, Pallas kernels for 22% -> 18%
where the time goes in v2:
time: 512 us; the launch traced here: 510 us
  waiting for transfers between devices  219 us (43%)
  Pallas kernels  116 us (23%)
  starting transfers between devices  96.2 us (19%)
  other arithmetic  49.7 us (10%)
  between operations  15.2 us (3%)
  local copies, waits for them, and re-layouts  14.2 us (3%)
    pallas_call x4, Pallas kernels, run_chunk(): pl.pallas_call(kernel, grid_spec=pltpu.PrefetchScalarGridSpec(num_scalar_...  116 us
    ppermute x17, waiting for transfers between devices, run(): lax.ppermute(to_left, 'row', left(nz - stop, nz - start))  115 us
    ppermute x17, waiting for transfers between devices, run(): self.from_left.append(lax.ppermute(to_right, 'row', right(start, stop)))  94.8 us
    ppermute x17, starting transfers between devices, run(): self.from_left.append(lax.ppermute(to_right, 'row', right(start, stop)))  68.9 us
    ppermute x17, starting transfers between devices, run(): lax.ppermute(to_left, 'row', left(nz - stop, nz - start))  19.7 us
    convert_element_type x13, other arithmetic, total_of(): return value.astype(BF)  13.4 us
    unnamed x94, local copies, waits for them, and re-layouts  13.3 us
    select_n x4, other arithmetic, run(): to_left = jnp.where(nz - 1 - self.z >= i, self.from_right[-1], to_left)  12.7 us
  transfers between devices with their start and end apart: 53, of which 23 were waited for; matrix products, arithmetic and copies ran while one was open for 9% of the time, Pallas kernels for 18%

profile of v2, /device:TPU:0, one launch (start us, length us, event | category | flops | bytes accessed | tf_op | source)
XLA Modules:
  0.0 510.1 jit_solution(2309576745741156350)
XLA Ops:
  13.6 5.6 %collective-permute-start.4 = (bf16[3,14,128,128]{3,2,1,0:T(8,128)(2,1)S(1)}, bf16[3,14,128,128]{3,2,1,0:T(8,128)(2,1)S(1)}, u32[]{:S(2)}, u32[]{:S(2)}) collective-permute-start(bf16[3,14,128,128]{3,2,1,0:T(8,128)(2,1)S(1)} %get-tuple-element.105), channel_id=1, source_target_pairs={{0,8},{4,12},{8,16},{12,20},{16,24},{20,28},{1,9},{5,13},{9,17},{1... | collective-permute-start | bytes 4128776 | tf_op jit(solution)/shard_map/ppermute | solution.py:259
  19.2 28.2 %collective-permute-done.6 = bf16[3,14,128,128]{3,2,1,0:T(8,128)(2,1)S(1)} collective-permute-done((bf16[3,14,128,128]{3,2,1,0:T(8,128)(2,1)S(1)}, bf16[3,14,128,128]{3,2,1,0:T(8,128)(2,1)S(1)}, u32[]{:S(2)}, u32[]{:S(2)}) %collective-permute-start.6) | collective-permute-done | bytes 1376288 | tf_op jit(solution)/shard_map/ppermute | solution.py:260
  50.5 30.3 %collective-permute-done.7 = bf16[3,14,128,128]{3,2,1,0:T(8,128)(2,1)} collective-permute-done((bf16[3,14,128,128]{3,2,1,0:T(8,128)(2,1)S(1)}, bf16[3,14,128,128]{3,2,1,0:T(8,128)(2,1)}, u32[]{:S(2)}, u32[]{:S(2)}) %collective-permute-start.7) | collective-permute-done | bytes 1376288 | tf_op jit(solution)/shard_map/ppermute | solution.py:260
  87.2 26.4 %collective-permute-done.8 = bf16[3,14,128,128]{3,2,1,0:T(8,128)(2,1)} collective-permute-done((bf16[3,14,128,128]{3,2,1,0:T(8,128)(2,1)}, bf16[3,14,128,128]{3,2,1,0:T(8,128)(2,1)}, u32[]{:S(2)}, u32[]{:S(2)}) %collective-permute-start.8) | collective-permute-done | bytes 1376288 | tf_op jit(solution)/shard_map/ppermute | solution.py:260
  121.6 12.7 %collective-permute-done.2.refs_1_ = bf16[3,7,128,128]{3,2,1,0:T(8,128)(2,1)S(1)} collective-permute-done((bf16[3,7,128,128]{3,2,1,0:T(8,128)(2,1)S(1)}, bf16[3,7,128,128]{3,2,1,0:T(8,128)(2,1)S(1)}, u32[]{:S(2)}, u32[]{:S(2)}) %collective-permute-start.2) | collective-permute-done | bytes 688160 | tf_op jit(solution)/shard_map/ppermute | solution.py:259
  134.2 4.6 collective-permute-done.3.refs_2_
  138.8 26.0 %ffn_chunk.4 = (bf16[2,3,7,128,128]{4,3,2,1,0:T(8,128)(2,1)S(1)}, bf16[2,3,7,128,128]{4,3,2,1,0:T(8,128)(2,1)S(1)}, bf16[2,3,7,128,128]{4,3,2,1,0:T(8,128)(2,1)}...) custom-call(s32[681]{0:T(1024)S(1)} %concatenate.18.scal, ...), custom_call_target="tpu_custom_call" | custom-call | flops 4227858432 | bytes 67108864 | tf_op jit(solution)/shard_map/ffn_chunk/pallas_call | solution.py:166
  167.6 5.7 %collective-permute-start = (bf16[3,7,128,128]{3,2,1,0:T(8,128)(2,1)}, bf16[3,7,128,128]{3,2,1,0:T(8,128)(2,1)S(1)}, u32[]{:S(2)}, u32[]{:S(2)}) collective-permute-start(bf16[3,7,128,128]{3,2,1,0:T(8,128)(2,1)} %get-tuple-element.129), channel_id=1, source_target_pairs={{0,8},{4,12},{8,16},{12,20},{16,24},{20,28},{1,9},{5,13},{9,17},{1... | collective-permute-start | bytes 2064392 | tf_op jit(solution)/shard_map/ppermute | solution.py:259
  178.3 5.4 %collective-permute-start.13 = (bf16[3,7,128,128]{3,2,1,0:T(8,128)(2,1)}, bf16[3,7,128,128]{3,2,1,0:T(8,128)(2,1)}, u32[]{:S(2)}, u32[]{:S(2)}) collective-permute-start(bf16[3,7,128,128]{3,2,1,0:T(8,128)(2,1)} %get-tuple-element.101), channel_id=1, source_target_pairs={{0,8},{4,12},{8,16},{12,20},{16,24},{20,28},{1,9},{5,13},{9,17},{1... | collective-permute-start | bytes 2064392 | tf_op jit(solution)/shard_map/ppermute | solution.py:259
  185.0 4.5 collective-permute-done.refs_1_
  193.8 31.0 %ffn_chunk.5 = (bf16[2,3,7,128,128]{4,3,2,1,0:T(8,128)(2,1)S(1)}, bf16[2,3,7,128,128]{4,3,2,1,0:T(8,128)(2,1)S(1)}, bf16[2,3,7,128,128]{4,3,2,1,0:T(8,128)(2,1)S...) custom-call(s32[681]{0:T(1024)S(1)} %concatenate.18.scal, ...), custom_call_target="tpu_custom_call" | custom-call | flops 4227858432 | bytes 67108864 | tf_op jit(solution)/shard_map/ffn_chunk/pallas_call | solution.py:166
  225.0 5.3 %fusion.35 = (bf16[3,7,128,128]{3,2,1,0:T(8,128)(2,1)}, bf16[3,7,128,128]{3,2,1,0:T(8,128)(2,1)}, bf16[1,3,7,128,128]{4,3,2,1,0:T(8,128)(2,1)}) fusion(bf16[3,7,128,128]{3,2,1,0:T(8,128)(2,1)} %collective-permute-done.14, pred[]{:T(512)S(6)} %ge.16, bf16[2,3,7,128,128]{4,3,2,1,0:T(8,128)(2,1)} %collective-permute-done.15, ...), kind=kLoop, calls=%fused_computation.92 | loop fusion | flops 4128768 | bytes 4816898 | tf_op jit(solution)/shard_map/jit(_where)/select_n | solution.py:256
  231.6 5.4 %collective-permute-start.17 = (bf16[3,7,128,128]{3,2,1,0:T(8,128)(2,1)}, bf16[3,7,128,128]{3,2,1,0:T(8,128)(2,1)}, u32[]{:S(2)}, u32[]{:S(2)}) collective-permute-start(bf16[3,7,128,128]{3,2,1,0:T(8,128)(2,1)} %get-tuple-element.99), channel_id=1, source_target_pairs={{0,8},{4,12},{8,16},{12,20},{16,24},{20,28},{1,9},{5,13},{9,17},{1... | collective-permute-start | bytes 2064392 | tf_op jit(solution)/shard_map/ppermute | solution.py:259
  238.9 10.1 %collective-permute-done.16 = bf16[3,7,128,128]{3,2,1,0:T(8,128)(2,1)} collective-permute-done((bf16[3,7,128,128]{3,2,1,0:T(8,128)(2,1)}, bf16[3,7,128,128]{3,2,1,0:T(8,128)(2,1)}, u32[]{:S(2)}, u32[]{:S(2)}) %collective-permute-start.16) | collective-permute-done | bytes 688160 | tf_op jit(solution)/shard_map/ppermute | solution.py:260
  250.2 4.8 fusion.32
  259.0 4.4 collective-permute-start.22
  264.7 12.4 %collective-permute-done.22 = bf16[3,7,128,128]{3,2,1,0:T(8,128)(2,1)S(1)} collective-permute-done((bf16[3,7,128,128]{3,2,1,0:T(8,128)(2,1)S(1)}, bf16[3,7,128,128]{3,2,1,0:T(8,128)(2,1)S(1)}, u32[]{:S(2)}, u32[]{:S(2)}) %collective-permute-start.22) | collective-permute-done | bytes 688160 | tf_op jit(solution)/shard_map/ppermute | solution.py:259
  284.3 5.4 %collective-permute-start.26 = (bf16[3,7,128,128]{3,2,1,0:T(8,128)(2,1)S(1)}, bf16[3,7,128,128]{3,2,1,0:T(8,128)(2,1)}, u32[]{:S(2)}, u32[]{:S(2)}) collective-permute-start(bf16[3,7,128,128]{3,2,1,0:T(8,128)(2,1)S(1)} %get-tuple-element.95), channel_id=1, source_target_pairs={{0,8},{4,12},{8,16},{12,20},{16,24},{20,28},{1,9},{5,13},{9,17},{1... | collective-permute-start | bytes 2064392 | tf_op jit(solution)/shard_map/ppermute | solution.py:259
  291.5 30.3 %ffn_chunk.6 = (bf16[2,3,7,128,128]{4,3,2,1,0:T(8,128)(2,1)S(1)}, bf16[2,3,7,128,128]{4,3,2,1,0:T(8,128)(2,1)S(1)}, bf16[2,3,7,128,128]{4,3,2,1,0:T(8,128)(2,1)S...) custom-call(s32[681]{0:T(1024)S(1)} %concatenate.18.scal, ...), custom_call_target="tpu_custom_call" | custom-call | flops 4227858432 | bytes 67108864 | tf_op jit(solution)/shard_map/ffn_chunk/pallas_call | solution.py:166
  322.4 5.0 fusion.38
  332.9 28.6 %ffn_chunk.7 = (bf16[2,3,7,128,128]{4,3,2,1,0:T(8,128)(2,1)S(1)}, bf16[2,3,7,128,128]{4,3,2,1,0:T(8,128)(2,1)S(1)}, bf16[2,3,7,128,128]{4,3,2,1,0:T(8,128)(2,1)}...) custom-call(s32[681]{0:T(1024)S(1)} %concatenate.18.scal, ...), custom_call_target="tpu_custom_call" | custom-call | flops 4227858432 | bytes 67108864 | tf_op jit(solution)/shard_map/ffn_chunk/pallas_call | solution.py:166
  372.5 11.2 %collective-permute-done.38 = bf16[3,7,128,128]{3,2,1,0:T(8,128)(2,1)S(1)} collective-permute-done((bf16[3,7,128,128]{3,2,1,0:T(8,128)(2,1)S(1)}, bf16[3,7,128,128]{3,2,1,0:T(8,128)(2,1)S(1)}, u32[]{:S(2)}, u32[]{:S(2)}) %collective-permute-start.38) | collective-permute-done | bytes 688160 | tf_op jit(solution)/shard_map/ppermute | solution.py:259
  387.8 5.6 %collective-permute-done.31 = bf16[2,128,2048]{2,1,0:T(8,128)(2,1)S(1)} collective-permute-done((bf16[2,128,2048]{2,1,0:T(8,128)(2,1)S(1)}, bf16[2,128,2048]{2,1,0:T(8,128)(2,1)S(1)}, u32[]{:S(2)}, u32[]{:S(2)}) %collective-permute-start.31) | collective-permute-done | bytes 1048608 | tf_op jit(solution)/shard_map/ppermute | solution.py:210
  398.4 4.4 collective-permute-start.35
  402.8 10.3 %collective-permute-done.39 = bf16[3,7,128,128]{3,2,1,0:T(8,128)(2,1)S(1)} collective-permute-done((bf16[3,7,128,128]{3,2,1,0:T(8,128)(2,1)S(1)}, bf16[3,7,128,128]{3,2,1,0:T(8,128)(2,1)S(1)}, u32[]{:S(2)}, u32[]{:S(2)}) %collective-permute-start.39) | collective-permute-done | bytes 688160 | tf_op jit(solution)/shard_map/ppermute | solution.py:259
  421.1 6.8 %collective-permute-done.35 = bf16[3,7,128,128]{3,2,1,0:T(8,128)(2,1)S(1)} collective-permute-done((bf16[3,7,128,128]{3,2,1,0:T(8,128)(2,1)S(1)}, bf16[3,7,128,128]{3,2,1,0:T(8,128)(2,1)S(1)}, u32[]{:S(2)}, u32[]{:S(2)}) %collective-permute-start.35) | collective-permute-done | bytes 688160 | tf_op jit(solution)/shard_map/ppermute | solution.py:259
  429.8 11.8 %collective-permute-done.46 = bf16[3,7,128,128]{3,2,1,0:T(8,128)(2,1)S(1)} collective-permute-done((bf16[3,7,128,128]{3,2,1,0:T(8,128)(2,1)S(1)}, bf16[3,7,128,128]{3,2,1,0:T(8,128)(2,1)S(1)}, u32[]{:S(2)}, u32[]{:S(2)}) %collective-permute-start.46) | collective-permute-done | bytes 688160 | tf_op jit(solution)/shard_map/ppermute | solution.py:259
  449.4 4.6 collective-permute-start.47
  454.0 7.8 %collective-permute-done.40 = bf16[3,7,128,128]{3,2,1,0:T(8,128)(2,1)S(1)} collective-permute-done((bf16[3,7,128,128]{3,2,1,0:T(8,128)(2,1)S(1)}, bf16[3,7,128,128]{3,2,1,0:T(8,128)(2,1)S(1)}, u32[]{:S(2)}, u32[]{:S(2)}) %collective-permute-start.40) | collective-permute-done | bytes 688160 | tf_op jit(solution)/shard_map/ppermute | solution.py:259
  467.2 7.4 %collective-permute-done.47 = bf16[3,7,128,128]{3,2,1,0:T(8,128)(2,1)S(1)} collective-permute-done((bf16[3,7,128,128]{3,2,1,0:T(8,128)(2,1)S(1)}, bf16[3,7,128,128]{3,2,1,0:T(8,128)(2,1)S(1)}, u32[]{:S(2)}, u32[]{:S(2)}) %collective-permute-start.47) | collective-permute-done | bytes 688160 | tf_op jit(solution)/shard_map/ppermute | solution.py:259
  475.5 8.0 %collective-permute-start.48 = (bf16[3,7,128,128]{3,2,1,0:T(8,128)(2,1)S(1)}, bf16[3,7,128,128]{3,2,1,0:T(8,128)(2,1)S(1)}, u32[]{:S(2)}, u32[]{:S(2)}) collective-permute-start(bf16[3,7,128,128]{3,2,1,0:T(8,128)(2,1)S(1)} %get-tuple-element.88), channel_id=1, source_target_pairs={{0,8},{4,12},{8,16},{12,20},{16,24},{20,28},{1,9},{5,13},{9,17},{1... | collective-permute-start | bytes 2064392 | tf_op jit(solution)/shard_map/ppermute | solution.py:259
  487.5 7.0 %collective-permute-done.48 = bf16[3,7,128,128]{3,2,1,0:T(8,128)(2,1)S(1)} collective-permute-done((bf16[3,7,128,128]{3,2,1,0:T(8,128)(2,1)S(1)}, bf16[3,7,128,128]{3,2,1,0:T(8,128)(2,1)S(1)}, u32[]{:S(2)}, u32[]{:S(2)}) %collective-permute-start.48) | collective-permute-done | bytes 688160 | tf_op jit(solution)/shard_map/ppermute | solution.py:259
  (226 shorter events, 118.0 us)
Async XLA Ops:
  7.2 131.7 %all-gather.3.cloned.1.call-start = ((), (), s32[]{:S(2)}) async-start(), calls=%async_computation | async-start | bytes 10485760 | tf_op jit(solution)/shard_map/all_gather | solution.py:287
  12.3 35.1 %collective-permute-start.6 = (bf16[3,14,128,128]{3,2,1,0:T(8,128)(2,1)S(1)}, bf16[3,14,128,128]{3,2,1,0:T(8,128)(2,1)S(1)}, u32[]{:S(2)}, u32[]{:S(2)}) collective-permute-start(bf16[3,14,128,128]{3,2,1,0:T(8,128)(2,1)S(1)} %get-tuple-element.105), channel_id=1, source_target_pairs={{8,0},{12,4},{16,8},{20,12},{24,16},{28,20},{9,1},{13,5},{17,9},{2... | collective-permute-start | bytes 4128776 | tf_op jit(solution)/shard_map/ppermute | solution.py:260
  13.6 35.1 %collective-permute-start.4 = (bf16[3,14,128,128]{3,2,1,0:T(8,128)(2,1)S(1)}, bf16[3,14,128,128]{3,2,1,0:T(8,128)(2,1)S(1)}, u32[]{:S(2)}, u32[]{:S(2)}) collective-permute-start(bf16[3,14,128,128]{3,2,1,0:T(8,128)(2,1)S(1)} %get-tuple-element.105), channel_id=1, source_target_pairs={{0,8},{4,12},{8,16},{12,20},{16,24},{20,28},{1,9},{5,13},{9,17},{1... | collective-permute-start | bytes 4128776 | tf_op jit(solution)/shard_map/ppermute | solution.py:259
  47.4 33.5 %collective-permute-start.7 = (bf16[3,14,128,128]{3,2,1,0:T(8,128)(2,1)S(1)}, bf16[3,14,128,128]{3,2,1,0:T(8,128)(2,1)}, u32[]{:S(2)}, u32[]{:S(2)}) collective-permute-start(bf16[3,14,128,128]{3,2,1,0:T(8,128)(2,1)S(1)} %collective-permute-done.6), channel_id=1, source_target_pairs={{8,0},{12,4},{16,8},{20,12},{9,1},{13,5},{17,9},{21,13},{10,2},{14... | collective-permute-start | bytes 4128776 | tf_op jit(solution)/shard_map/ppermute | solution.py:260
  48.7 33.4 %collective-permute-start.5 = (bf16[3,14,128,128]{3,2,1,0:T(8,128)(2,1)S(1)}, bf16[3,14,128,128]{3,2,1,0:T(8,128)(2,1)}, u32[]{:S(2)}, u32[]{:S(2)}) collective-permute-start(bf16[3,14,128,128]{3,2,1,0:T(8,128)(2,1)S(1)} %collective-permute-done.4), channel_id=1, source_target_pairs={{8,16},{12,20},{16,24},{20,28},{9,17},{13,21},{17,25},{21,29},{10,... | collective-permute-start | bytes 4128776 | tf_op jit(solution)/shard_map/ppermute | solution.py:259
  80.8 32.8 %collective-permute-start.8 = (bf16[3,14,128,128]{3,2,1,0:T(8,128)(2,1)}, bf16[3,14,128,128]{3,2,1,0:T(8,128)(2,1)}, u32[]{:S(2)}, u32[]{:S(2)}) collective-permute-start(bf16[3,14,128,128]{3,2,1,0:T(8,128)(2,1)} %collective-permute-done.7), channel_id=1, source_target_pairs={{8,0},{12,4},{9,1},{13,5},{10,2},{14,6},{11,3},{15,7}} | collective-permute-start | bytes 4128776 | tf_op jit(solution)/shard_map/ppermute | solution.py:260
  82.1 32.9 %collective-permute-start.9 = (bf16[3,14,128,128]{3,2,1,0:T(8,128)(2,1)}, bf16[3,14,128,128]{3,2,1,0:T(8,128)(2,1)}, u32[]{:S(2)}, u32[]{:S(2)}) collective-permute-start(bf16[3,14,128,128]{3,2,1,0:T(8,128)(2,1)} %collective-permute-done.5), channel_id=1, source_target_pairs={{16,24},{20,28},{17,25},{21,29},{18,26},{22,30},{19,27},{23,31}} | collective-permute-start | bytes 4128776 | tf_op jit(solution)/shard_map/ppermute | solution.py:259
  87.2 51.6 %collective-permute-start.10 = (bf16[2,3,14,128,128]{4,3,2,1,0:T(8,128)(2,1)}, bf16[2,3,14,128,128]{4,3,2,1,0:T(8,128)(2,1)}, u32[]{:S(2)}, u32[]{:S(2)}) collective-permute-start(bf16[2,3,14,128,128]{4,3,2,1,0:T(8,128)(2,1)} %pad_maximum_fusion.refs_3_.refs_6_), channel_id=1, source_target_pairs={{0,4},{4,0},{8,12},{12,8},{16,20},{20,16},{24,28},{28,24},{1,5},{5... | collective-permute-start | bytes 8257544 | tf_op jit(solution)/shard_map/ppermute | solution.py:213
  165.9 59.0 %collective-permute-start.15 = (bf16[2,3,7,128,128]{4,3,2,1,0:T(8,128)(2,1)}, bf16[2,3,7,128,128]{4,3,2,1,0:T(8,128)(2,1)}, u32[]{:S(2)}, u32[]{:S(2)}) collective-permute-start(bf16[2,3,7,128,128]{4,3,2,1,0:T(8,128)(2,1)} %get-tuple-element.39), channel_id=1, source_target_pairs={{0,4},{4,0},{8,12},{12,8},{16,20},{20,16},{24,28},{28,24},{1,5},{5... | collective-permute-start | bytes 4128776 | tf_op jit(solution)/shard_map/ppermute | solution.py:213
  178.3 46.7 %collective-permute-start.13 = (bf16[3,7,128,128]{3,2,1,0:T(8,128)(2,1)}, bf16[3,7,128,128]{3,2,1,0:T(8,128)(2,1)}, u32[]{:S(2)}, u32[]{:S(2)}) collective-permute-start(bf16[3,7,128,128]{3,2,1,0:T(8,128)(2,1)} %get-tuple-element.101), channel_id=1, source_target_pairs={{0,8},{4,12},{8,16},{12,20},{16,24},{20,28},{1,9},{5,13},{9,17},{1... | collective-permute-start | bytes 2064392 | tf_op jit(solution)/shard_map/ppermute | solution.py:259
  183.7 41.3 %collective-permute-start.14 = (bf16[3,7,128,128]{3,2,1,0:T(8,128)(2,1)}, bf16[3,7,128,128]{3,2,1,0:T(8,128)(2,1)}, u32[]{:S(2)}, u32[]{:S(2)}) collective-permute-start(bf16[3,7,128,128]{3,2,1,0:T(8,128)(2,1)} %get-tuple-element.100), channel_id=1, source_target_pairs={{8,0},{12,4},{16,8},{20,12},{24,16},{28,20},{9,1},{13,5},{17,9},{2... | collective-permute-start | bytes 2064392 | tf_op jit(solution)/shard_map/ppermute | solution.py:260
  224.8 30.4 %collective-permute-start.21 = (bf16[2,3,7,128,128]{4,3,2,1,0:T(8,128)(2,1)}, bf16[2,3,7,128,128]{4,3,2,1,0:T(8,128)(2,1)}, u32[]{:S(2)}, u32[]{:S(2)}) collective-permute-start(bf16[2,3,7,128,128]{4,3,2,1,0:T(8,128)(2,1)} %get-tuple-element.44), channel_id=1, source_target_pairs={{0,4},{4,0},{8,12},{12,8},{16,20},{20,16},{24,28},{28,24},{1,5},{5... | collective-permute-start | bytes 4128776 | tf_op jit(solution)/shard_map/ppermute | solution.py:213
  237.0 27.7 %collective-permute-start.24 = (bf16[2,3,7,128,128]{4,3,2,1,0:T(8,128)(2,1)}, bf16[2,3,7,128,128]{4,3,2,1,0:T(8,128)(2,1)S(1)}, u32[]{:S(2)}, u32[]{:S(2)}) collective-permute-start(bf16[2,3,7,128,128]{4,3,2,1,0:T(8,128)(2,1)} %copy-done.9), channel_id=1, source_target_pairs={{0,4},{4,0},{8,12},{12,8},{16,20},{20,16},{24,28},{28,24},{1,5},{5... | collective-permute-start | bytes 4128776 | tf_op jit(solution)/shard_map/ppermute | solution.py:213
  238.4 51.6 %collective-permute-start.18 = (bf16[2,3,7,128,128]{4,3,2,1,0:T(8,128)(2,1)S(1)}, bf16[2,3,7,128,128]{4,3,2,1,0:T(8,128)(2,1)S(1)}, u32[]{:S(2)}, u32[]{:S(2)}) collective-permute-start(bf16[2,3,7,128,128]{4,3,2,1,0:T(8,128)(2,1)S(1)} %pad_maximum_fusion.6.refs_3_), channel_id=1, source_target_pairs={{0,4},{4,0},{8,12},{12,8},{16,20},{20,16},{24,28},{28,24},{1,5},{5... | collective-permute-start | bytes 4128776 | tf_op jit(solution)/shard_map/ppermute | solution.py:213
  255.2 34.8 %collective-permute-start.19 = (bf16[2,3,7,128,128]{4,3,2,1,0:T(8,128)(2,1)S(1)}, bf16[2,3,7,128,128]{4,3,2,1,0:T(8,128)(2,1)S(1)}, u32[]{:S(2)}, u32[]{:S(2)}) collective-permute-start(bf16[2,3,7,128,128]{4,3,2,1,0:T(8,128)(2,1)S(1)} %pad_maximum_fusion.7.refs_4_), channel_id=1, source_target_pairs={{0,4},{4,0},{8,12},{12,8},{16,20},{20,16},{24,28},{28,24},{1,5},{5... | collective-permute-start | bytes 4128776 | tf_op jit(solution)/shard_map/ppermute | solution.py:213
  283.0 39.4 %collective-permute-start.25 = (bf16[3,7,128,128]{3,2,1,0:T(8,128)(2,1)}, bf16[3,7,128,128]{3,2,1,0:T(8,128)(2,1)}, u32[]{:S(2)}, u32[]{:S(2)}) collective-permute-start(bf16[3,7,128,128]{3,2,1,0:T(8,128)(2,1)} %get-tuple-element.94), channel_id=1, source_target_pairs={{8,0},{12,4},{16,8},{20,12},{24,16},{28,20},{9,1},{13,5},{17,9},{2... | collective-permute-start | bytes 2064392 | tf_op jit(solution)/shard_map/ppermute | solution.py:260
  284.3 38.1 %collective-permute-start.26 = (bf16[3,7,128,128]{3,2,1,0:T(8,128)(2,1)S(1)}, bf16[3,7,128,128]{3,2,1,0:T(8,128)(2,1)}, u32[]{:S(2)}, u32[]{:S(2)}) collective-permute-start(bf16[3,7,128,128]{3,2,1,0:T(8,128)(2,1)S(1)} %get-tuple-element.95), channel_id=1, source_target_pairs={{0,8},{4,12},{8,16},{12,20},{16,24},{20,28},{1,9},{5,13},{9,17},{1... | collective-permute-start | bytes 2064392 | tf_op jit(solution)/shard_map/ppermute | solution.py:259
  289.9 38.2 %collective-permute-start.27 = (bf16[2,3,7,128,128]{4,3,2,1,0:T(8,128)(2,1)S(1)}, bf16[2,3,7,128,128]{4,3,2,1,0:T(8,128)(2,1)S(1)}, u32[]{:S(2)}, u32[]{:S(2)}) collective-permute-start(bf16[2,3,7,128,128]{4,3,2,1,0:T(8,128)(2,1)S(1)} %pad_maximum_fusion.8.refs_4_), channel_id=1, source_target_pairs={{0,4},{4,0},{8,12},{12,8},{16,20},{20,16},{24,28},{28,24},{1,5},{5... | collective-permute-start | bytes 4128776 | tf_op jit(solution)/shard_map/ppermute | solution.py:213
  327.7 42.3 %collective-permute-start.37 = (bf16[2,3,7,128,128]{4,3,2,1,0:T(8,128)(2,1)S(1)}, bf16[2,3,7,128,128]{4,3,2,1,0:T(8,128)(2,1)}, u32[]{:S(2)}, u32[]{:S(2)}) collective-permute-start(bf16[2,3,7,128,128]{4,3,2,1,0:T(8,128)(2,1)S(1)} %get-tuple-element.53), channel_id=1, source_target_pairs={{0,4},{4,0},{8,12},{12,8},{16,20},{20,16},{24,28},{28,24},{1,5},{5... | collective-permute-start | bytes 4128776 | tf_op jit(solution)/shard_map/ppermute | solution.py:213
  361.5 25.3 %collective-permute-start.29 = (bf16[2,128,2048]{2,1,0:T(8,128)(2,1)S(1)}, bf16[2,128,2048]{2,1,0:T(8,128)(2,1)S(1)}, u32[]{:S(2)}, u32[]{:S(2)}) collective-permute-start(bf16[2,128,2048]{2,1,0:T(8,128)(2,1)S(1)} %get-tuple-element.49), channel_id=1, source_target_pairs={{0,2},{1,3},{2,0},{3,1},{4,6},{5,7},{6,4},{7,5},{8,10},{9,11},{10,... | collective-permute-start | bytes 3145736 | tf_op jit(solution)/shard_map/ppermute | solution.py:210
  368.6 24.7 %collective-permute-start.31 = (bf16[2,128,2048]{2,1,0:T(8,128)(2,1)S(1)}, bf16[2,128,2048]{2,1,0:T(8,128)(2,1)S(1)}, u32[]{:S(2)}, u32[]{:S(2)}) collective-permute-start(bf16[2,128,2048]{2,1,0:T(8,128)(2,1)S(1)} %get-tuple-element.51), channel_id=1, source_target_pairs={{0,1},{1,0},{2,3},{3,2},{4,5},{5,4},{6,7},{7,6},{8,9},{9,8},{10,11... | collective-permute-start | bytes 3145736 | tf_op jit(solution)/shard_map/ppermute | solution.py:210
  371.0 27.4 %collective-permute-start.33 = (bf16[3,7,128,128]{3,2,1,0:T(8,128)(2,1)S(1)}, bf16[3,7,128,128]{3,2,1,0:T(8,128)(2,1)S(1)}, u32[]{:S(2)}, u32[]{:S(2)}) collective-permute-start(bf16[3,7,128,128]{3,2,1,0:T(8,128)(2,1)S(1)} %copy-done.35), channel_id=1, source_target_pairs={{0,8},{4,12},{8,16},{12,20},{16,24},{20,28},{1,9},{5,13},{9,17},{1... | collective-permute-start | bytes 2064392 | tf_op jit(solution)/shard_map/ppermute | solution.py:259
  383.7 36.1 %collective-permute-start.34 = (bf16[3,7,128,128]{3,2,1,0:T(8,128)(2,1)S(1)}, bf16[3,7,128,128]{3,2,1,0:T(8,128)(2,1)S(1)}, u32[]{:S(2)}, u32[]{:S(2)}) collective-permute-start(bf16[3,7,128,128]{3,2,1,0:T(8,128)(2,1)S(1)} %copy-done.34), channel_id=1, source_target_pairs={{8,0},{12,4},{16,8},{20,12},{24,16},{28,20},{9,1},{13,5},{17,9},{2... | collective-permute-start | bytes 2064392 | tf_op jit(solution)/shard_map/ppermute | solution.py:260
  386.8 42.2 %collective-permute-start.44 = (bf16[2,3,7,128,128]{4,3,2,1,0:T(8,128)(2,1)S(1)}, bf16[2,3,7,128,128]{4,3,2,1,0:T(8,128)(2,1)S(1)}, u32[]{:S(2)}, u32[]{:S(2)}) collective-permute-start(bf16[2,3,7,128,128]{4,3,2,1,0:T(8,128)(2,1)S(1)} %copy-done.42), channel_id=1, source_target_pairs={{0,4},{4,0},{8,12},{12,8},{16,20},{20,16},{24,28},{28,24},{1,5},{5... | collective-permute-start | bytes 4128776 | tf_op jit(solution)/shard_map/ppermute | solution.py:213
  395.3 22.8 %collective-permute-start.42 = (bf16[3,7,128,128]{3,2,1,0:T(8,128)(2,1)S(1)}, bf16[3,7,128,128]{3,2,1,0:T(8,128)(2,1)S(1)}, u32[]{:S(2)}, u32[]{:S(2)}) collective-permute-start(bf16[3,7,128,128]{3,2,1,0:T(8,128)(2,1)S(1)} %get-tuple-element.85), channel_id=1, source_target_pairs={{16,8},{20,12},{24,16},{28,20},{17,9},{21,13},{25,17},{29,21},{18,... | collective-permute-start | bytes 2064392 | tf_op jit(solution)/shard_map/ppermute | solution.py:260
  398.4 29.5 %collective-permute-start.35 = (bf16[3,7,128,128]{3,2,1,0:T(8,128)(2,1)S(1)}, bf16[3,7,128,128]{3,2,1,0:T(8,128)(2,1)S(1)}, u32[]{:S(2)}, u32[]{:S(2)}) collective-permute-start(bf16[3,7,128,128]{3,2,1,0:T(8,128)(2,1)S(1)} %copy-done.37), channel_id=1, source_target_pairs={{0,8},{4,12},{8,16},{12,20},{16,24},{20,28},{1,9},{5,13},{9,17},{1... | collective-permute-start | bytes 2064392 | tf_op jit(solution)/shard_map/ppermute | solution.py:259
  413.2 28.4 %collective-permute-start.46 = (bf16[3,7,128,128]{3,2,1,0:T(8,128)(2,1)S(1)}, bf16[3,7,128,128]{3,2,1,0:T(8,128)(2,1)S(1)}, u32[]{:S(2)}, u32[]{:S(2)}) collective-permute-start(bf16[3,7,128,128]{3,2,1,0:T(8,128)(2,1)S(1)} %get-tuple-element.92), channel_id=1, source_target_pairs={{0,8},{4,12},{1,9},{5,13},{2,10},{6,14},{3,11},{7,15}} | collective-permute-start | bytes 2064392 | tf_op jit(solution)/shard_map/ppermute | solution.py:259
  418.1 29.5 %collective-permute-start.49 = (bf16[3,7,128,128]{3,2,1,0:T(8,128)(2,1)S(1)}, bf16[3,7,128,128]{3,2,1,0:T(8,128)(2,1)S(1)}, u32[]{:S(2)}, u32[]{:S(2)}) collective-permute-start(bf16[3,7,128,128]{3,2,1,0:T(8,128)(2,1)S(1)} %get-tuple-element.93), channel_id=1, source_target_pairs={{24,16},{28,20},{25,17},{29,21},{26,18},{30,22},{27,19},{31,23}} | collective-permute-start | bytes 2064392 | tf_op jit(solution)/shard_map/ppermute | solution.py:260
  419.8 29.6 %collective-permute-start.36 = (bf16[3,7,128,128]{3,2,1,0:T(8,128)(2,1)S(1)}, bf16[3,7,128,128]{3,2,1,0:T(8,128)(2,1)S(1)}, u32[]{:S(2)}, u32[]{:S(2)}) collective-permute-start(bf16[3,7,128,128]{3,2,1,0:T(8,128)(2,1)S(1)} %copy-done.36), channel_id=1, source_target_pairs={{8,0},{12,4},{16,8},{20,12},{24,16},{28,20},{9,1},{13,5},{17,9},{2... | collective-permute-start | bytes 2064392 | tf_op jit(solution)/shard_map/ppermute | solution.py:260
  427.9 56.9 %collective-permute-start.30 = (bf16[2,256,2048]{2,1,0:T(8,128)(2,1)S(1)}, bf16[2,256,2048]{2,1,0:T(8,128)(2,1)S(1)}, u32[]{:S(2)}, u32[]{:S(2)}) collective-permute-start(bf16[2,256,2048]{2,1,0:T(8,128)(2,1)S(1)} %pad_maximum_fusion.3), channel_id=1, source_target_pairs={{0,1},{1,0},{2,3},{3,2},{4,5},{5,4},{6,7},{7,6},{8,9},{9,8},{10,11... | collective-permute-start | bytes 6291464 | tf_op jit(solution)/shard_map/ppermute | solution.py:210
  429.0 55.8 %collective-permute-start.32 = (bf16[2,256,2048]{2,1,0:T(8,128)(2,1)S(1)}, bf16[2,256,2048]{2,1,0:T(8,128)(2,1)S(1)}, u32[]{:S(2)}, u32[]{:S(2)}) collective-permute-start(bf16[2,256,2048]{2,1,0:T(8,128)(2,1)S(1)} %pad_maximum_fusion.4), channel_id=1, source_target_pairs={{0,2},{1,3},{2,0},{3,1},{4,6},{5,7},{6,4},{7,5},{8,10},{9,11},{10,... | collective-permute-start | bytes 6291464 | tf_op jit(solution)/shard_map/ppermute | solution.py:210
  449.4 25.2 %collective-permute-start.47 = (bf16[3,7,128,128]{3,2,1,0:T(8,128)(2,1)S(1)}, bf16[3,7,128,128]{3,2,1,0:T(8,128)(2,1)S(1)}, u32[]{:S(2)}, u32[]{:S(2)}) collective-permute-start(bf16[3,7,128,128]{3,2,1,0:T(8,128)(2,1)S(1)} %get-tuple-element.90), channel_id=1, source_target_pairs={{0,8},{4,12},{8,16},{12,20},{1,9},{5,13},{9,17},{13,21},{2,10},{6,... | collective-permute-start | bytes 2064392 | tf_op jit(solution)/shard_map/ppermute | solution.py:259
  (65 other events, 720.6 us)
Sparse Core Ops, SparseCore 0:
  10.4 90.2 all-gather.2

commit v3 on v2

--- a/solution.py
+++ b/solution.py
@@ -270,6 +270,19 @@
         def total(self):
             return total_of(*self.part(0), self.from_left[-1], self.from_right[-1])
 
+    class Halves:
+        def __init__(self, z, grads):
+            self.even_z = z % 2 == 0
+            self.grads = grads
+            self.near = lax.ppermute(total_of(grads[1], grads[3]), "row", [(r, r ^ 2) for r in range(n_row)])
+
+        def total(self):
+            keep, _, got, _ = self.grads
+            far = jnp.where(self.even_z, self.near[1], self.near[0])
+            mine = jnp.where(self.even_z, self.near[0], self.near[1])
+            rest = lax.ppermute(total_of(keep[1], got[1], far), "row", [(r, r ^ 4) for r in range(n_row)])
+            return total_of(keep[0], got[0], mine, rest)
+
     def shards(tokens, out_grad, gate_weight, up_weight, down_weight, gate_rows, up_rows, down_columns):
         f_total, part = gate_weight.shape[:2]
         kg = gate_rows.shape[1]
@@ -299,23 +312,24 @@
                 for a, b in ((even, other_even), (odd, other_odd))
             ]
 
-        def exchanged(tile_grads):
+        def exchanged(tile_grads, hold):
             if whole_tiles:
                 keep, give = tile_grads[:2], tile_grads[2:]
             else:
                 keep = [lax.dynamic_slice_in_dim(g, core * part, part, 4) for g in tile_grads]
                 give = [lax.dynamic_slice_in_dim(g, (1 - core) * part, part, 4) for g in tile_grads]
+            give, _ = lax.optimization_barrier((give, hold))
             got_odd = swap(give[1])
             return [keep[0], keep[1], swap(give[0]), got_odd]
 
-        if f_total % 4 == 0:
+        if f_total % 4 == 0 and nz == 4 and whole_tiles:
             sizes = [f_total // 4] * 4
         else:
             sizes = [f_total]
         starts = [sum(sizes[:i]) for i in range(len(sizes) + 1)]
         accs = None
 
-        def compute(i, tiles, tile_first, accs, after=()):
+        def compute(i, tiles, tile_first, accs, after=(), hold=()):
             tile_grads, accs = run_chunk(
                 scal,
                 panels,
@@ -329,7 +343,7 @@
                 tile_first=tile_first,
                 last=i == len(sizes) - 1,
             )
-            return exchanged(tile_grads), accs
+            return exchanged(tile_grads, hold), accs
 
         if len(sizes) == 1:
             gather = Chain(z, own_tiles(0, f_total)).run(nz - 1)
@@ -341,17 +355,21 @@
             one, two = Chain(z, own_tiles(starts[2], starts[3])), Chain(z, own_tiles(starts[3], starts[4]))
             one.run(1)
             two.run(1)
-            one.grads, accs = compute(0, tiles, 0, None, (one.from_left[0], one.from_right[0]))
+            hold = (one.from_left[0], one.from_right[0], two.from_left[0], two.from_right[0])
+            one.grads, accs = compute(0, tiles, 0, None, (), hold)
             one.run(1)
-            after = (two.from_left[0], two.from_right[0], one.grads[3])
-            two.grads, accs = compute(1, tiles, starts[1], accs, after)
-            one.run(nz - 2)
-            grads, accs = compute(2, all_tiles(one.slots()), 0, accs)
-            three = Chain(z, None, grads)
-            two.run(nz - 1)
-            grads, accs = compute(3, all_tiles(two.slots()), 0, accs, (grads[3],))
-            four = Chain(z, None, grads)
-            sums = [one.total(), two.total(), three.run(nz - 1).total(), four.run(nz - 1).total()]
+            two.grads, accs = compute(1, tiles, starts[1], accs, (one.grads[3],), (one.from_left[1], one.from_right[1]))
+            one.run(1)
+            two.run(1)
+            mine = one.slots()
+            one.run(nz - 3)
+            two.run(1)
+            hold = (one.from_left[3], one.from_right[3], two.from_left[2], two.from_right[2])
+            grads, accs = compute(2, all_tiles(mine), 0, accs, (), hold)
+            three = Halves(z, grads)
+            last, accs = compute(3, all_tiles(two.slots()), 0, accs, (grads[3],), (three.near,))
+            two.run(nz - 3)
+            sums = [one.total(), two.total(), three.total(), Halves(z, last).total()]
 
         output, input_grad = sum_columns(accs)
         weight_grads = [jnp.concatenate([jnp.swapaxes(g[kind], 1, 2) for g in sums], axis=0) for kind in range(3)]

time: 512 us -> 476 us (0.930)
  waiting for transfers between devices: 219 us -> 194 us
  starting transfers between devices: 96.2 us -> 77.3 us
    ppermute x0 -> x4, waiting for transfers between devices: none -> 66.8 us  [the longest x2 66.8 us: total(): lax.ppermute(total_of(keep[1], got[1], far), 'row', [(r, r ^ 4) for r in...]
    ppermute x17 -> x11, waiting for transfers between devices: 94.8 us -> 29.9 us  [run(): self.from_left.append(lax.ppermute(to_right, 'row', right(start, stop)))]
    ppermute x17 -> x11, waiting for transfers between devices: 115 us -> 81.2 us  [run(): lax.ppermute(to_left, 'row', left(nz - stop, nz - start))]
    ppermute x17 -> x11, starting transfers between devices: 68.9 us -> 45.3 us  [run(): self.from_left.append(lax.ppermute(to_right, 'row', right(start, stop)))]
    ppermute x0 -> x4, starting transfers between devices: none -> 10.1 us  [the longest x2 6.59 us: total(): lax.ppermute(total_of(keep[1], got[1], far), 'row', [(r, r ^ 4) for r in...]
    ppermute x4, waiting for transfers between devices: 5.61 us -> 12.5 us  [over(): return lax.ppermute(value, 'col', [(i, i ^ offset) for i in range(n_col)])]
    select_n x4 -> x5, other arithmetic: 12.7 us -> 19 us  [run(): to_left = jnp.where(nz - 1 - self.z >= i, self.from_right[-1], to_left)]
    ppermute x17 -> x11, starting transfers between devices: 19.7 us -> 14.3 us  [run(): lax.ppermute(to_left, 'row', left(nz - stop, nz - start))]
  transfers between devices with their start and end apart: 53 -> 45, of which waited for: 23 -> 12; matrix products, arithmetic and copies ran while one was open for 9% -> 11% of each run, Pallas kernels for 18% -> 24%
where the time goes in v3:
time: 476 us; the launch traced here: 475 us
  waiting for transfers between devices  194 us (41%)
  Pallas kernels  116 us (24%)
  starting transfers between devices  77.3 us (16%)
  other arithmetic  53.5 us (11%)
  local copies, waits for them, and re-layouts  18.3 us (4%)
  between operations  15.2 us (3%)
    pallas_call x4, Pallas kernels, run_chunk(): pl.pallas_call(kernel, grid_spec=pltpu.PrefetchScalarGridSpec(num_scalar_...  116 us
    ppermute x11, waiting for transfers between devices, run(): lax.ppermute(to_left, 'row', left(nz - stop, nz - start))  81.2 us
    ppermute x2, waiting for transfers between devices, total(): lax.ppermute(total_of(keep[1], got[1], far), 'row', [(r, r ^ 4) for r in...  66.8 us
    ppermute x11, starting transfers between devices, run(): self.from_left.append(lax.ppermute(to_right, 'row', right(start, stop)))  45.3 us
    ppermute x11, waiting for transfers between devices, run(): self.from_left.append(lax.ppermute(to_right, 'row', right(start, stop)))  29.9 us
    select_n x5, other arithmetic, run(): to_left = jnp.where(nz - 1 - self.z >= i, self.from_right[-1], to_left)  19 us
    unnamed x106, local copies, waits for them, and re-layouts  16.1 us
    ppermute x11, starting transfers between devices, run(): lax.ppermute(to_left, 'row', left(nz - stop, nz - start))  14.3 us
  transfers between devices with their start and end apart: 45, of which 12 were waited for; matrix products, arithmetic and copies ran while one was open for 11% of the time, Pallas kernels for 24%

profile of v3, /device:TPU:0, one launch (start us, length us, event | category | flops | bytes accessed | tf_op | source)
XLA Modules:
  0.0 474.7 jit_solution(13994854783528029342)
XLA Ops:
  7.2 3.0 pad_maximum_fusion.2
  13.4 5.0 %collective-permute-start = (bf16[3,14,128,128]{3,2,1,0:T(8,128)(2,1)S(1)}, bf16[3,14,128,128]{3,2,1,0:T(8,128)(2,1)S(1)}, u32[]{:S(2)}, u32[]{:S(2)}) collective-permute-start(bf16[3,14,128,128]{3,2,1,0:T(8,128)(2,1)S(1)} %get-tuple-element.109), channel_id=1, source_target_pairs={{0,8},{4,12},{8,16},{12,20},{16,24},{20,28},{1,9},{5,13},{9,17},{1... | collective-permute-start | bytes 4128776 | tf_op jit(solution)/shard_map/ppermute | solution.py:259
  19.7 28.0 %collective-permute-done = bf16[3,14,128,128]{3,2,1,0:T(8,128)(2,1)S(1)} collective-permute-done((bf16[3,14,128,128]{3,2,1,0:T(8,128)(2,1)S(1)}, bf16[3,14,128,128]{3,2,1,0:T(8,128)(2,1)S(1)}, u32[]{:S(2)}, u32[]{:S(2)}) %collective-permute-start) | collective-permute-done | bytes 1376288 | tf_op jit(solution)/shard_map/ppermute | solution.py:259
  55.0 32.1 %collective-permute-done.3 = bf16[3,14,128,128]{3,2,1,0:T(8,128)(2,1)} collective-permute-done((bf16[3,14,128,128]{3,2,1,0:T(8,128)(2,1)S(1)}, bf16[3,14,128,128]{3,2,1,0:T(8,128)(2,1)}, u32[]{:S(2)}, u32[]{:S(2)}) %collective-permute-start.3) | collective-permute-done | bytes 1376288 | tf_op jit(solution)/shard_map/ppermute | solution.py:260
  92.0 27.5 %collective-permute-done.4 = bf16[3,14,128,128]{3,2,1,0:T(8,128)(2,1)} collective-permute-done((bf16[3,14,128,128]{3,2,1,0:T(8,128)(2,1)}, bf16[3,14,128,128]{3,2,1,0:T(8,128)(2,1)}, u32[]{:S(2)}, u32[]{:S(2)}) %collective-permute-start.4) | collective-permute-done | bytes 1376288 | tf_op jit(solution)/shard_map/ppermute | solution.py:260
  125.0 2.3 collective-permute-start.8
  129.8 4.6 collective-permute-start.10
  136.4 25.9 %ffn_chunk.4 = (bf16[2,3,7,128,128]{4,3,2,1,0:T(8,128)(2,1)S(1)}, bf16[2,3,7,128,128]{4,3,2,1,0:T(8,128)(2,1)S(1)}, bf16[2,3,7,128,128]{4,3,2,1,0:T(8,128)(2,1)}...) custom-call(s32[681]{0:T(1024)S(1)} %concatenate.18.scal, ...), custom_call_target="tpu_custom_call" | custom-call | flops 4227858432 | bytes 67108864 | tf_op jit(solution)/shard_map/ffn_chunk/pallas_call | solution.py:166
  164.0 3.9 collective-permute-done.12.refs_1_
  167.9 4.3 fusion.23
  173.5 6.0 %collective-permute-start.13 = (bf16[3,7,128,128]{3,2,1,0:T(8,128)(2,1)}, bf16[3,7,128,128]{3,2,1,0:T(8,128)(2,1)}, u32[]{:S(2)}, u32[]{:S(2)}) collective-permute-start(bf16[3,7,128,128]{3,2,1,0:T(8,128)(2,1)} %get-tuple-element.105), channel_id=1, source_target_pairs={{0,8},{4,12},{8,16},{12,20},{16,24},{20,28},{1,9},{5,13},{9,17},{1... | collective-permute-start | bytes 2064392 | tf_op jit(solution)/shard_map/ppermute | solution.py:259
  179.6 30.9 %ffn_chunk.5 = (bf16[2,3,7,128,128]{4,3,2,1,0:T(8,128)(2,1)S(1)}, bf16[2,3,7,128,128]{4,3,2,1,0:T(8,128)(2,1)S(1)}, bf16[2,3,7,128,128]{4,3,2,1,0:T(8,128)(2,1)S...) custom-call(s32[681]{0:T(1024)S(1)} %concatenate.18.scal, ...), custom_call_target="tpu_custom_call" | custom-call | flops 4227858432 | bytes 67108864 | tf_op jit(solution)/shard_map/ffn_chunk/pallas_call | solution.py:166
  210.6 4.8 %fusion.25 = (bf16[3,7,128,128]{3,2,1,0:T(8,128)(2,1)}, bf16[3,7,128,128]{3,2,1,0:T(8,128)(2,1)}, bf16[1,3,7,128,128]{4,3,2,1,0:T(8,128)(2,1)}) fusion(bf16[3,7,128,128]{3,2,1,0:T(8,128)(2,1)} %collective-permute-done.14, pred[]{:T(512)S(6)} %ge.16, bf16[2,3,7,128,128]{4,3,2,1,0:T(8,128)(2,1)} %collective-permute-done.15, ...), kind=kLoop, calls=%fused_computation.68 | loop fusion | flops 4128768 | bytes 4816898 | tf_op jit(solution)/shard_map/jit(_where)/select_n | solution.py:256
  216.8 5.4 %collective-permute-start.17 = (bf16[3,7,128,128]{3,2,1,0:T(8,128)(2,1)}, bf16[3,7,128,128]{3,2,1,0:T(8,128)(2,1)}, u32[]{:S(2)}, u32[]{:S(2)}) collective-permute-start(bf16[3,7,128,128]{3,2,1,0:T(8,128)(2,1)} %get-tuple-element.103), channel_id=1, source_target_pairs={{0,8},{4,12},{8,16},{12,20},{16,24},{20,28},{1,9},{5,13},{9,17},{1... | collective-permute-start | bytes 2064392 | tf_op jit(solution)/shard_map/ppermute | solution.py:259
  224.3 10.5 %collective-permute-done.16 = bf16[3,7,128,128]{3,2,1,0:T(8,128)(2,1)} collective-permute-done((bf16[3,7,128,128]{3,2,1,0:T(8,128)(2,1)}, bf16[3,7,128,128]{3,2,1,0:T(8,128)(2,1)}, u32[]{:S(2)}, u32[]{:S(2)}) %collective-permute-start.16) | collective-permute-done | bytes 688160 | tf_op jit(solution)/shard_map/ppermute | solution.py:260
  236.0 5.1 %fusion.20 = (bf16[3,7,128,128]{3,2,1,0:T(8,128)(2,1)}, bf16[3,7,128,128]{3,2,1,0:T(8,128)(2,1)}, bf16[1,3,7,128,128]{4,3,2,1,0:T(8,128)(2,1)S(1)}, bf16[1,3,7,128,128]{4,3,2,1,0:T(8,128)(2,1)S(1)}) fusion(bf16[3,7,128,128]{3,2,1,0:T(8,128)(2,1)} %collective-permute-done.16, pred[]{:T(512)S(6)} %ge.17, ...), kind=kLoop, calls=%fused_computation.63 | loop fusion | flops 5505024 | bytes 8257539 | tf_op jit(solution)/shard_map/jit(_where)/select_n | solution.py:256
  241.4 3.0 fusion.31
  245.7 5.3 %collective-permute-start.23 = (bf16[3,7,128,128]{3,2,1,0:T(8,128)(2,1)S(1)}, bf16[3,7,128,128]{3,2,1,0:T(8,128)(2,1)S(1)}, u32[]{:S(2)}, u32[]{:S(2)}) collective-permute-start(bf16[3,7,128,128]{3,2,1,0:T(8,128)(2,1)S(1)} %get-tuple-element.99), channel_id=1, source_target_pairs={{0,8},{4,12},{8,16},{12,20},{16,24},{20,28},{1,9},{5,13},{9,17},{1... | collective-permute-start | bytes 2064392 | tf_op jit(solution)/shard_map/ppermute | solution.py:259
  251.0 3.9 collective-permute-start.20
  254.9 9.8 %collective-permute-done.26 = bf16[3,7,128,128]{3,2,1,0:T(8,128)(2,1)S(1)} collective-permute-done((bf16[3,7,128,128]{3,2,1,0:T(8,128)(2,1)S(1)}, bf16[3,7,128,128]{3,2,1,0:T(8,128)(2,1)S(1)}, u32[]{:S(2)}, u32[]{:S(2)}) %collective-permute-start.26) | collective-permute-done | bytes 688160 | tf_op jit(solution)/shard_map/ppermute | solution.py:260
  268.3 4.4 collective-permute-start.25
  275.4 30.2 %ffn_chunk.6 = (bf16[2,3,7,128,128]{4,3,2,1,0:T(8,128)(2,1)S(1)}, bf16[2,3,7,128,128]{4,3,2,1,0:T(8,128)(2,1)S(1)}, bf16[2,3,7,128,128]{4,3,2,1,0:T(8,128)(2,1)S...) custom-call(s32[681]{0:T(1024)S(1)} %concatenate.18.scal, ...), custom_call_target="tpu_custom_call" | custom-call | flops 4227858432 | bytes 67108864 | tf_op jit(solution)/shard_map/ffn_chunk/pallas_call | solution.py:166
  305.8 5.8 %fusion.30 = (bf16[3,7,128,128]{3,2,1,0:T(8,128)(2,1)}, bf16[3,7,128,128]{3,2,1,0:T(8,128)(2,1)}, bf16[1,3,7,128,128]{4,3,2,1,0:T(8,128)(2,1)S(1)}, bf16[1,3,7,128,128]{4,3,2,1,0:T(8,128)(2,1)S(1)}) fusion(bf16[3,7,128,128]{3,2,1,0:T(8,128)(2,1)S(1)} %collective-permute-done.25, pred[]{:T(512)S(6)} %ge.14, ...), kind=kLoop, calls=%fused_computation.73 | loop fusion | flops 5505024 | bytes 8257539 | tf_op jit(solution)/shard_map/jit(_where)/select_n | solution.py:255
  313.7 2.7 collective-permute-start.38
  317.9 29.1 %ffn_chunk.7 = (bf16[2,3,7,128,128]{4,3,2,1,0:T(8,128)(2,1)S(1)}, bf16[2,3,7,128,128]{4,3,2,1,0:T(8,128)(2,1)S(1)}, bf16[2,3,7,128,128]{4,3,2,1,0:T(8,128)(2,1)}...) custom-call(s32[681]{0:T(1024)S(1)} %concatenate.18.scal, ...), custom_call_target="tpu_custom_call" | custom-call | flops 4227858432 | bytes 67108864 | tf_op jit(solution)/shard_map/ffn_chunk/pallas_call | solution.py:166
  357.1 4.9 %collective-permute-start.35 = (bf16[3,7,128,128]{3,2,1,0:T(8,128)(2,1)S(1)}, bf16[3,7,128,128]{3,2,1,0:T(8,128)(2,1)S(1)}, u32[]{:S(2)}, u32[]{:S(2)}) collective-permute-start(bf16[3,7,128,128]{3,2,1,0:T(8,128)(2,1)S(1)} %copy-done.43), channel_id=1, source_target_pairs={{0,8},{4,12},{8,16},{12,20},{16,24},{20,28},{1,9},{5,13},{9,17},{1... | collective-permute-start | bytes 2064392 | tf_op jit(solution)/shard_map/ppermute | solution.py:259
  362.0 12.5 %collective-permute-done.33 = bf16[2,128,2048]{2,1,0:T(8,128)(2,1)} collective-permute-done((bf16[2,128,2048]{2,1,0:T(8,128)(2,1)}, bf16[2,128,2048]{2,1,0:T(8,128)(2,1)}, u32[]{:S(2)}, u32[]{:S(2)}) %collective-permute-start.33) | collective-permute-done | bytes 1048608 | tf_op jit(solution)/shard_map/ppermute | solution.py:210
  384.1 3.1 collective-permute-start.39
  387.8 39.4 %collective-permute-done.39 = bf16[3,7,128,128]{3,2,1,0:T(8,128)(2,1)S(1)} collective-permute-done((bf16[3,7,128,128]{3,2,1,0:T(8,128)(2,1)S(1)}, bf16[3,7,128,128]{3,2,1,0:T(8,128)(2,1)S(1)}, u32[]{:S(2)}, u32[]{:S(2)}) %collective-permute-start.39) | collective-permute-done | bytes 688160 | tf_op jit(solution)/shard_map/ppermute | solution.py:283
  429.5 3.4 collective-permute-start.43
  433.0 2.6 fusion.19
  435.6 27.4 %collective-permute-done.43 = bf16[3,7,128,128]{3,2,1,0:T(8,128)(2,1)S(1)} collective-permute-done((bf16[3,7,128,128]{3,2,1,0:T(8,128)(2,1)S(1)}, bf16[3,7,128,128]{3,2,1,0:T(8,128)(2,1)S(1)}, u32[]{:S(2)}, u32[]{:S(2)}) %collective-permute-start.43) | collective-permute-done | bytes 688160 | tf_op jit(solution)/shard_map/ppermute | solution.py:283
  (220 shorter events, 72.5 us)
Async XLA Ops:
  7.2 129.2 %all-gather.3.cloned.1.call-start = ((), (), s32[]{:S(2)}) async-start(), calls=%async_computation | async-start | bytes 10485760 | tf_op jit(solution)/shard_map/all_gather | solution.py:300
  13.4 34.3 %collective-permute-start = (bf16[3,14,128,128]{3,2,1,0:T(8,128)(2,1)S(1)}, bf16[3,14,128,128]{3,2,1,0:T(8,128)(2,1)S(1)}, u32[]{:S(2)}, u32[]{:S(2)}) collective-permute-start(bf16[3,14,128,128]{3,2,1,0:T(8,128)(2,1)S(1)} %get-tuple-element.109), channel_id=1, source_target_pairs={{0,8},{4,12},{8,16},{12,20},{16,24},{20,28},{1,9},{5,13},{9,17},{1... | collective-permute-start | bytes 4128776 | tf_op jit(solution)/shard_map/ppermute | solution.py:259
  18.4 33.5 %collective-permute-start.2 = (bf16[3,14,128,128]{3,2,1,0:T(8,128)(2,1)S(1)}, bf16[3,14,128,128]{3,2,1,0:T(8,128)(2,1)S(1)}, u32[]{:S(2)}, u32[]{:S(2)}) collective-permute-start(bf16[3,14,128,128]{3,2,1,0:T(8,128)(2,1)S(1)} %get-tuple-element.109), channel_id=1, source_target_pairs={{8,0},{12,4},{16,8},{20,12},{24,16},{28,20},{9,1},{13,5},{17,9},{2... | collective-permute-start | bytes 4128776 | tf_op jit(solution)/shard_map/ppermute | solution.py:260
  51.9 35.1 %collective-permute-start.3 = (bf16[3,14,128,128]{3,2,1,0:T(8,128)(2,1)S(1)}, bf16[3,14,128,128]{3,2,1,0:T(8,128)(2,1)}, u32[]{:S(2)}, u32[]{:S(2)}) collective-permute-start(bf16[3,14,128,128]{3,2,1,0:T(8,128)(2,1)S(1)} %collective-permute-done.2), channel_id=1, source_target_pairs={{8,0},{12,4},{16,8},{20,12},{9,1},{13,5},{17,9},{21,13},{10,2},{14... | collective-permute-start | bytes 4128776 | tf_op jit(solution)/shard_map/ppermute | solution.py:260
  53.2 37.3 %collective-permute-start.5 = (bf16[3,14,128,128]{3,2,1,0:T(8,128)(2,1)}, bf16[3,14,128,128]{3,2,1,0:T(8,128)(2,1)}, u32[]{:S(2)}, u32[]{:S(2)}) collective-permute-start(bf16[3,14,128,128]{3,2,1,0:T(8,128)(2,1)} %collective-permute-done.1), channel_id=1, source_target_pairs={{16,24},{20,28},{17,25},{21,29},{18,26},{22,30},{19,27},{23,31}} | collective-permute-start | bytes 4128776 | tf_op jit(solution)/shard_map/ppermute | solution.py:259
  87.1 32.4 %collective-permute-start.4 = (bf16[3,14,128,128]{3,2,1,0:T(8,128)(2,1)}, bf16[3,14,128,128]{3,2,1,0:T(8,128)(2,1)}, u32[]{:S(2)}, u32[]{:S(2)}) collective-permute-start(bf16[3,14,128,128]{3,2,1,0:T(8,128)(2,1)} %collective-permute-done.3), channel_id=1, source_target_pairs={{8,0},{12,4},{9,1},{13,5},{10,2},{14,6},{11,3},{15,7}} | collective-permute-start | bytes 4128776 | tf_op jit(solution)/shard_map/ppermute | solution.py:260
  90.4 44.0 %collective-permute-start.6 = (bf16[2,3,14,128,128]{4,3,2,1,0:T(8,128)(2,1)S(1)}, bf16[2,3,14,128,128]{4,3,2,1,0:T(8,128)(2,1)}, u32[]{:S(2)}, u32[]{:S(2)}) collective-permute-start(bf16[2,3,14,128,128]{4,3,2,1,0:T(8,128)(2,1)S(1)} %pad_maximum_fusion.refs_1_.refs_4_), channel_id=1, source_target_pairs={{0,4},{4,0},{8,12},{12,8},{16,20},{20,16},{24,28},{28,24},{1,5},{5... | collective-permute-start | bytes 8257544 | tf_op jit(solution)/shard_map/ppermute | solution.py:213
  125.0 38.3 %collective-permute-start.8 = (bf16[3,7,128,128]{3,2,1,0:T(8,128)(2,1)}, bf16[3,7,128,128]{3,2,1,0:T(8,128)(2,1)}, u32[]{:S(2)}, u32[]{:S(2)}) collective-permute-start(bf16[3,7,128,128]{3,2,1,0:T(8,128)(2,1)} %get-tuple-element.135), channel_id=1, source_target_pairs={{0,8},{4,12},{8,16},{12,20},{16,24},{20,28},{1,9},{5,13},{9,17},{1... | collective-permute-start | bytes 2064392 | tf_op jit(solution)/shard_map/ppermute | solution.py:259
  127.3 36.1 %collective-permute-start.9 = (bf16[3,7,128,128]{3,2,1,0:T(8,128)(2,1)}, bf16[3,7,128,128]{3,2,1,0:T(8,128)(2,1)}, u32[]{:S(2)}, u32[]{:S(2)}) collective-permute-start(bf16[3,7,128,128]{3,2,1,0:T(8,128)(2,1)} %get-tuple-element.135), channel_id=1, source_target_pairs={{8,0},{12,4},{16,8},{20,12},{24,16},{28,20},{9,1},{13,5},{17,9},{2... | collective-permute-start | bytes 2064392 | tf_op jit(solution)/shard_map/ppermute | solution.py:260
  129.8 33.6 %collective-permute-start.10 = (bf16[3,7,128,128]{3,2,1,0:T(8,128)(2,1)}, bf16[3,7,128,128]{3,2,1,0:T(8,128)(2,1)S(1)}, u32[]{:S(2)}, u32[]{:S(2)}) collective-permute-start(bf16[3,7,128,128]{3,2,1,0:T(8,128)(2,1)} %get-tuple-element.132), channel_id=1, source_target_pairs={{0,8},{4,12},{8,16},{12,20},{16,24},{20,28},{1,9},{5,13},{9,17},{1... | collective-permute-start | bytes 2064392 | tf_op jit(solution)/shard_map/ppermute | solution.py:259
  134.4 29.0 %collective-permute-start.11 = (bf16[3,7,128,128]{3,2,1,0:T(8,128)(2,1)}, bf16[3,7,128,128]{3,2,1,0:T(8,128)(2,1)}, u32[]{:S(2)}, u32[]{:S(2)}) collective-permute-start(bf16[3,7,128,128]{3,2,1,0:T(8,128)(2,1)} %get-tuple-element.132), channel_id=1, source_target_pairs={{8,0},{12,4},{16,8},{20,12},{24,16},{28,20},{9,1},{13,5},{17,9},{2... | collective-permute-start | bytes 2064392 | tf_op jit(solution)/shard_map/ppermute | solution.py:260
  163.5 47.1 %collective-permute-start.15 = (bf16[2,3,7,128,128]{4,3,2,1,0:T(8,128)(2,1)}, bf16[2,3,7,128,128]{4,3,2,1,0:T(8,128)(2,1)}, u32[]{:S(2)}, u32[]{:S(2)}) collective-permute-start(bf16[2,3,7,128,128]{4,3,2,1,0:T(8,128)(2,1)} %get-tuple-element.49), channel_id=1, source_target_pairs={{0,4},{4,0},{8,12},{12,8},{16,20},{20,16},{24,28},{28,24},{1,5},{5... | collective-permute-start | bytes 4128776 | tf_op jit(solution)/shard_map/ppermute | solution.py:213
  172.2 38.3 %collective-permute-start.14 = (bf16[3,7,128,128]{3,2,1,0:T(8,128)(2,1)}, bf16[3,7,128,128]{3,2,1,0:T(8,128)(2,1)}, u32[]{:S(2)}, u32[]{:S(2)}) collective-permute-start(bf16[3,7,128,128]{3,2,1,0:T(8,128)(2,1)} %get-tuple-element.104), channel_id=1, source_target_pairs={{8,0},{12,4},{16,8},{20,12},{24,16},{28,20},{9,1},{13,5},{17,9},{2... | collective-permute-start | bytes 2064392 | tf_op jit(solution)/shard_map/ppermute | solution.py:260
  173.5 37.0 %collective-permute-start.13 = (bf16[3,7,128,128]{3,2,1,0:T(8,128)(2,1)}, bf16[3,7,128,128]{3,2,1,0:T(8,128)(2,1)}, u32[]{:S(2)}, u32[]{:S(2)}) collective-permute-start(bf16[3,7,128,128]{3,2,1,0:T(8,128)(2,1)} %get-tuple-element.105), channel_id=1, source_target_pairs={{0,8},{4,12},{8,16},{12,20},{16,24},{20,28},{1,9},{5,13},{9,17},{1... | collective-permute-start | bytes 2064392 | tf_op jit(solution)/shard_map/ppermute | solution.py:259
  210.5 30.8 %collective-permute-start.22 = (bf16[2,3,7,128,128]{4,3,2,1,0:T(8,128)(2,1)}, bf16[2,3,7,128,128]{4,3,2,1,0:T(8,128)(2,1)}, u32[]{:S(2)}, u32[]{:S(2)}) collective-permute-start(bf16[2,3,7,128,128]{4,3,2,1,0:T(8,128)(2,1)} %get-tuple-element.55), channel_id=1, source_target_pairs={{0,4},{4,0},{8,12},{12,8},{16,20},{20,16},{24,28},{28,24},{1,5},{5... | collective-permute-start | bytes 4128776 | tf_op jit(solution)/shard_map/ppermute | solution.py:213
  223.7 49.1 %collective-permute-start.18 = (bf16[2,3,7,128,128]{4,3,2,1,0:T(8,128)(2,1)S(1)}, bf16[2,3,7,128,128]{4,3,2,1,0:T(8,128)(2,1)S(1)}, u32[]{:S(2)}, u32[]{:S(2)}) collective-permute-start(bf16[2,3,7,128,128]{4,3,2,1,0:T(8,128)(2,1)S(1)} %pad_maximum_fusion.6.refs_3_), channel_id=1, source_target_pairs={{0,4},{4,0},{8,12},{12,8},{16,20},{20,16},{24,28},{28,24},{1,5},{5... | collective-permute-start | bytes 4128776 | tf_op jit(solution)/shard_map/ppermute | solution.py:213
  223.9 27.0 %collective-permute-start.24 = (bf16[2,3,7,128,128]{4,3,2,1,0:T(8,128)(2,1)S(1)}, bf16[2,3,7,128,128]{4,3,2,1,0:T(8,128)(2,1)S(1)}, u32[]{:S(2)}, u32[]{:S(2)}) collective-permute-start(bf16[2,3,7,128,128]{4,3,2,1,0:T(8,128)(2,1)S(1)} %copy-done.11), channel_id=1, source_target_pairs={{0,4},{4,0},{8,12},{12,8},{16,20},{20,16},{24,28},{28,24},{1,5},{5... | collective-permute-start | bytes 4128776 | tf_op jit(solution)/shard_map/ppermute | solution.py:213
  241.3 33.0 %collective-permute-start.19 = (bf16[2,3,7,128,128]{4,3,2,1,0:T(8,128)(2,1)S(1)}, bf16[2,3,7,128,128]{4,3,2,1,0:T(8,128)(2,1)S(1)}, u32[]{:S(2)}, u32[]{:S(2)}) collective-permute-start(bf16[2,3,7,128,128]{4,3,2,1,0:T(8,128)(2,1)S(1)} %pad_maximum_fusion.7.refs_4_), channel_id=1, source_target_pairs={{0,4},{4,0},{8,12},{12,8},{16,20},{20,16},{24,28},{28,24},{1,5},{5... | collective-permute-start | bytes 4128776 | tf_op jit(solution)/shard_map/ppermute | solution.py:213
  251.0 54.7 %collective-permute-start.20 = (bf16[3,7,128,128]{3,2,1,0:T(8,128)(2,1)}, bf16[3,7,128,128]{3,2,1,0:T(8,128)(2,1)S(1)}, u32[]{:S(2)}, u32[]{:S(2)}) collective-permute-start(bf16[3,7,128,128]{3,2,1,0:T(8,128)(2,1)} %get-tuple-element.101), channel_id=1, source_target_pairs={{0,8},{4,12},{8,16},{12,20},{16,24},{20,28},{1,9},{5,13},{9,17},{1... | collective-permute-start | bytes 2064392 | tf_op jit(solution)/shard_map/ppermute | solution.py:259
  264.7 40.9 %collective-permute-start.21 = (bf16[3,7,128,128]{3,2,1,0:T(8,128)(2,1)}, bf16[3,7,128,128]{3,2,1,0:T(8,128)(2,1)S(1)}, u32[]{:S(2)}, u32[]{:S(2)}) collective-permute-start(bf16[3,7,128,128]{3,2,1,0:T(8,128)(2,1)} %get-tuple-element.100), channel_id=1, source_target_pairs={{8,0},{12,4},{16,8},{20,12},{24,16},{28,20},{9,1},{13,5},{17,9},{2... | collective-permute-start | bytes 2064392 | tf_op jit(solution)/shard_map/ppermute | solution.py:260
  268.3 37.3 %collective-permute-start.25 = (bf16[3,7,128,128]{3,2,1,0:T(8,128)(2,1)}, bf16[3,7,128,128]{3,2,1,0:T(8,128)(2,1)S(1)}, u32[]{:S(2)}, u32[]{:S(2)}) collective-permute-start(bf16[3,7,128,128]{3,2,1,0:T(8,128)(2,1)} %get-tuple-element.97), channel_id=1, source_target_pairs={{0,8},{4,12},{8,16},{12,20},{16,24},{20,28},{1,9},{5,13},{9,17},{1... | collective-permute-start | bytes 2064392 | tf_op jit(solution)/shard_map/ppermute | solution.py:259
  272.8 32.9 %collective-permute-start.27 = (bf16[3,7,128,128]{3,2,1,0:T(8,128)(2,1)}, bf16[3,7,128,128]{3,2,1,0:T(8,128)(2,1)}, u32[]{:S(2)}, u32[]{:S(2)}) collective-permute-start(bf16[3,7,128,128]{3,2,1,0:T(8,128)(2,1)} %get-tuple-element.96), channel_id=1, source_target_pairs={{8,0},{12,4},{16,8},{20,12},{24,16},{28,20},{9,1},{13,5},{17,9},{2... | collective-permute-start | bytes 2064392 | tf_op jit(solution)/shard_map/ppermute | solution.py:260
  274.3 42.1 %collective-permute-start.29 = (bf16[2,3,7,128,128]{4,3,2,1,0:T(8,128)(2,1)S(1)}, bf16[2,3,7,128,128]{4,3,2,1,0:T(8,128)(2,1)S(1)}, u32[]{:S(2)}, u32[]{:S(2)}) collective-permute-start(bf16[2,3,7,128,128]{4,3,2,1,0:T(8,128)(2,1)S(1)} %pad_maximum_fusion.8.refs_4_), channel_id=1, source_target_pairs={{0,4},{4,0},{8,12},{12,8},{16,20},{20,16},{24,28},{28,24},{1,5},{5... | collective-permute-start | bytes 4128776 | tf_op jit(solution)/shard_map/ppermute | solution.py:213
  313.7 43.3 %collective-permute-start.38 = (bf16[2,3,7,128,128]{4,3,2,1,0:T(8,128)(2,1)}, bf16[2,3,7,128,128]{4,3,2,1,0:T(8,128)(2,1)}, u32[]{:S(2)}, u32[]{:S(2)}) collective-permute-start(bf16[2,3,7,128,128]{4,3,2,1,0:T(8,128)(2,1)} %add_convert_fusion.1), channel_id=1, source_target_pairs={{0,8},{4,12},{8,0},{12,4},{16,24},{20,28},{24,16},{28,20},{1,9},{5... | collective-permute-start | bytes 4128776 | tf_op jit(solution)/shard_map/ppermute | solution.py:277
  354.0 27.4 %collective-permute-start.37 = (bf16[2,3,7,128,128]{4,3,2,1,0:T(8,128)(2,1)S(1)}, bf16[2,3,7,128,128]{4,3,2,1,0:T(8,128)(2,1)S(1)}, u32[]{:S(2)}, u32[]{:S(2)}) collective-permute-start(bf16[2,3,7,128,128]{4,3,2,1,0:T(8,128)(2,1)S(1)} %copy-done.9), channel_id=1, source_target_pairs={{0,4},{4,0},{8,12},{12,8},{16,20},{20,16},{24,28},{28,24},{1,5},{5... | collective-permute-start | bytes 4128776 | tf_op jit(solution)/shard_map/ppermute | solution.py:213
  357.1 27.0 %collective-permute-start.35 = (bf16[3,7,128,128]{3,2,1,0:T(8,128)(2,1)S(1)}, bf16[3,7,128,128]{3,2,1,0:T(8,128)(2,1)S(1)}, u32[]{:S(2)}, u32[]{:S(2)}) collective-permute-start(bf16[3,7,128,128]{3,2,1,0:T(8,128)(2,1)S(1)} %copy-done.43), channel_id=1, source_target_pairs={{0,8},{4,12},{8,16},{12,20},{16,24},{20,28},{1,9},{5,13},{9,17},{1... | collective-permute-start | bytes 2064392 | tf_op jit(solution)/shard_map/ppermute | solution.py:259
  376.4 56.6 %collective-permute-start.34 = (bf16[2,256,2048]{2,1,0:T(8,128)(2,1)S(1)}, bf16[2,256,2048]{2,1,0:T(8,128)(2,1)S(1)}, u32[]{:S(2)}, u32[]{:S(2)}) collective-permute-start(bf16[2,256,2048]{2,1,0:T(8,128)(2,1)S(1)} %pad_maximum_fusion.4), channel_id=1, source_target_pairs={{0,2},{1,3},{2,0},{3,1},{4,6},{5,7},{6,4},{7,5},{8,10},{9,11},{10,... | collective-permute-start | bytes 6291464 | tf_op jit(solution)/shard_map/ppermute | solution.py:210
  378.5 54.5 %collective-permute-start.32 = (bf16[2,256,2048]{2,1,0:T(8,128)(2,1)S(1)}, bf16[2,256,2048]{2,1,0:T(8,128)(2,1)S(1)}, u32[]{:S(2)}, u32[]{:S(2)}) collective-permute-start(bf16[2,256,2048]{2,1,0:T(8,128)(2,1)S(1)} %pad_maximum_fusion.3), channel_id=1, source_target_pairs={{0,1},{1,0},{2,3},{3,2},{4,5},{5,4},{6,7},{7,6},{8,9},{9,8},{10,11... | collective-permute-start | bytes 6291464 | tf_op jit(solution)/shard_map/ppermute | solution.py:210
  381.5 47.6 %collective-permute-start.40 = (bf16[2,3,7,128,128]{4,3,2,1,0:T(8,128)(2,1)S(1)}, bf16[2,3,7,128,128]{4,3,2,1,0:T(8,128)(2,1)S(1)}, u32[]{:S(2)}, u32[]{:S(2)}) collective-permute-start(bf16[2,3,7,128,128]{4,3,2,1,0:T(8,128)(2,1)S(1)} %copy-done.49), channel_id=1, source_target_pairs={{0,4},{4,0},{8,12},{12,8},{16,20},{20,16},{24,28},{28,24},{1,5},{5... | collective-permute-start | bytes 4128776 | tf_op jit(solution)/shard_map/ppermute | solution.py:213
  381.5 47.6 %collective-permute-start.42 = (bf16[2,3,7,128,128]{4,3,2,1,0:T(8,128)(2,1)S(1)}, bf16[2,3,7,128,128]{4,3,2,1,0:T(8,128)(2,1)S(1)}, u32[]{:S(2)}, u32[]{:S(2)}) collective-permute-start(bf16[2,3,7,128,128]{4,3,2,1,0:T(8,128)(2,1)S(1)} %add_convert_fusion), channel_id=1, source_target_pairs={{0,8},{4,12},{8,0},{12,4},{16,24},{20,28},{24,16},{28,20},{1,9},{5... | collective-permute-start | bytes 4128776 | tf_op jit(solution)/shard_map/ppermute | solution.py:277
  384.1 43.1 %collective-permute-start.39 = (bf16[3,7,128,128]{3,2,1,0:T(8,128)(2,1)S(1)}, bf16[3,7,128,128]{3,2,1,0:T(8,128)(2,1)S(1)}, u32[]{:S(2)}, u32[]{:S(2)}) collective-permute-start(bf16[3,7,128,128]{3,2,1,0:T(8,128)(2,1)S(1)} %fusion.32), channel_id=1, source_target_pairs={{0,16},{4,20},{8,24},{12,28},{16,0},{20,4},{24,8},{28,12},{1,17},{... | collective-permute-start | bytes 2064392 | tf_op jit(solution)/shard_map/ppermute | solution.py:283
  429.5 33.5 %collective-permute-start.43 = (bf16[3,7,128,128]{3,2,1,0:T(8,128)(2,1)S(1)}, bf16[3,7,128,128]{3,2,1,0:T(8,128)(2,1)S(1)}, u32[]{:S(2)}, u32[]{:S(2)}) collective-permute-start(bf16[3,7,128,128]{3,2,1,0:T(8,128)(2,1)S(1)} %fusion.33), channel_id=1, source_target_pairs={{0,16},{4,20},{8,24},{12,28},{16,0},{20,4},{24,8},{28,12},{1,17},{... | collective-permute-start | bytes 2064392 | tf_op jit(solution)/shard_map/ppermute | solution.py:283
  (63 other events, 584.5 us)
Sparse Core Ops, SparseCore 0:
  10.4 90.2 all-gather.2

commit v4 on v3

v4 whole, which is shorter than its diff:
```python
import functools

import jax
import jax.numpy as jnp
from jax import lax
from jax.experimental import pallas as pl
from jax.experimental.pallas import tpu as pltpu
from jax.sharding import PartitionSpec as P

BS = 128
BF = jnp.bfloat16
F32 = jnp.float32


def contract(a, b, da, db):
    return lax.dot_general(a, b, (((da,), (db,)), ((), ())), preferred_element_type=F32)


def taker(refs):
    refs = list(refs)

    def take(count):
        got = refs[:count]
        del refs[:count]
        return got

    return take


def places(scal, table, f, *, kg, f_total, blocks):
    found = []
    for s in range(kg):
        block = scal[table * f_total * kg + f * kg + scal[3 * f_total * kg + s]]
        found.append((block // blocks, pl.multiple_of(lax.rem(block, blocks) * BS, BS)))
    return found


def stacked(tiles, kind, j):
    return jnp.concatenate([tile[i, kind, j] for tile in tiles for i in range(tile.shape[0])], axis=0)


def grad_kernel(scal, *refs, n_col, groups, waits, per, kg, f_total, f_first, blocks):
    take = taker(refs)
    (panels,) = take(1)
    take(waits)
    tiles = take(groups)
    tile_grads = take(groups)
    stash, x_all, y_all, load_sem = take(4)
    step = pl.program_id(0)
    both = (x_all, y_all)
    loads = [
        [pltpu.make_async_copy(panels.at[slot, kind], both[kind].at[slot], load_sem.at[kind, slot]) for slot in range(n_col)]
        for kind in range(2)
    ]

    def picked(source, table, j):
        where = places(scal, table, f_first + step * per + j, kg=kg, f_total=f_total, blocks=blocks)
        return jnp.concatenate([source[slot, :, pl.ds(at, BS)] for slot, at in where], axis=1)

    def put(kind, j, grads):
        s = 0
        for ref in tile_grads:
            for i in range(ref.shape[0]):
                ref[i, kind, j] = grads[:, s * BS : (s + 1) * BS].astype(BF)
                s += 1

    def body(before_y):
        fs = range(per)
        x_gate = [picked(x_all, 0, j) for j in fs]
        x_up = [picked(x_all, 1, j) for j in fs]
        gates = [contract(x_gate[j], stacked(tiles, 0, j), 1, 0) for j in fs]
        ups = [contract(x_up[j], stacked(tiles, 1, j), 1, 0) for j in fs]
        before_y()
        y_down = [picked(y_all, 2, j) for j in fs]
        downs = [contract(y_down[j], stacked(tiles, 2, j), 1, 0) for j in fs]
        for j in fs:
            gate, up, hidden_grad = gates[j], ups[j], downs[j]
            sig = jax.nn.sigmoid(gate)
            silu = gate * sig
            hidden = (silu * up).astype(BF)
            gate_grad = (hidden_grad * up * sig * (1.0 + gate * (1.0 - sig))).astype(BF)
            up_grad = (hidden_grad * silu).astype(BF)
            for kind, value in enumerate((gate_grad, up_grad, hidden)):
                stash[kind, j] = value
            put(2, j, contract(hidden, y_down[j], 0, 0))
            put(0, j, contract(gate_grad, x_gate[j], 0, 0))
            put(1, j, contract(up_grad, x_up[j], 0, 0))

    @pl.when(step == 0)
    def _():
        for copy in loads[0] + loads[1]:
            copy.start()
        for copy in loads[0]:
            copy.wait()

        def wait_y():
            for copy in loads[1]:
                copy.wait()

        body(wait_y)

    @pl.when(step > 0)
    def _():
        body(lambda: None)


def run_grads(scal, panels, after, tiles, *, f_total, f_first, f_here, tile_first):
    n_col, _, tokens, width = panels.shape
    kg = sum(t.shape[0] for t in tiles)
    per = 2 if f_here % 2 == 0 and tile_first % 2 == 0 else 1
    anywhere = pl.BlockSpec(memory_space=pl.ANY)

    def tile_spec(t, first):
        return pl.BlockSpec((t.shape[0], 3, per, BS, BS), lambda f, scal: (0, 0, f + first, 0, 0))

    kernel = functools.partial(
        grad_kernel,
        n_col=n_col,
        groups=len(tiles),
        waits=len(after),
        per=per,
        kg=kg,
        f_total=f_total,
        f_first=f_first,
        blocks=width // BS,
    )
    out = pl.pallas_call(
        kernel,
        grid_spec=pltpu.PrefetchScalarGridSpec(
            num_scalar_prefetch=1,
            grid=(f_here // per,),
            in_specs=[anywhere] * (1 + len(after)) + [tile_spec(t, tile_first // per) for t in tiles],
            out_specs=[tile_spec(t, 0) for t in tiles]
            + [pl.BlockSpec((3, per, tokens, BS), lambda f, scal: (0, f, 0, 0))],
            scratch_shapes=[
                pltpu.VMEM((n_col, tokens, width), BF),
                pltpu.VMEM((n_col, tokens, width), BF),
                pltpu.SemaphoreType.DMA((2, n_col)),
            ],
        ),
        out_shape=[jax.ShapeDtypeStruct((t.shape[0], 3, f_here, BS, BS), BF) for t in tiles]
        + [jax.ShapeDtypeStruct((3, f_here, tokens, BS), BF)],
        compiler_params=pltpu.CompilerParams(vmem_limit_bytes=48 * 1024 * 1024),
        cost_estimate=pl.CostEstimate(
            flops=6 * 2 * tokens * f_here * kg * BS * BS, bytes_accessed=f_here * 6 * 1024 * 1024, transcendentals=0
        ),
        name="ffn_grads",
    )(scal, panels, *after, *tiles)
    return out[: len(tiles)], out[-1]


def add_kernel(scal, *refs, n_col, pieces, groups, waits, segments, per, kg, f_total, blocks, first, last):
    take = taker(refs)
    take(waits)
    acc_in = [] if first else take(2)
    parts = [(take(1)[0], take(groups)) for _ in segments]
    results = take(len(pieces)) if last else take(2)
    totals = take(2)
    rounded = take(2) if last else []
    acc_sem, store_sem = take(2)
    step = pl.program_id(0)
    me = scal[3 * f_total * kg + kg]
    acc_loads = [pltpu.make_async_copy(src, dst, acc_sem.at[i]) for i, (src, dst) in enumerate(zip(acc_in, totals))]

    def scatter(total, where, left, right):
        for s in range(0, kg, 2):
            two = contract(left, right[s * BS : (s + 2) * BS], 1, 1)
            for i in range(2):
                slot, at = where[s + i]
                total[slot ^ me, :, pl.ds(at, BS)] += two[:, i * BS : (i + 1) * BS]

    @pl.when(step == 0)
    def _():
        for copy in acc_loads:
            copy.start()
        if first:
            for total in totals:
                total[...] = jnp.zeros_like(total)
        for copy in acc_loads:
            copy.wait()

    before = 0
    for (f_first, _, steps), (stash, tiles) in zip(segments, parts):

        @pl.when((step >= before) & (step < before + steps))
        def _():
            for j in range(per):
                f = f_first + (step - before) * per + j
                for kind, total in ((2, totals[0]), (0, totals[1]), (1, totals[1])):
                    where = places(scal, kind, f, kg=kg, f_total=f_total, blocks=blocks)
                    scatter(total, where, stash[kind, j], stacked(tiles, kind, j))

        before += steps

    @pl.when(step == before - 1)
    def _():
        stores = []
        for kind, total in enumerate(totals):
            if last:
                for s in range(n_col):
                    for t in range(0, total.shape[1], 32):
                        rounded[kind][s, t : t + 32] = total[s, t : t + 32].astype(BF)
                    here = [
                        pltpu.make_async_copy(
                            rounded[kind].at[slot, pl.ds(at, rows)], results[p].at[kind], store_sem.at[kind, p]
                        )
                        for p, (slot, at, rows) in enumerate(pieces)
                        if slot == s
                    ]
                    for copy in here:
                        copy.start()
                    stores += here
            else:
                copy = pltpu.make_async_copy(total, results[kind], acc_sem.at[kind])
                copy.start()
                stores.append(copy)
        for copy in stores:
            copy.wait()


def run_adds(scal, accs, after, parts, pieces, *, n_col, width, f_total, last):
    tokens = parts[0][1].shape[2]
    kg = sum(t.shape[0] for t in parts[0][2])
    first = accs is None
    anywhere = pl.BlockSpec(memory_space=pl.ANY)
    per = 2 if all(stash.shape[1] % 2 == 0 and at % 2 == 0 for _, stash, _, at in parts) else 1
    segments, specs, operands, before = [], [], [], 0
    for f_first, stash, tiles, at in parts:
        steps = stash.shape[1] // per

        def spot(f, before=before, steps=steps):
            return jnp.clip(f - before, 0, steps - 1)

        specs.append(pl.BlockSpec((3, per, tokens, BS), lambda f, scal, spot=spot: (0, spot(f), 0, 0)))
        for t in tiles:
            specs.append(
                pl.BlockSpec(
                    (t.shape[0], 3, per, BS, BS),
                    lambda f, scal, spot=spot, start=at // per: (0, 0, spot(f) + start, 0, 0),
                )
            )
        operands += [stash, *tiles]
        segments.append((f_first, at, steps))
        before += steps
    acc_shape = (n_col, tokens, width)
    if last:
        results = [jax.ShapeDtypeStruct((2, rows, width), BF) for _, _, rows in pieces]
    else:
        results = [jax.ShapeDtypeStruct(acc_shape, F32)] * 2
    kernel = functools.partial(
        add_kernel,
        n_col=n_col,
        pieces=pieces,
        groups=len(parts[0][2]),
        waits=len(after),
        segments=segments,
        per=per,
        kg=kg,
        f_total=f_total,
        blocks=width // BS,
        first=first,
        last=last,
    )
    return pl.pallas_call(
        kernel,
        grid_spec=pltpu.PrefetchScalarGridSpec(
            num_scalar_prefetch=1,
            grid=(before,),
            in_specs=[anywhere] * (len(after) + (0 if first else 2)) + specs,
            out_specs=[anywhere] * len(results),
            scratch_shapes=[pltpu.VMEM(acc_shape, F32)] * 2
            + ([pltpu.VMEM(acc_shape, BF)] * 2 if last else [])
            + [pltpu.SemaphoreType.DMA((2,)), pltpu.SemaphoreType.DMA((2, len(pieces)))],
        ),
        out_shape=results,
        compiler_params=pltpu.CompilerParams(vmem_limit_bytes=56 * 1024 * 1024),
        cost_estimate=pl.CostEstimate(
            flops=3 * 2 * tokens * before * per * kg * BS * BS, bytes_accessed=48 * 1024 * 1024, transcendentals=0
        ),
        name="ffn_adds",
    )(scal, *after, *([] if first else accs), *operands)


def total_of(*terms):
    value = terms[0].astype(F32)
    for term in terms[1:]:
        value = value + term.astype(F32)
    return value.astype(BF)


def make_shards(n_row, n_col):
    nz = n_row // 2
    across = [(r, r ^ 1) for r in range(n_row)]
    two_phase = n_col == 4

    def right(first, stop):
        return [(2 * z + c, 2 * z + 2 + c) for z in range(first, stop) for c in (0, 1)]

    def left(first, stop):
        return [(2 * z + c, 2 * z - 2 + c) for z in range(first, stop) for c in (0, 1)]

    def over(value, offset):
        return lax.ppermute(value, "col", [(i, i ^ offset) for i in range(n_col)])

    def swap(value):
        return lax.ppermute(value, "row", across)

    def pieces_of(tokens):
        half = tokens // 2
        if two_phase:
            return ((0, 0, tokens), (1, 0, tokens), (2, 0, tokens), (3, 0, half), (3, half, half))
        return tuple((s, 0, tokens) for s in range(n_col))

    def sum_columns(parts):
        if two_phase:
            mine, beside, above, low, high = parts
            half = low.shape[1]
            low, high = over(low, 1), over(high, 2)
            above = jnp.concatenate([total_of(above[:, :half], low), above[:, half:]], axis=1)
            beside = jnp.concatenate([beside[:, :half], total_of(beside[:, half:], high)], axis=1)
            got = [over(beside, 1), over(above, 2)]
        else:
            mine = parts[0]
            got = [over(parts[o], o) for o in range(1, n_col)]
        return [total_of(mine[i], *[g[i] for g in got]) for i in range(2)]

    class Chain:
        def __init__(self, z, own=None, grads=None):
            self.z, self.own, self.grads = z, own, grads
            self.from_left, self.from_right = [], []
            self.tick = 0 if own is not None else 1

        def part(self, slot):
            return [g[slot // 2] for g in self.grads[slot % 2 :: 2]]

        def run(self, count):
            for _ in range(count):
                i = self.tick
                summing = self.grads is not None
                if i == 0:
                    to_right = to_left = self.own
                elif not summing:
                    to_right, to_left = self.from_left[-1], self.from_right[-1]
                else:
                    to_right = total_of(*self.part(i), *self.from_left[-1:])
                    to_left = total_of(*self.part(nz - i), *self.from_right[-1:])
                    if self.own is not None:
                        to_right = jnp.where(self.z >= i, self.from_left[-1], to_right)
                        to_left = jnp.where(nz - 1 - self.z >= i, self.from_right[-1], to_left)
                start = 0 if summing else i
                stop = nz - 1 if self.own is not None else i
                self.from_left.append(lax.ppermute(to_right, "row", right(start, stop)))
                self.from_right.append(lax.ppermute(to_left, "row", left(nz - stop, nz - start)))
                self.tick += 1
            return self

        def slots(self):
            found = [self.own]
            for o in range(1, nz):
                found.append(jnp.where(self.z >= o, self.from_left[o - 1], self.from_right[nz - o - 1]))
            return found

        def total(self):
            return total_of(*self.part(0), self.from_left[-1], self.from_right[-1])

    class Halves:
        def __init__(self, z, grads):
            self.even_z = z % 2 == 0
            self.grads = grads
            self.near = lax.ppermute(total_of(grads[1], grads[3]), "row", [(r, r ^ 2) for r in range(n_row)])

        def total(self):
            keep, _, got, _ = self.grads
            far = jnp.where(self.even_z, self.near[1], self.near[0])
            mine = jnp.where(self.even_z, self.near[0], self.near[1])
            rest = lax.ppermute(total_of(keep[1], got[1], far), "row", [(r, r ^ 4) for r in range(n_row)])
            return total_of(keep[0], got[0], mine, rest)

    def shards(tokens, out_grad, gate_weight, up_weight, down_weight, gate_rows, up_rows, down_columns):
        f_total, part = gate_weight.shape[:2]
        kg = gate_rows.shape[1]
        row = lax.axis_index("row")
        z, core = row // 2, row % 2
        whole_tiles = part == BS
        slots = list(range(0, nz, 2)) + list(range(1, nz, 2))
        spots = (z - jnp.array(slots, dtype=jnp.int32)) % nz
        order = jnp.concatenate([2 * spots + core, 2 * spots + 1 - core]) if whole_tiles else spots
        scal = jnp.concatenate(
            [t.reshape(-1) for t in (gate_rows, up_rows, down_columns)]
            + [order.astype(jnp.int32), lax.axis_index("col").astype(jnp.int32).reshape(1)]
        )
        pieces = pieces_of(tokens.shape[0])
        panels = lax.all_gather(jnp.stack([tokens, out_grad]), "col")

        def own_tiles(start, stop):
            return jnp.stack([w[start:stop] for w in (gate_weight, up_weight, down_weight)])

        def all_tiles(mine):
            even, odd = jnp.stack(mine[0::2]), jnp.stack(mine[1::2])
            other_even, other_odd = swap(even), swap(odd)
            if whole_tiles:
                return [even, odd, other_even, other_odd]
            return [
                jnp.where(core == 0, jnp.concatenate([a, b], -2), jnp.concatenate([b, a], -2))
                for a, b in ((even, other_even), (odd, other_odd))
            ]

        def exchanged(tile_grads, hold):
            if whole_tiles:
                keep, give = tile_grads[:2], tile_grads[2:]
            else:
                keep = [lax.dynamic_slice_in_dim(g, core * part, part, 4) for g in tile_grads]
                give = [lax.dynamic_slice_in_dim(g, (1 - core) * part, part, 4) for g in tile_grads]
            give, _ = lax.optimization_barrier((give, hold))
            got_odd = swap(give[1])
            return [keep[0], keep[1], swap(give[0]), got_odd]

        width = tokens.shape[1]

        def compute(f_first, f_here, tiles, tile_first, after=(), hold=()):
            tile_grads, stash = run_grads(
                scal, panels, after, tiles, f_total=f_total, f_first=f_first, f_here=f_here, tile_first=tile_first
            )
            return exchanged(tile_grads, hold), (f_first, stash, tiles, tile_first)

        def add_up(accs, parts, last, after=()):
            return run_adds(scal, accs, after, parts, pieces, n_col=n_col, width=width, f_total=f_total, last=last)

        if f_total % 4 == 0 and nz == 4 and whole_tiles:
            half = f_total // 2
            big = half // 2 + half // 2 % 2
            small = half - big
            second, third, fourth = big, half, half + big
            tiles = all_tiles(Chain(z, own_tiles(0, half)).run(3).slots())
            one, two = Chain(z, own_tiles(third, fourth)).run(1), Chain(z, own_tiles(fourth, f_total)).run(1)
            hold = (one.from_left[0], one.from_right[0], two.from_left[0], two.from_right[0])
            one.grads, part_0 = compute(0, big, tiles, 0, (), hold)
            one.run(1)
            two.grads, part_1 = compute(
                second, small, tiles, second, (one.grads[3],), (one.from_left[1], one.from_right[1])
            )
            accs = add_up(None, [part_0, part_1], False)
            one.from_left[1], one.from_right[1], _ = lax.optimization_barrier(
                (one.from_left[1], one.from_right[1], two.grads[3])
            )
            one.run(1)
            two.run(1)
            mine = one.slots()
            one.run(1)
            two.run(1)
            hold = (one.from_left[3], one.from_right[3], two.from_left[2], two.from_right[2])
            grads, part_2 = compute(third, big, all_tiles(mine), 0, (accs[0],), hold)
            three = Halves(z, grads)
            last, part_3 = compute(fourth, small, all_tiles(two.slots()), 0, (grads[3],))
            accs = add_up(accs, [part_2, part_3], True, (last[3],))
            two.run(1)
            sums = [one.total(), two.total(), three.total(), Halves(z, last).total()]
        else:
            gather = Chain(z, own_tiles(0, f_total)).run(nz - 1)
            grads, part_0 = compute(0, f_total, all_tiles(gather.slots()), 0)
            accs = add_up(None, [part_0], True)
            sums = [Chain(z, None, grads).run(nz - 1).total()]

        output, input_grad = sum_columns(accs)
        weight_grads = [jnp.concatenate([jnp.swapaxes(g[kind], 1, 2) for g in sums], axis=0) for kind in range(3)]
        return (output, input_grad, *weight_grads)

    return shards


def solution(mesh):
    in_specs = (
        P("row", "col"),
        P("row", "col"),
        P("col", "row", None),
        P("col", "row", None),
        P("col", "row", None),
        P("col", None),
        P("col", None),
        P("col", None),
    )
    out_specs = in_specs[:5]
    shards = make_shards(mesh.shape["row"], mesh.shape["col"])
    return jax.shard_map(shards, mesh=mesh, in_specs=in_specs, out_specs=out_specs, check_vma=False)
```

time: 476 us -> 481 us (1.011); the launches traced: 475 us -> 473 us
  Pallas kernels: 116 us -> 99.3 us
  waiting for transfers between devices: 194 us -> 203 us
  other arithmetic: 53.5 us -> 60.2 us
    ppermute x2, waiting for transfers between devices: 66.8 us -> 23.4 us  [total(): lax.ppermute(total_of(keep[1], got[1], far), 'row', [(r, r ^ 4) for r in...]
    ppermute x2, waiting for transfers between devices: 0.01 us -> 30.3 us  [__init__(): lax.ppermute(total_of(grads[1], grads[3]), 'row', [(r, r ^ 2) for r in ra...]
    ppermute x11, waiting for transfers between devices: 81.2 us -> 110 us  [run(): lax.ppermute(to_left, 'row', left(nz - stop, nz - start))]
    pallas_call x4 -> x6, Pallas kernels: 116 us -> 99.3 us  [the longest x2 52.4 us: run_adds(): pl.pallas_call(kernel, grid_spec=pltpu.PrefetchScalarGridSpec(num_scalar_...]
    ppermute x11, waiting for transfers between devices: 29.9 us -> 14.4 us  [run(): self.from_left.append(lax.ppermute(to_right, 'row', right(start, stop)))]
    convert_element_type x11, other arithmetic: 14 us -> 20.3 us  [total_of(): return value.astype(BF)]
    ppermute x14, waiting for transfers between devices: 3.95 us -> 9.42 us  [swap(): return lax.ppermute(value, 'row', across)]
  transfers between devices with their start and end apart: 45 -> 45, of which waited for: 12 -> 18; matrix products, arithmetic and copies ran while one was open for 11% -> 11% of each run, Pallas kernels for 24% -> 19%
where the time goes in v4:
time: 481 us; the launch traced here: 473 us
  waiting for transfers between devices  203 us (42%)
  Pallas kernels  99.3 us (21%)
  starting transfers between devices  75.6 us (16%)
  other arithmetic  60.2 us (13%)
  local copies, waits for them, and re-layouts  19.7 us (4%)
  between operations  15.5 us (3%)
    ppermute x11, waiting for transfers between devices, run(): lax.ppermute(to_left, 'row', left(nz - stop, nz - start))  110 us
    pallas_call x2, Pallas kernels, run_adds(): pl.pallas_call(kernel, grid_spec=pltpu.PrefetchScalarGridSpec(num_scalar_...  52.4 us
    pallas_call x4, Pallas kernels, run_grads(): pl.pallas_call(kernel, grid_spec=pltpu.PrefetchScalarGridSpec(num_scalar_...  46.9 us
    ppermute x11, starting transfers between devices, run(): self.from_left.append(lax.ppermute(to_right, 'row', right(start, stop)))  45.8 us
    ppermute x2, waiting for transfers between devices, __init__(): lax.ppermute(total_of(grads[1], grads[3]), 'row', [(r, r ^ 2) for r in ra...  30.3 us
    ppermute x2, waiting for transfers between devices, total(): lax.ppermute(total_of(keep[1], got[1], far), 'row', [(r, r ^ 4) for r in...  23.4 us
    convert_element_type x11, other arithmetic, total_of(): return value.astype(BF)  20.3 us
    unnamed x106, local copies, waits for them, and re-layouts  17.4 us
  transfers between devices with their start and end apart: 45, of which 18 were waited for; matrix products, arithmetic and copies ran while one was open for 11% of the time, Pallas kernels for 19%

profile of v4, /device:TPU:0, one launch (start us, length us, event | category | flops | bytes accessed | tf_op | source)
XLA Modules:
  0.0 473.1 jit_solution(11430623655711795788)
XLA Ops:
  7.2 3.0 pad_maximum_fusion.2
  14.6 5.6 %collective-permute-start = (bf16[3,14,128,128]{3,2,1,0:T(8,128)(2,1)S(1)}, bf16[3,14,128,128]{3,2,1,0:T(8,128)(2,1)S(1)}, u32[]{:S(2)}, u32[]{:S(2)}) collective-permute-start(bf16[3,14,128,128]{3,2,1,0:T(8,128)(2,1)S(1)} %get-tuple-element.112), channel_id=1, source_target_pairs={{0,8},{4,12},{8,16},{12,20},{16,24},{20,28},{1,9},{5,13},{9,17},{1... | collective-permute-start | bytes 4128776 | tf_op jit(solution)/shard_map/ppermute | solution.py:352
  20.3 28.2 %collective-permute-done.2 = bf16[3,14,128,128]{3,2,1,0:T(8,128)(2,1)S(1)} collective-permute-done((bf16[3,14,128,128]{3,2,1,0:T(8,128)(2,1)S(1)}, bf16[3,14,128,128]{3,2,1,0:T(8,128)(2,1)S(1)}, u32[]{:S(2)}, u32[]{:S(2)}) %collective-permute-start.2) | collective-permute-done | bytes 1376288 | tf_op jit(solution)/shard_map/ppermute | solution.py:353
  52.6 30.4 %collective-permute-done.3 = bf16[3,14,128,128]{3,2,1,0:T(8,128)(2,1)} collective-permute-done((bf16[3,14,128,128]{3,2,1,0:T(8,128)(2,1)S(1)}, bf16[3,14,128,128]{3,2,1,0:T(8,128)(2,1)}, u32[]{:S(2)}, u32[]{:S(2)}) %collective-permute-start.3) | collective-permute-done | bytes 1376288 | tf_op jit(solution)/shard_map/ppermute | solution.py:353
  88.2 27.6 %collective-permute-done.4 = bf16[3,14,128,128]{3,2,1,0:T(8,128)(2,1)} collective-permute-done((bf16[3,14,128,128]{3,2,1,0:T(8,128)(2,1)}, bf16[3,14,128,128]{3,2,1,0:T(8,128)(2,1)}, u32[]{:S(2)}, u32[]{:S(2)}) %collective-permute-start.4) | collective-permute-done | bytes 1376288 | tf_op jit(solution)/shard_map/ppermute | solution.py:353
  125.4 6.1 %collective-permute-start.10 = (bf16[3,6,128,128]{3,2,1,0:T(8,128)(2,1)}, bf16[3,6,128,128]{3,2,1,0:T(8,128)(2,1)}, u32[]{:S(2)}, u32[]{:S(2)}) collective-permute-start(bf16[3,6,128,128]{3,2,1,0:T(8,128)(2,1)} %get-tuple-element.133), channel_id=1, source_target_pairs={{0,8},{4,12},{8,16},{12,20},{16,24},{20,28},{1,9},{5,13},{9,17},{1... | collective-permute-start | bytes 1769480 | tf_op jit(solution)/shard_map/ppermute | solution.py:352
  133.5 12.6 %ffn_grads.4 = (bf16[2,3,8,128,128]{4,3,2,1,0:T(8,128)(2,1)S(1)}, bf16[2,3,8,128,128]{4,3,2,1,0:T(8,128)(2,1)S(1)}, bf16[2,3,8,128,128]{4,3,2,1,0:T(8,128)(2,1)}...) custom-call(s32[681]{0:T(1024)S(1)} %concatenate.18.scal, bf16[4,2,256,2048]{3,2,1,0:T(8,128)(2,1)} %bitcast.188, ...), custom_call_target="tpu_custom_call" | custom-call | flops 3221225472 | bytes 50331648 | tf_op jit(solution)/shard_map/ffn_grads/pallas_call | solution.py:127
  147.3 5.5 %collective-permute-done.10 = bf16[3,6,128,128]{3,2,1,0:T(8,128)(2,1)} collective-permute-done((bf16[3,6,128,128]{3,2,1,0:T(8,128)(2,1)}, bf16[3,6,128,128]{3,2,1,0:T(8,128)(2,1)}, u32[]{:S(2)}, u32[]{:S(2)}) %collective-permute-start.10) | collective-permute-done | bytes 589856 | tf_op jit(solution)/shard_map/ppermute | solution.py:352
  152.7 4.7 %collective-permute-done.11 = bf16[3,6,128,128]{3,2,1,0:T(8,128)(2,1)S(1)} collective-permute-done((bf16[3,6,128,128]{3,2,1,0:T(8,128)(2,1)}, bf16[3,6,128,128]{3,2,1,0:T(8,128)(2,1)S(1)}, u32[]{:S(2)}, u32[]{:S(2)}) %collective-permute-start.11) | collective-permute-done | bytes 589856 | tf_op jit(solution)/shard_map/ppermute | solution.py:353
  157.6 3.7 collective-permute-done.12.refs_1_
  164.3 6.7 %collective-permute-start.13 = (bf16[3,8,128,128]{3,2,1,0:T(8,128)(2,1)S(1)}, bf16[3,8,128,128]{3,2,1,0:T(8,128)(2,1)}, u32[]{:S(2)}, u32[]{:S(2)}) collective-permute-start(bf16[3,8,128,128]{3,2,1,0:T(8,128)(2,1)S(1)} %get-tuple-element.103), channel_id=1, source_target_pairs={{0,8},{4,12},{8,16},{12,20},{16,24},{20,28},{1,9},{5,13},{9,17},{1... | collective-permute-start | bytes 2359304 | tf_op jit(solution)/shard_map/ppermute | solution.py:352
  172.5 10.7 %ffn_grads.5 = (bf16[2,3,6,128,128]{4,3,2,1,0:T(8,128)(2,1)S(1)}, bf16[2,3,6,128,128]{4,3,2,1,0:T(8,128)(2,1)S(1)}, bf16[2,3,6,128,128]{4,3,2,1,0:T(8,128)(2,1)S...) custom-call(s32[681]{0:T(1024)S(1)} %concatenate.18.scal, bf16[4,2,256,2048]{3,2,1,0:T(8,128)(2,1)} %bitcast.189, ...), custom_call_target="tpu_custom_call" | custom-call | flops 2415919104 | bytes 37748736 | tf_op jit(solution)/shard_map/ffn_grads/pallas_call | solution.py:127
  187.1 5.1 %collective-permute-done.14 = bf16[3,8,128,128]{3,2,1,0:T(8,128)(2,1)} collective-permute-done((bf16[3,8,128,128]{3,2,1,0:T(8,128)(2,1)S(1)}, bf16[3,8,128,128]{3,2,1,0:T(8,128)(2,1)}, u32[]{:S(2)}, u32[]{:S(2)}) %collective-permute-start.14) | collective-permute-done | bytes 786464 | tf_op jit(solution)/shard_map/ppermute | solution.py:353
  192.2 3.2 collective-permute-done.15
  195.4 4.8 %fusion.14 = (bf16[3,8,128,128]{3,2,1,0:T(8,128)(2,1)}, bf16[3,8,128,128]{3,2,1,0:T(8,128)(2,1)}, bf16[1,3,8,128,128]{4,3,2,1,0:T(8,128)(2,1)}) fusion(bf16[3,8,128,128]{3,2,1,0:T(8,128)(2,1)} %collective-permute-done.14, pred[]{:T(512)S(6)} %ge.16, bf16[2,3,8,128,128]{4,3,2,1,0:T(8,128)(2,1)} %collective-permute-done.16, ...), kind=kLoop, calls=%fused_computation.43 | loop fusion | flops 4718592 | bytes 5505026 | tf_op jit(solution)/shard_map/jit(_where)/select_n | solution.py:349
  201.5 5.5 %collective-permute-start.18 = (bf16[3,8,128,128]{3,2,1,0:T(8,128)(2,1)}, bf16[3,8,128,128]{3,2,1,0:T(8,128)(2,1)}, u32[]{:S(2)}, u32[]{:S(2)}) collective-permute-start(bf16[3,8,128,128]{3,2,1,0:T(8,128)(2,1)} %get-tuple-element.101), channel_id=1, source_target_pairs={{0,8},{4,12},{8,16},{12,20},{16,24},{20,28},{1,9},{5,13},{9,17},{1... | collective-permute-start | bytes 2359304 | tf_op jit(solution)/shard_map/ppermute | solution.py:352
  209.1 12.9 %collective-permute-done.17 = bf16[3,8,128,128]{3,2,1,0:T(8,128)(2,1)} collective-permute-done((bf16[3,8,128,128]{3,2,1,0:T(8,128)(2,1)}, bf16[3,8,128,128]{3,2,1,0:T(8,128)(2,1)}, u32[]{:S(2)}, u32[]{:S(2)}) %collective-permute-start.17) | collective-permute-done | bytes 786464 | tf_op jit(solution)/shard_map/ppermute | solution.py:353
  223.1 5.4 %fusion.9 = (bf16[3,8,128,128]{3,2,1,0:T(8,128)(2,1)}, bf16[3,8,128,128]{3,2,1,0:T(8,128)(2,1)}, bf16[1,3,8,128,128]{4,3,2,1,0:T(8,128)(2,1)S(1)}, bf16[1,3,8,128,128]{4,3,2,1,0:T(8,128)(2,1)S(1)}) fusion(bf16[3,8,128,128]{3,2,1,0:T(8,128)(2,1)} %collective-permute-done.17, pred[]{:T(512)S(6)} %ge.17, ...), kind=kLoop, calls=%fused_computation.38 | loop fusion | flops 6291456 | bytes 9437187 | tf_op jit(solution)/shard_map/jit(_where)/select_n | solution.py:349
  232.1 4.4 collective-permute-start.23
  237.8 5.5 %collective-permute-start.21 = (bf16[3,8,128,128]{3,2,1,0:T(8,128)(2,1)}, bf16[3,8,128,128]{3,2,1,0:T(8,128)(2,1)}, u32[]{:S(2)}, u32[]{:S(2)}) collective-permute-start(bf16[3,8,128,128]{3,2,1,0:T(8,128)(2,1)} %get-tuple-element.99), channel_id=1, source_target_pairs={{0,8},{4,12},{8,16},{12,20},{16,24},{20,28},{1,9},{5,13},{9,17},{1... | collective-permute-start | bytes 2359304 | tf_op jit(solution)/shard_map/ppermute | solution.py:352
  243.3 6.9 %collective-permute-done.23 = bf16[3,6,128,128]{3,2,1,0:T(8,128)(2,1)S(1)} collective-permute-done((bf16[3,6,128,128]{3,2,1,0:T(8,128)(2,1)S(1)}, bf16[3,6,128,128]{3,2,1,0:T(8,128)(2,1)S(1)}, u32[]{:S(2)}, u32[]{:S(2)}) %collective-permute-start.23) | collective-permute-done | bytes 589856 | tf_op jit(solution)/shard_map/ppermute | solution.py:352
  254.6 4.4 collective-permute-start.25
  260.5 25.1 %ffn_adds.2 = (f32[4,256,2048]{2,1,0:T(8,128)}, f32[4,256,2048]{2,1,0:T(8,128)}) custom-call(s32[681]{0:T(1024)} %copy-done.9, bf16[3,8,256,128]{3,2,1,0:T(8,128)(2,1)} %get-tuple-element.42.refs_0_, bf16[2,3,14,128,128]{4,3,2,1,0:T(8,128)(2,1)} %copy-done.14, bf16[2,3,14,128,128]{4,3,2,1,0:T(8,128)(2,1)} %pad_maximum_fusion.1.refs_2_.refs_3_.refs_7_, ...), custom_call_target="tpu_custom_call" | custom-call | flops 2818572288 | bytes 50331648 | tf_op jit(solution)/shard_map/ffn_adds/pallas_call | solution.py:264
  287.0 12.6 %ffn_grads.6 = (bf16[2,3,8,128,128]{4,3,2,1,0:T(8,128)(2,1)S(1)}, bf16[2,3,8,128,128]{4,3,2,1,0:T(8,128)(2,1)S(1)}, bf16[2,3,8,128,128]{4,3,2,1,0:T(8,128)(2,1)}...) custom-call(s32[681]{0:T(1024)S(1)} %copy-done.10, bf16[4,2,256,2048]{3,2,1,0:T(8,128)(2,1)} %bitcast.190, ...), custom_call_target="tpu_custom_call" | custom-call | flops 3221225472 | bytes 50331648 | tf_op jit(solution)/shard_map/ffn_grads/pallas_call | solution.py:127
  299.7 4.1 fusion.30
  309.1 10.9 %ffn_grads.7 = (bf16[2,3,6,128,128]{4,3,2,1,0:T(8,128)(2,1)S(1)}, bf16[2,3,6,128,128]{4,3,2,1,0:T(8,128)(2,1)S(1)}, bf16[2,3,6,128,128]{4,3,2,1,0:T(8,128)(2,1)S...) custom-call(s32[681]{0:T(1024)S(1)} %copy-done.10, bf16[4,2,256,2048]{3,2,1,0:T(8,128)(2,1)} %bitcast.191, ...), custom_call_target="tpu_custom_call" | custom-call | flops 2415919104 | bytes 37748736 | tf_op jit(solution)/shard_map/ffn_grads/pallas_call | solution.py:127
  320.6 4.0 add_convert_fusion
  330.3 27.4 %ffn_adds.3 = (bf16[2,256,2048]{2,1,0:T(8,128)(2,1)}, bf16[2,256,2048]{2,1,0:T(8,128)(2,1)}, bf16[2,256,2048]{2,1,0:T(8,128)(2,1)}, bf16[2,128,2048]{2,1,0:T(8,128)(2,1)}, bf16[2,128,2048]{2,1,0:T(8,128)(2,1)}) custom-call(s32[681]{0:T(1024)} %copy-done.9, bf16[2,3,6,128,128]{4,3,2,1,0:T(8,128)(2,1)} %collective-permute-done.31.refs_0_, ...), custom_call_target="tpu_custom_call" | custom-call | flops 2818572288 | bytes 50331648 | tf_op jit(solution)/shard_map/ffn_adds/pallas_call | solution.py:264
  369.9 13.4 %collective-permute-done.32 = bf16[2,128,2048]{2,1,0:T(8,128)(2,1)S(1)} collective-permute-done((bf16[2,128,2048]{2,1,0:T(8,128)(2,1)}, bf16[2,128,2048]{2,1,0:T(8,128)(2,1)S(1)}, u32[]{:S(2)}, u32[]{:S(2)}) %collective-permute-start.32) | collective-permute-done | bytes 1048608 | tf_op jit(solution)/shard_map/ppermute | solution.py:303
  397.2 30.3 %collective-permute-done.42 = bf16[2,3,6,128,128]{4,3,2,1,0:T(8,128)(2,1)S(1)} collective-permute-done((bf16[2,3,6,128,128]{4,3,2,1,0:T(8,128)(2,1)S(1)}, bf16[2,3,6,128,128]{4,3,2,1,0:T(8,128)(2,1)S(1)}, u32[]{:S(2)}, u32[]{:S(2)}) %collective-permute-start.42) | collective-permute-done | bytes 1179680 | tf_op jit(solution)/shard_map/ppermute | solution.py:370
  431.0 23.4 %collective-permute-done.43 = bf16[3,6,128,128]{3,2,1,0:T(8,128)(2,1)S(1)} collective-permute-done((bf16[3,6,128,128]{3,2,1,0:T(8,128)(2,1)S(1)}, bf16[3,6,128,128]{3,2,1,0:T(8,128)(2,1)S(1)}, u32[]{:S(2)}, u32[]{:S(2)}) %collective-permute-start.43) | collective-permute-done | bytes 589856 | tf_op jit(solution)/shard_map/ppermute | solution.py:376
  461.0 4.7 fusion.25
  (224 shorter events, 98.9 us)
Async XLA Ops:
  7.2 126.3 %all-gather.3.cloned.1.call-start = ((), (), s32[]{:S(2)}) async-start(), calls=%async_computation | async-start | bytes 10485760 | tf_op jit(solution)/shard_map/all_gather | solution.py:393
  13.3 35.1 %collective-permute-start.2 = (bf16[3,14,128,128]{3,2,1,0:T(8,128)(2,1)S(1)}, bf16[3,14,128,128]{3,2,1,0:T(8,128)(2,1)S(1)}, u32[]{:S(2)}, u32[]{:S(2)}) collective-permute-start(bf16[3,14,128,128]{3,2,1,0:T(8,128)(2,1)S(1)} %get-tuple-element.112), channel_id=1, source_target_pairs={{8,0},{12,4},{16,8},{20,12},{24,16},{28,20},{9,1},{13,5},{17,9},{2... | collective-permute-start | bytes 4128776 | tf_op jit(solution)/shard_map/ppermute | solution.py:353
  14.6 36.2 %collective-permute-start = (bf16[3,14,128,128]{3,2,1,0:T(8,128)(2,1)S(1)}, bf16[3,14,128,128]{3,2,1,0:T(8,128)(2,1)S(1)}, u32[]{:S(2)}, u32[]{:S(2)}) collective-permute-start(bf16[3,14,128,128]{3,2,1,0:T(8,128)(2,1)S(1)} %get-tuple-element.112), channel_id=1, source_target_pairs={{0,8},{4,12},{8,16},{12,20},{16,24},{20,28},{1,9},{5,13},{9,17},{1... | collective-permute-start | bytes 4128776 | tf_op jit(solution)/shard_map/ppermute | solution.py:352
  49.5 33.5 %collective-permute-start.3 = (bf16[3,14,128,128]{3,2,1,0:T(8,128)(2,1)S(1)}, bf16[3,14,128,128]{3,2,1,0:T(8,128)(2,1)}, u32[]{:S(2)}, u32[]{:S(2)}) collective-permute-start(bf16[3,14,128,128]{3,2,1,0:T(8,128)(2,1)S(1)} %collective-permute-done.2), channel_id=1, source_target_pairs={{8,0},{12,4},{16,8},{20,12},{9,1},{13,5},{17,9},{21,13},{10,2},{14... | collective-permute-start | bytes 4128776 | tf_op jit(solution)/shard_map/ppermute | solution.py:353
  50.8 33.4 %collective-permute-start.1 = (bf16[3,14,128,128]{3,2,1,0:T(8,128)(2,1)S(1)}, bf16[3,14,128,128]{3,2,1,0:T(8,128)(2,1)}, u32[]{:S(2)}, u32[]{:S(2)}) collective-permute-start(bf16[3,14,128,128]{3,2,1,0:T(8,128)(2,1)S(1)} %collective-permute-done), channel_id=1, source_target_pairs={{8,16},{12,20},{16,24},{20,28},{9,17},{13,21},{17,25},{21,29},{10,... | collective-permute-start | bytes 4128776 | tf_op jit(solution)/shard_map/ppermute | solution.py:352
  83.0 32.8 %collective-permute-start.4 = (bf16[3,14,128,128]{3,2,1,0:T(8,128)(2,1)}, bf16[3,14,128,128]{3,2,1,0:T(8,128)(2,1)}, u32[]{:S(2)}, u32[]{:S(2)}) collective-permute-start(bf16[3,14,128,128]{3,2,1,0:T(8,128)(2,1)} %collective-permute-done.3), channel_id=1, source_target_pairs={{8,0},{12,4},{9,1},{13,5},{10,2},{14,6},{11,3},{15,7}} | collective-permute-start | bytes 4128776 | tf_op jit(solution)/shard_map/ppermute | solution.py:353
  84.3 33.0 %collective-permute-start.5 = (bf16[3,14,128,128]{3,2,1,0:T(8,128)(2,1)}, bf16[3,14,128,128]{3,2,1,0:T(8,128)(2,1)}, u32[]{:S(2)}, u32[]{:S(2)}) collective-permute-start(bf16[3,14,128,128]{3,2,1,0:T(8,128)(2,1)} %collective-permute-done.1), channel_id=1, source_target_pairs={{16,24},{20,28},{17,25},{21,29},{18,26},{22,30},{19,27},{23,31}} | collective-permute-start | bytes 4128776 | tf_op jit(solution)/shard_map/ppermute | solution.py:352
  88.1 43.4 %collective-permute-start.6 = (bf16[2,3,14,128,128]{4,3,2,1,0:T(8,128)(2,1)S(1)}, bf16[2,3,14,128,128]{4,3,2,1,0:T(8,128)(2,1)}, u32[]{:S(2)}, u32[]{:S(2)}) collective-permute-start(bf16[2,3,14,128,128]{4,3,2,1,0:T(8,128)(2,1)S(1)} %pad_maximum_fusion.refs_1_.refs_2_.refs_6_), channel_id=1, source_target_pairs={{0,4},{4,0},{8,12},{12,8},{16,20},{20,16},{24,28},{28,24},{1,5},{5... | collective-permute-start | bytes 8257544 | tf_op jit(solution)/shard_map/ppermute | solution.py:306
  121.5 36.0 %collective-permute-start.8 = (bf16[3,8,128,128]{3,2,1,0:T(8,128)(2,1)}, bf16[3,8,128,128]{3,2,1,0:T(8,128)(2,1)S(1)}, u32[]{:S(2)}, u32[]{:S(2)}) collective-permute-start(bf16[3,8,128,128]{3,2,1,0:T(8,128)(2,1)} %get-tuple-element.123), channel_id=1, source_target_pairs={{0,8},{4,12},{8,16},{12,20},{16,24},{20,28},{1,9},{5,13},{9,17},{1... | collective-permute-start | bytes 2359304 | tf_op jit(solution)/shard_map/ppermute | solution.py:352
  123.0 34.5 %collective-permute-start.9 = (bf16[3,8,128,128]{3,2,1,0:T(8,128)(2,1)}, bf16[3,8,128,128]{3,2,1,0:T(8,128)(2,1)}, u32[]{:S(2)}, u32[]{:S(2)}) collective-permute-start(bf16[3,8,128,128]{3,2,1,0:T(8,128)(2,1)} %get-tuple-element.123), channel_id=1, source_target_pairs={{8,0},{12,4},{16,8},{20,12},{24,16},{28,20},{9,1},{13,5},{17,9},{2... | collective-permute-start | bytes 2359304 | tf_op jit(solution)/shard_map/ppermute | solution.py:353
  125.4 27.3 %collective-permute-start.10 = (bf16[3,6,128,128]{3,2,1,0:T(8,128)(2,1)}, bf16[3,6,128,128]{3,2,1,0:T(8,128)(2,1)}, u32[]{:S(2)}, u32[]{:S(2)}) collective-permute-start(bf16[3,6,128,128]{3,2,1,0:T(8,128)(2,1)} %get-tuple-element.133), channel_id=1, source_target_pairs={{0,8},{4,12},{8,16},{12,20},{16,24},{20,28},{1,9},{5,13},{9,17},{1... | collective-permute-start | bytes 1769480 | tf_op jit(solution)/shard_map/ppermute | solution.py:352
  131.5 26.0 %collective-permute-start.11 = (bf16[3,6,128,128]{3,2,1,0:T(8,128)(2,1)}, bf16[3,6,128,128]{3,2,1,0:T(8,128)(2,1)S(1)}, u32[]{:S(2)}, u32[]{:S(2)}) collective-permute-start(bf16[3,6,128,128]{3,2,1,0:T(8,128)(2,1)} %get-tuple-element.133), channel_id=1, source_target_pairs={{8,0},{12,4},{16,8},{20,12},{24,16},{28,20},{9,1},{13,5},{17,9},{2... | collective-permute-start | bytes 1769480 | tf_op jit(solution)/shard_map/ppermute | solution.py:353
  172.4 23.0 %collective-permute-start.16 = (bf16[2,3,8,128,128]{4,3,2,1,0:T(8,128)(2,1)}, bf16[2,3,8,128,128]{4,3,2,1,0:T(8,128)(2,1)}, u32[]{:S(2)}, u32[]{:S(2)}) collective-permute-start(bf16[2,3,8,128,128]{4,3,2,1,0:T(8,128)(2,1)} %get-tuple-element.55), channel_id=1, source_target_pairs={{0,4},{4,0},{8,12},{12,8},{16,20},{20,16},{24,28},{28,24},{1,5},{5... | collective-permute-start | bytes 4718600 | tf_op jit(solution)/shard_map/ppermute | solution.py:306
  207.0 30.8 %collective-permute-start.24 = (bf16[2,3,6,128,128]{4,3,2,1,0:T(8,128)(2,1)}, bf16[2,3,6,128,128]{4,3,2,1,0:T(8,128)(2,1)S(1)}, u32[]{:S(2)}, u32[]{:S(2)}) collective-permute-start(bf16[2,3,6,128,128]{4,3,2,1,0:T(8,128)(2,1)} %copy-done.13), channel_id=1, source_target_pairs={{0,4},{4,0},{8,12},{12,8},{16,20},{20,16},{24,28},{28,24},{1,5},{5... | collective-permute-start | bytes 3538952 | tf_op jit(solution)/shard_map/ppermute | solution.py:306
  208.5 50.5 %collective-permute-start.19 = (bf16[2,3,8,128,128]{4,3,2,1,0:T(8,128)(2,1)S(1)}, bf16[2,3,8,128,128]{4,3,2,1,0:T(8,128)(2,1)S(1)}, u32[]{:S(2)}, u32[]{:S(2)}) collective-permute-start(bf16[2,3,8,128,128]{4,3,2,1,0:T(8,128)(2,1)S(1)} %pad_maximum_fusion.5.refs_2_.refs_4_), channel_id=1, source_target_pairs={{0,4},{4,0},{8,12},{12,8},{16,20},{20,16},{24,28},{28,24},{1,5},{5... | collective-permute-start | bytes 4718600 | tf_op jit(solution)/shard_map/ppermute | solution.py:306
  228.8 57.0 %collective-permute-start.20 = (bf16[2,3,8,128,128]{4,3,2,1,0:T(8,128)(2,1)S(1)}, bf16[2,3,8,128,128]{4,3,2,1,0:T(8,128)(2,1)S(1)}, u32[]{:S(2)}, u32[]{:S(2)}) collective-permute-start(bf16[2,3,8,128,128]{4,3,2,1,0:T(8,128)(2,1)S(1)} %pad_maximum_fusion.6.refs_3_.refs_5_), channel_id=1, source_target_pairs={{0,4},{4,0},{8,12},{12,8},{16,20},{20,16},{24,28},{28,24},{1,5},{5... | collective-permute-start | bytes 4718600 | tf_op jit(solution)/shard_map/ppermute | solution.py:306
  237.8 61.8 %collective-permute-start.21 = (bf16[3,8,128,128]{3,2,1,0:T(8,128)(2,1)}, bf16[3,8,128,128]{3,2,1,0:T(8,128)(2,1)}, u32[]{:S(2)}, u32[]{:S(2)}) collective-permute-start(bf16[3,8,128,128]{3,2,1,0:T(8,128)(2,1)} %get-tuple-element.99), channel_id=1, source_target_pairs={{0,8},{4,12},{8,16},{12,20},{16,24},{20,28},{1,9},{5,13},{9,17},{1... | collective-permute-start | bytes 2359304 | tf_op jit(solution)/shard_map/ppermute | solution.py:352
  250.2 49.4 %collective-permute-start.22 = (bf16[3,8,128,128]{3,2,1,0:T(8,128)(2,1)}, bf16[3,8,128,128]{3,2,1,0:T(8,128)(2,1)}, u32[]{:S(2)}, u32[]{:S(2)}) collective-permute-start(bf16[3,8,128,128]{3,2,1,0:T(8,128)(2,1)} %get-tuple-element.98), channel_id=1, source_target_pairs={{8,0},{12,4},{16,8},{20,12},{24,16},{28,20},{9,1},{13,5},{17,9},{2... | collective-permute-start | bytes 2359304 | tf_op jit(solution)/shard_map/ppermute | solution.py:353
  254.6 44.9 %collective-permute-start.25 = (bf16[3,6,128,128]{3,2,1,0:T(8,128)(2,1)}, bf16[3,6,128,128]{3,2,1,0:T(8,128)(2,1)}, u32[]{:S(2)}, u32[]{:S(2)}) collective-permute-start(bf16[3,6,128,128]{3,2,1,0:T(8,128)(2,1)} %get-tuple-element.107), channel_id=1, source_target_pairs={{0,8},{4,12},{8,16},{12,20},{16,24},{20,28},{1,9},{5,13},{9,17},{1... | collective-permute-start | bytes 1769480 | tf_op jit(solution)/shard_map/ppermute | solution.py:352
  259.0 40.6 %collective-permute-start.27 = (bf16[3,6,128,128]{3,2,1,0:T(8,128)(2,1)}, bf16[3,6,128,128]{3,2,1,0:T(8,128)(2,1)}, u32[]{:S(2)}, u32[]{:S(2)}) collective-permute-start(bf16[3,6,128,128]{3,2,1,0:T(8,128)(2,1)} %get-tuple-element.106), channel_id=1, source_target_pairs={{8,0},{12,4},{16,8},{20,12},{24,16},{28,20},{9,1},{13,5},{17,9},{2... | collective-permute-start | bytes 1769480 | tf_op jit(solution)/shard_map/ppermute | solution.py:353
  320.5 45.6 %collective-permute-start.38 = (bf16[2,3,8,128,128]{4,3,2,1,0:T(8,128)(2,1)}, bf16[2,3,8,128,128]{4,3,2,1,0:T(8,128)(2,1)}, u32[]{:S(2)}, u32[]{:S(2)}) collective-permute-start(bf16[2,3,8,128,128]{4,3,2,1,0:T(8,128)(2,1)} %get-tuple-element.74), channel_id=1, source_target_pairs={{0,4},{4,0},{8,12},{12,8},{16,20},{20,16},{24,28},{28,24},{1,5},{5... | collective-permute-start | bytes 4718600 | tf_op jit(solution)/shard_map/ppermute | solution.py:306
  324.6 43.1 %collective-permute-start.39 = (bf16[2,3,8,128,128]{4,3,2,1,0:T(8,128)(2,1)}, bf16[2,3,8,128,128]{4,3,2,1,0:T(8,128)(2,1)}, u32[]{:S(2)}, u32[]{:S(2)}) collective-permute-start(bf16[2,3,8,128,128]{4,3,2,1,0:T(8,128)(2,1)} %add_convert_fusion), channel_id=1, source_target_pairs={{0,8},{4,12},{8,0},{12,4},{16,24},{20,28},{24,16},{28,20},{1,9},{5... | collective-permute-start | bytes 4718600 | tf_op jit(solution)/shard_map/ppermute | solution.py:370
  327.6 66.0 %collective-permute-start.36 = (bf16[3,6,128,128]{3,2,1,0:T(8,128)(2,1)}, bf16[3,6,128,128]{3,2,1,0:T(8,128)(2,1)}, u32[]{:S(2)}, u32[]{:S(2)}) collective-permute-start(bf16[3,6,128,128]{3,2,1,0:T(8,128)(2,1)} %get-tuple-element.104), channel_id=1, source_target_pairs={{0,8},{4,12},{8,16},{12,20},{16,24},{20,28},{1,9},{5,13},{9,17},{1... | collective-permute-start | bytes 1769480 | tf_op jit(solution)/shard_map/ppermute | solution.py:352
  357.7 25.5 %collective-permute-start.32 = (bf16[2,128,2048]{2,1,0:T(8,128)(2,1)}, bf16[2,128,2048]{2,1,0:T(8,128)(2,1)S(1)}, u32[]{:S(2)}, u32[]{:S(2)}) collective-permute-start(bf16[2,128,2048]{2,1,0:T(8,128)(2,1)} %get-tuple-element.70), channel_id=1, source_target_pairs={{0,2},{1,3},{2,0},{3,1},{4,6},{5,7},{6,4},{7,5},{8,10},{9,11},{10,... | collective-permute-start | bytes 3145736 | tf_op jit(solution)/shard_map/ppermute | solution.py:303
  362.8 24.9 %collective-permute-start.34 = (bf16[2,128,2048]{2,1,0:T(8,128)(2,1)S(1)}, bf16[2,128,2048]{2,1,0:T(8,128)(2,1)S(1)}, u32[]{:S(2)}, u32[]{:S(2)}) collective-permute-start(bf16[2,128,2048]{2,1,0:T(8,128)(2,1)S(1)} %copy-done.49), channel_id=1, source_target_pairs={{0,1},{1,0},{2,3},{3,2},{4,5},{5,4},{6,7},{7,6},{8,9},{9,8},{10,11... | collective-permute-start | bytes 3145736 | tf_op jit(solution)/shard_map/ppermute | solution.py:303
  366.1 28.9 %collective-permute-start.37 = (bf16[3,6,128,128]{3,2,1,0:T(8,128)(2,1)S(1)}, bf16[3,6,128,128]{3,2,1,0:T(8,128)(2,1)S(1)}, u32[]{:S(2)}, u32[]{:S(2)}) collective-permute-start(bf16[3,6,128,128]{3,2,1,0:T(8,128)(2,1)S(1)} %copy-done.44), channel_id=1, source_target_pairs={{8,0},{12,4},{16,8},{20,12},{24,16},{28,20},{9,1},{13,5},{17,9},{2... | collective-permute-start | bytes 1769480 | tf_op jit(solution)/shard_map/ppermute | solution.py:353
  367.7 29.5 %collective-permute-start.41 = (bf16[2,3,6,128,128]{4,3,2,1,0:T(8,128)(2,1)S(1)}, bf16[2,3,6,128,128]{4,3,2,1,0:T(8,128)(2,1)S(1)}, u32[]{:S(2)}, u32[]{:S(2)}) collective-permute-start(bf16[2,3,6,128,128]{4,3,2,1,0:T(8,128)(2,1)S(1)} %copy-done.12), channel_id=1, source_target_pairs={{0,4},{4,0},{8,12},{12,8},{16,20},{20,16},{24,28},{28,24},{1,5},{5... | collective-permute-start | bytes 3538952 | tf_op jit(solution)/shard_map/ppermute | solution.py:306
  383.2 44.3 %collective-permute-start.42 = (bf16[2,3,6,128,128]{4,3,2,1,0:T(8,128)(2,1)S(1)}, bf16[2,3,6,128,128]{4,3,2,1,0:T(8,128)(2,1)S(1)}, u32[]{:S(2)}, u32[]{:S(2)}) collective-permute-start(bf16[2,3,6,128,128]{4,3,2,1,0:T(8,128)(2,1)S(1)} %add_convert_fusion.1), channel_id=1, source_target_pairs={{0,8},{4,12},{8,0},{12,4},{16,24},{20,28},{24,16},{28,20},{1,9},{5... | collective-permute-start | bytes 3538952 | tf_op jit(solution)/shard_map/ppermute | solution.py:370
  387.7 41.1 %collective-permute-start.40 = (bf16[3,8,128,128]{3,2,1,0:T(8,128)(2,1)S(1)}, bf16[3,8,128,128]{3,2,1,0:T(8,128)(2,1)S(1)}, u32[]{:S(2)}, u32[]{:S(2)}) collective-permute-start(bf16[3,8,128,128]{3,2,1,0:T(8,128)(2,1)S(1)} %fusion.32), channel_id=1, source_target_pairs={{0,16},{4,20},{8,24},{12,28},{16,0},{20,4},{24,8},{28,12},{1,17},{... | collective-permute-start | bytes 2359304 | tf_op jit(solution)/shard_map/ppermute | solution.py:376
  393.6 67.4 %collective-permute-start.33 = (bf16[2,256,2048]{2,1,0:T(8,128)(2,1)}, bf16[2,256,2048]{2,1,0:T(8,128)(2,1)}, u32[]{:S(2)}, u32[]{:S(2)}) collective-permute-start(bf16[2,256,2048]{2,1,0:T(8,128)(2,1)} %pad_maximum_fusion.3), channel_id=1, source_target_pairs={{0,1},{1,0},{2,3},{3,2},{4,5},{5,4},{6,7},{7,6},{8,9},{9,8},{10,11... | collective-permute-start | bytes 6291464 | tf_op jit(solution)/shard_map/ppermute | solution.py:303
  394.9 66.0 %collective-permute-start.35 = (bf16[2,256,2048]{2,1,0:T(8,128)(2,1)}, bf16[2,256,2048]{2,1,0:T(8,128)(2,1)}, u32[]{:S(2)}, u32[]{:S(2)}) collective-permute-start(bf16[2,256,2048]{2,1,0:T(8,128)(2,1)} %pad_maximum_fusion.4), channel_id=1, source_target_pairs={{0,2},{1,3},{2,0},{3,1},{4,6},{5,7},{6,4},{7,5},{8,10},{9,11},{10,... | collective-permute-start | bytes 6291464 | tf_op jit(solution)/shard_map/ppermute | solution.py:303
  427.9 26.5 %collective-permute-start.43 = (bf16[3,6,128,128]{3,2,1,0:T(8,128)(2,1)S(1)}, bf16[3,6,128,128]{3,2,1,0:T(8,128)(2,1)S(1)}, u32[]{:S(2)}, u32[]{:S(2)}) collective-permute-start(bf16[3,6,128,128]{3,2,1,0:T(8,128)(2,1)S(1)} %fusion.33), channel_id=1, source_target_pairs={{0,16},{4,20},{8,24},{12,28},{16,0},{20,4},{24,8},{28,12},{1,17},{... | collective-permute-start | bytes 1769480 | tf_op jit(solution)/shard_map/ppermute | solution.py:376
  (63 other events, 674.8 us)
Sparse Core Ops, SparseCore 0:
  10.4 90.2 all-gather.2

commit v5 on v4

--- a/solution.py
+++ b/solution.py
@@ -31,7 +31,7 @@
     found = []
     for s in range(kg):
         block = scal[table * f_total * kg + f * kg + scal[3 * f_total * kg + s]]
-        found.append((block // blocks, pl.multiple_of(lax.rem(block, blocks) * BS, BS)))
+        found.append((block // blocks, lax.rem(block, blocks)))
     return found
 
 
@@ -55,7 +55,7 @@
 
     def picked(source, table, j):
         where = places(scal, table, f_first + step * per + j, kg=kg, f_total=f_total, blocks=blocks)
-        return jnp.concatenate([source[slot, :, pl.ds(at, BS)] for slot, at in where], axis=1)
+        return jnp.concatenate([source[slot, :, pl.ds(pl.multiple_of(block * BS, BS), BS)] for slot, block in where], axis=1)
 
     def put(kind, j, grads):
         s = 0
@@ -80,11 +80,10 @@
             hidden = (silu * up).astype(BF)
             gate_grad = (hidden_grad * up * sig * (1.0 + gate * (1.0 - sig))).astype(BF)
             up_grad = (hidden_grad * silu).astype(BF)
-            for kind, value in enumerate((gate_grad, up_grad, hidden)):
-                stash[kind, j] = value
-            put(2, j, contract(hidden, y_down[j], 0, 0))
-            put(0, j, contract(gate_grad, x_gate[j], 0, 0))
-            put(1, j, contract(up_grad, x_up[j], 0, 0))
+            for kind, value, source in ((2, hidden, y_down[j]), (0, gate_grad, x_gate[j]), (1, up_grad, x_up[j])):
+                turned = value.T
+                stash[kind, j] = turned
+                put(kind, j, contract(turned, source, 1, 0))
 
     @pl.when(step == 0)
     def _():
@@ -131,7 +130,7 @@
             grid=(f_here // per,),
             in_specs=[anywhere] * (1 + len(after)) + [tile_spec(t, tile_first // per) for t in tiles],
             out_specs=[tile_spec(t, 0) for t in tiles]
-            + [pl.BlockSpec((3, per, tokens, BS), lambda f, scal: (0, f, 0, 0))],
+            + [pl.BlockSpec((3, per, BS, tokens), lambda f, scal: (0, f, 0, 0))],
             scratch_shapes=[
                 pltpu.VMEM((n_col, tokens, width), BF),
                 pltpu.VMEM((n_col, tokens, width), BF),
@@ -139,7 +138,7 @@
             ],
         ),
         out_shape=[jax.ShapeDtypeStruct((t.shape[0], 3, f_here, BS, BS), BF) for t in tiles]
-        + [jax.ShapeDtypeStruct((3, f_here, tokens, BS), BF)],
+        + [jax.ShapeDtypeStruct((3, f_here, BS, tokens), BF)],
         compiler_params=pltpu.CompilerParams(vmem_limit_bytes=48 * 1024 * 1024),
         cost_estimate=pl.CostEstimate(
             flops=6 * 2 * tokens * f_here * kg * BS * BS, bytes_accessed=f_here * 6 * 1024 * 1024, transcendentals=0
@@ -162,12 +161,10 @@
     me = scal[3 * f_total * kg + kg]
     acc_loads = [pltpu.make_async_copy(src, dst, acc_sem.at[i]) for i, (src, dst) in enumerate(zip(acc_in, totals))]
 
-    def scatter(total, where, left, right):
-        for s in range(0, kg, 2):
-            two = contract(left, right[s * BS : (s + 2) * BS], 1, 1)
-            for i in range(2):
-                slot, at = where[s + i]
-                total[slot ^ me, :, pl.ds(at, BS)] += two[:, i * BS : (i + 1) * BS]
+    def scatter(total, where, tile_rows, turned):
+        added = contract(tile_rows, turned, 1, 0)
+        for s, (slot, block) in enumerate(where):
+            total[(slot ^ me) * blocks + block] += added[s * BS : (s + 1) * BS]
 
     @pl.when(step == 0)
     def _():
@@ -188,7 +185,7 @@
                 f = f_first + (step - before) * per + j
                 for kind, total in ((2, totals[0]), (0, totals[1]), (1, totals[1])):
                     where = places(scal, kind, f, kg=kg, f_total=f_total, blocks=blocks)
-                    scatter(total, where, stash[kind, j], stacked(tiles, kind, j))
+                    scatter(total, where, stacked(tiles, kind, j), stash[kind, j])
 
         before += steps
 
@@ -198,13 +195,13 @@
         for kind, total in enumerate(totals):
             if last:
                 for s in range(n_col):
-                    for t in range(0, total.shape[1], 32):
-                        rounded[kind][s, t : t + 32] = total[s, t : t + 32].astype(BF)
+                    for i in range(s * blocks, (s + 1) * blocks):
+                        rounded[kind][i] = total[i].astype(BF)
                     here = [
                         pltpu.make_async_copy(
-                            rounded[kind].at[slot, pl.ds(at, rows)], results[p].at[kind], store_sem.at[kind, p]
+                            rounded[kind].at[pl.ds(slot * blocks + at, count)], results[p].at[kind], store_sem.at[kind, p]
                         )
-                        for p, (slot, at, rows) in enumerate(pieces)
+                        for p, (slot, at, count) in enumerate(pieces)
                         if slot == s
                     ]
                     for copy in here:
@@ -219,7 +216,7 @@
 
 
 def run_adds(scal, accs, after, parts, pieces, *, n_col, width, f_total, last):
-    tokens = parts[0][1].shape[2]
+    tokens = parts[0][1].shape[3]
     kg = sum(t.shape[0] for t in parts[0][2])
     first = accs is None
     anywhere = pl.BlockSpec(memory_space=pl.ANY)
@@ -231,7 +228,7 @@
         def spot(f, before=before, steps=steps):
             return jnp.clip(f - before, 0, steps - 1)
 
-        specs.append(pl.BlockSpec((3, per, tokens, BS), lambda f, scal, spot=spot: (0, spot(f), 0, 0)))
+        specs.append(pl.BlockSpec((3, per, BS, tokens), lambda f, scal, spot=spot: (0, spot(f), 0, 0)))
         for t in tiles:
             specs.append(
                 pl.BlockSpec(
@@ -242,9 +239,9 @@
         operands += [stash, *tiles]
         segments.append((f_first, at, steps))
         before += steps
-    acc_shape = (n_col, tokens, width)
+    acc_shape = (n_col * width // BS, BS, tokens)
     if last:
-        results = [jax.ShapeDtypeStruct((2, rows, width), BF) for _, _, rows in pieces]
+        results = [jax.ShapeDtypeStruct((2, count, BS, tokens), BF) for _, _, count in pieces]
     else:
         results = [jax.ShapeDtypeStruct(acc_shape, F32)] * 2
     kernel = functools.partial(
@@ -305,11 +302,11 @@
     def swap(value):
         return lax.ppermute(value, "row", across)
 
-    def pieces_of(tokens):
-        half = tokens // 2
+    def pieces_of(blocks):
+        half = blocks // 2
         if two_phase:
-            return ((0, 0, tokens), (1, 0, tokens), (2, 0, tokens), (3, 0, half), (3, half, half))
-        return tuple((s, 0, tokens) for s in range(n_col))
+            return ((0, 0, blocks), (1, 0, blocks), (2, 0, blocks), (3, 0, half), (3, half, blocks - half))
+        return tuple((s, 0, blocks) for s in range(n_col))
 
     def sum_columns(parts):
         if two_phase:
@@ -322,7 +319,8 @@
         else:
             mine = parts[0]
             got = [over(parts[o], o) for o in range(1, n_col)]
-        return [total_of(mine[i], *[g[i] for g in got]) for i in range(2)]
+        sums = [total_of(mine[i], *[g[i] for g in got]) for i in range(2)]
+        return [total.reshape(-1, total.shape[-1]).T for total in sums]
 
     class Chain:
         def __init__(self, z, own=None, grads=None):
@@ -354,6 +352,12 @@
                 self.tick += 1
             return self
 
+        def received(self, i):
+            return (self.from_left[i], self.from_right[i])
+
+        def tie(self, i, other):
+            self.from_left[i], self.from_right[i], _ = lax.optimization_barrier((*self.received(i), other))
+
         def slots(self):
             found = [self.own]
             for o in range(1, nz):
@@ -389,7 +393,7 @@
             [t.reshape(-1) for t in (gate_rows, up_rows, down_columns)]
             + [order.astype(jnp.int32), lax.axis_index("col").astype(jnp.int32).reshape(1)]
         )
-        pieces = pieces_of(tokens.shape[0])
+        pieces = pieces_of(tokens.shape[1] // BS)
         panels = lax.all_gather(jnp.stack([tokens, out_grad]), "col")
 
         def own_tiles(start, stop):
@@ -426,35 +430,43 @@
         def add_up(accs, parts, last, after=()):
             return run_adds(scal, accs, after, parts, pieces, n_col=n_col, width=width, f_total=f_total, last=last)
 
-        if f_total % 4 == 0 and nz == 4 and whole_tiles:
-            half = f_total // 2
-            big = half // 2 + half // 2 % 2
-            small = half - big
-            second, third, fourth = big, half, half + big
-            tiles = all_tiles(Chain(z, own_tiles(0, half)).run(3).slots())
-            one, two = Chain(z, own_tiles(third, fourth)).run(1), Chain(z, own_tiles(fourth, f_total)).run(1)
-            hold = (one.from_left[0], one.from_right[0], two.from_left[0], two.from_right[0])
-            one.grads, part_0 = compute(0, big, tiles, 0, (), hold)
+        if f_total % 7 == 0 and f_total > 7 and nz == 4 and whole_tiles:
+            few = f_total // 7
+            at = [0, few, 3 * few, 4 * few, 6 * few, 7 * few]
+            tiles = all_tiles(Chain(z, own_tiles(at[0], at[2])).run(3).slots())
+            one, two, three = [Chain(z, own_tiles(at[i], at[i + 1])) for i in (2, 3, 4)]
+            one.run(1)
+            two.run(1)
+            one.grads, part_0 = compute(at[0], few, tiles, at[0], (), one.received(0))
             one.run(1)
             two.grads, part_1 = compute(
-                second, small, tiles, second, (one.grads[3],), (one.from_left[1], one.from_right[1])
+                at[1], 2 * few, tiles, at[1], (one.grads[3],), one.received(1) + two.received(0)
             )
+            one.tie(1, two.grads[0])
             accs = add_up(None, [part_0, part_1], False)
-            one.from_left[1], one.from_right[1], _ = lax.optimization_barrier(
-                (one.from_left[1], one.from_right[1], two.grads[3])
-            )
             one.run(1)
             two.run(1)
+            one.tie(2, accs[0])
             mine = one.slots()
             one.run(1)
             two.run(1)
-            hold = (one.from_left[3], one.from_right[3], two.from_left[2], two.from_right[2])
-            grads, part_2 = compute(third, big, all_tiles(mine), 0, (accs[0],), hold)
-            three = Halves(z, grads)
-            last, part_3 = compute(fourth, small, all_tiles(two.slots()), 0, (grads[3],))
-            accs = add_up(accs, [part_2, part_3], True, (last[3],))
+            three.run(1)
+            three.grads, part_2 = compute(
+                at[2], few, all_tiles(mine), 0, (), three.received(0) + two.received(1)
+            )
+            three.run(1)
+            grads, part_3 = compute(
+                at[3], 2 * few, all_tiles(two.slots()), 0, (three.grads[3],), three.received(1) + one.received(3)
+            )
+            fourth = Halves(z, grads)
+            three.run(1)
+            mine = three.slots()
+            last, part_4 = compute(at[4], few, all_tiles(mine), 0, (grads[3],))
+            accs = add_up(accs, [part_2, part_3, part_4], True, (last[3],))
+            *accs, _ = lax.optimization_barrier((*accs, fourth.near))
             two.run(1)
-            sums = [one.total(), two.total(), three.total(), Halves(z, last).total()]
+            three.run(1)
+            sums = [one.total(), two.total(), three.total(), fourth.total(), Halves(z, last).total()]
         else:
             gather = Chain(z, own_tiles(0, f_total)).run(nz - 1)
             grads, part_0 = compute(0, f_total, all_tiles(gather.slots()), 0)

time: 481 us -> 473 us (0.983)
  waiting for transfers between devices: 203 us -> 173 us
  starting transfers between devices: 75.6 us -> 102 us
  local copies, waits for them, and re-layouts: 19.7 us -> 31.1 us
  other arithmetic: 60.2 us -> 51.5 us
  Pallas kernels: 99.3 us -> 91.7 us
    ppermute x2, waiting for transfers between devices: 30.3 us -> 5.67 us  [__init__(): lax.ppermute(total_of(grads[1], grads[3]), 'row', [(r, r ^ 2) for r in ra...]
    ppermute x11 -> x15, waiting for transfers between devices: 110 us -> 86.1 us  [run(): lax.ppermute(to_left, 'row', left(nz - stop, nz - start))]
    ppermute x11 -> x15, starting transfers between devices: 45.8 us -> 63.8 us  [run(): self.from_left.append(lax.ppermute(to_right, 'row', right(start, stop)))]
    ppermute x11 -> x15, waiting for transfers between devices: 14.4 us -> 29.4 us  [run(): self.from_left.append(lax.ppermute(to_right, 'row', right(start, stop)))]
    ppermute x2, waiting for transfers between devices: 23.4 us -> 35.8 us  [total(): lax.ppermute(total_of(keep[1], got[1], far), 'row', [(r, r ^ 4) for r in...]
    pallas_call x2, Pallas kernels: 52.4 us -> 40.8 us  [run_adds(): pl.pallas_call(kernel, grid_spec=pltpu.PrefetchScalarGridSpec(num_scalar_...]
    another operation x6, local copies, waits for them, and re-layouts: 0.19 us -> 7.74 us  [own_tiles(): jnp.stack([w[start:stop] for w in (gate_weight, up_weight, down_weight)])]
    ppermute x11 -> x15, starting transfers between devices: 14.8 us -> 19.7 us  [run(): lax.ppermute(to_left, 'row', left(nz - stop, nz - start))]
  transfers between devices with their start and end apart: 45 -> 57, of which waited for: 18 -> 18; matrix products, arithmetic and copies ran while one was open for 11% -> 12% of each run, Pallas kernels for 19% -> 20%
where the time goes in v5:
time: 473 us; the launch traced here: 465 us
  waiting for transfers between devices  173 us (37%)
  starting transfers between devices  102 us (22%)
  Pallas kernels  91.7 us (19%)
  other arithmetic  51.5 us (11%)
  local copies, waits for them, and re-layouts  31.1 us (7%)
  between operations  15.6 us (3%)
    ppermute x15, waiting for transfers between devices, run(): lax.ppermute(to_left, 'row', left(nz - stop, nz - start))  86.1 us
    ppermute x15, starting transfers between devices, run(): self.from_left.append(lax.ppermute(to_right, 'row', right(start, stop)))  63.8 us
    pallas_call x5, Pallas kernels, run_grads(): pl.pallas_call(kernel, grid_spec=pltpu.PrefetchScalarGridSpec(num_scalar_...  50.9 us
    pallas_call x2, Pallas kernels, run_adds(): pl.pallas_call(kernel, grid_spec=pltpu.PrefetchScalarGridSpec(num_scalar_...  40.8 us
    ppermute x2, waiting for transfers between devices, total(): lax.ppermute(total_of(keep[1], got[1], far), 'row', [(r, r ^ 4) for r in...  35.8 us
    ppermute x15, waiting for transfers between devices, run(): self.from_left.append(lax.ppermute(to_right, 'row', right(start, stop)))  29.4 us
    unnamed x128, local copies, waits for them, and re-layouts  20 us
    ppermute x15, starting transfers between devices, run(): lax.ppermute(to_left, 'row', left(nz - stop, nz - start))  19.7 us
  transfers between devices with their start and end apart: 57, of which 18 were waited for; matrix products, arithmetic and copies ran while one was open for 12% of the time, Pallas kernels for 20%

profile of v5, /device:TPU:0, one launch (start us, length us, event | category | flops | bytes accessed | tf_op | source)
XLA Modules:
  0.0 464.8 jit_solution(9157311960655092682)
XLA Ops:
  12.7 5.0 %collective-permute-start.1 = (bf16[3,12,128,128]{3,2,1,0:T(8,128)(2,1)S(1)}, bf16[3,12,128,128]{3,2,1,0:T(8,128)(2,1)S(1)}, u32[]{:S(2)}, u32[]{:S(2)}) collective-permute-start(bf16[3,12,128,128]{3,2,1,0:T(8,128)(2,1)S(1)} %get-tuple-element.146), channel_id=1, source_target_pairs={{0,8},{4,12},{8,16},{12,20},{16,24},{20,28},{1,9},{5,13},{9,17},{1... | collective-permute-start | bytes 3538952 | tf_op jit(solution)/shard_map/ppermute | solution.py:350
  19.0 23.8 %collective-permute-done.1 = bf16[3,12,128,128]{3,2,1,0:T(8,128)(2,1)S(1)} collective-permute-done((bf16[3,12,128,128]{3,2,1,0:T(8,128)(2,1)S(1)}, bf16[3,12,128,128]{3,2,1,0:T(8,128)(2,1)S(1)}, u32[]{:S(2)}, u32[]{:S(2)}) %collective-permute-start.1) | collective-permute-done | bytes 1179680 | tf_op jit(solution)/shard_map/ppermute | solution.py:350
  50.0 26.7 %collective-permute-done.4 = bf16[3,12,128,128]{3,2,1,0:T(8,128)(2,1)} collective-permute-done((bf16[3,12,128,128]{3,2,1,0:T(8,128)(2,1)S(1)}, bf16[3,12,128,128]{3,2,1,0:T(8,128)(2,1)}, u32[]{:S(2)}, u32[]{:S(2)}) %collective-permute-start.4) | collective-permute-done | bytes 1179680 | tf_op jit(solution)/shard_map/ppermute | solution.py:351
  81.2 23.8 %collective-permute-done.5 = bf16[3,12,128,128]{3,2,1,0:T(8,128)(2,1)} collective-permute-done((bf16[3,12,128,128]{3,2,1,0:T(8,128)(2,1)}, bf16[3,12,128,128]{3,2,1,0:T(8,128)(2,1)}, u32[]{:S(2)}, u32[]{:S(2)}) %collective-permute-start.5) | collective-permute-done | bytes 1179680 | tf_op jit(solution)/shard_map/ppermute | solution.py:351
  116.7 9.0 %ffn_grads.5 = (bf16[2,3,4,128,128]{4,3,2,1,0:T(8,128)(2,1)S(1)}, bf16[2,3,4,128,128]{4,3,2,1,0:T(8,128)(2,1)S(1)}, bf16[2,3,4,128,128]{4,3,2,1,0:T(8,128)(2,1)}...) custom-call(s32[681]{0:T(1024)S(1)} %concatenate.18.scal, bf16[4,2,256,2048]{3,2,1,0:T(8,128)(2,1)} %bitcast.283, ...), custom_call_target="tpu_custom_call" | custom-call | flops 1610612736 | bytes 25165824 | tf_op jit(solution)/shard_map/ffn_grads/pallas_call | solution.py:126
  133.0 5.4 %collective-permute-start.20 = (bf16[3,8,128,128]{3,2,1,0:T(8,128)(2,1)}, bf16[3,8,128,128]{3,2,1,0:T(8,128)(2,1)}, u32[]{:S(2)}, u32[]{:S(2)}) collective-permute-start(bf16[3,8,128,128]{3,2,1,0:T(8,128)(2,1)} %get-tuple-element.164), channel_id=1, source_target_pairs={{0,8},{4,12},{8,16},{12,20},{16,24},{20,28},{1,9},{5,13},{9,17},{1... | collective-permute-start | bytes 2359304 | tf_op jit(solution)/shard_map/ppermute | solution.py:350
  141.5 4.8 %collective-permute-start.11 = (bf16[3,4,128,128]{3,2,1,0:T(8,128)(2,1)S(1)}, bf16[3,4,128,128]{3,2,1,0:T(8,128)(2,1)S(1)}, u32[]{:S(2)}, u32[]{:S(2)}) collective-permute-start(bf16[3,4,128,128]{3,2,1,0:T(8,128)(2,1)S(1)} %get-tuple-element.144), channel_id=1, source_target_pairs={{0,8},{4,12},{8,16},{12,20},{16,24},{20,28},{1,9},{5,13},{9,17},{1... | collective-permute-start | bytes 1179656 | tf_op jit(solution)/shard_map/ppermute | solution.py:350
  146.3 12.6 %ffn_grads.6 = (bf16[2,3,8,128,128]{4,3,2,1,0:T(8,128)(2,1)S(1)}, bf16[2,3,8,128,128]{4,3,2,1,0:T(8,128)(2,1)S(1)}, bf16[2,3,8,128,128]{4,3,2,1,0:T(8,128)(2,1)}...) custom-call(s32[681]{0:T(1024)S(1)} %concatenate.18.scal, bf16[4,2,256,2048]{3,2,1,0:T(8,128)(2,1)} %bitcast.284, ...), custom_call_target="tpu_custom_call" | custom-call | flops 3221225472 | bytes 50331648 | tf_op jit(solution)/shard_map/ffn_grads/pallas_call | solution.py:126
  163.8 5.3 %collective-permute-done.22 = bf16[2,3,8,128,128]{4,3,2,1,0:T(8,128)(2,1)S(1)} collective-permute-done((bf16[2,3,8,128,128]{4,3,2,1,0:T(8,128)(2,1)}, bf16[2,3,8,128,128]{4,3,2,1,0:T(8,128)(2,1)S(1)}, u32[]{:S(2)}, u32[]{:S(2)}) %collective-permute-start.22) | collective-permute-done | bytes 1572896 | tf_op jit(solution)/shard_map/ppermute | solution.py:303
  169.2 5.0 %fusion.12 = (bf16[3,8,128,128]{3,2,1,0:T(8,128)(2,1)}, bf16[3,8,128,128]{3,2,1,0:T(8,128)(2,1)}) fusion(bf16[3,8,128,128]{3,2,1,0:T(8,128)(2,1)} %collective-permute-done.21, pred[]{:T(512)S(6)} %ge.15, bf16[2,3,8,128,128]{4,3,2,1,0:T(8,128)(2,1)S(1)} %collective-permute-done.22, bf16[2,3,8,128,128]{4,3,2,1,0:T(8,128)(2,1)S(1)} %get-tuple-element.72, ...), kind=kLoop, calls=%fused_computation.37 | loop fusion | flops 5505024 | bytes 6291458 | tf_op jit(solution)/shard_map/jit(_where)/select_n | solution.py:347
  175.5 5.9 %collective-permute-start.23 = (bf16[3,8,128,128]{3,2,1,0:T(8,128)(2,1)}, bf16[3,8,128,128]{3,2,1,0:T(8,128)(2,1)}, u32[]{:S(2)}, u32[]{:S(2)}) collective-permute-start(bf16[3,8,128,128]{3,2,1,0:T(8,128)(2,1)} %get-tuple-element.131), channel_id=1, source_target_pairs={{0,8},{4,12},{8,16},{12,20},{16,24},{20,28},{1,9},{5,13},{9,17},{1... | collective-permute-start | bytes 2359304 | tf_op jit(solution)/shard_map/ppermute | solution.py:350
  184.5 4.6 collective-permute-start.14
  189.1 8.1 %collective-permute-done.24 = bf16[3,8,128,128]{3,2,1,0:T(8,128)(2,1)} collective-permute-done((bf16[3,8,128,128]{3,2,1,0:T(8,128)(2,1)}, bf16[3,8,128,128]{3,2,1,0:T(8,128)(2,1)}, u32[]{:S(2)}, u32[]{:S(2)}) %collective-permute-start.24) | collective-permute-done | bytes 786464 | tf_op jit(solution)/shard_map/ppermute | solution.py:351
  198.7 4.6 fusion.14
  204.6 5.3 %collective-permute-start.28 = (bf16[3,8,128,128]{3,2,1,0:T(8,128)(2,1)}, bf16[3,8,128,128]{3,2,1,0:T(8,128)(2,1)S(1)}, u32[]{:S(2)}, u32[]{:S(2)}) collective-permute-start(bf16[3,8,128,128]{3,2,1,0:T(8,128)(2,1)} %get-tuple-element.129), channel_id=1, source_target_pairs={{0,8},{4,12},{8,16},{12,20},{16,24},{20,28},{1,9},{5,13},{9,17},{1... | collective-permute-start | bytes 2359304 | tf_op jit(solution)/shard_map/ppermute | solution.py:350
  209.9 17.5 %ffn_adds.2 = (f32[64,128,256]{2,1,0:T(8,128)}, f32[64,128,256]{2,1,0:T(8,128)}) custom-call(s32[681]{0:T(1024)} %copy-done.17, bf16[3,4,128,256]{3,2,1,0:T(8,128)(2,1)} %copy-done.8, bf16[2,3,12,128,128]{4,3,2,1,0:T(8,128)(2,1)} %copy-done.23, bf16[2,3,12,128,128]{4,3,2,1,0:T(8,128)(2,1)} %pad_maximum_fusion.1.refs_2_.refs_3_.refs_7_, ...), custom_call_target="tpu_custom_call" | custom-call | flops 2415919104 | bytes 50331648 | tf_op jit(solution)/shard_map/ffn_adds/pallas_call | solution.py:261
  240.1 4.9 %collective-permute-start.18 = (bf16[3,4,128,128]{3,2,1,0:T(8,128)(2,1)S(1)}, bf16[3,4,128,128]{3,2,1,0:T(8,128)(2,1)S(1)}, u32[]{:S(2)}, u32[]{:S(2)}) collective-permute-start(bf16[3,4,128,128]{3,2,1,0:T(8,128)(2,1)S(1)} %get-tuple-element.178), channel_id=1, source_target_pairs={{0,8},{4,12},{8,16},{12,20},{16,24},{20,28},{1,9},{5,13},{9,17},{1... | collective-permute-start | bytes 1179656 | tf_op jit(solution)/shard_map/ppermute | solution.py:350
  246.0 8.1 %ffn_grads.7 = (bf16[2,3,4,128,128]{4,3,2,1,0:T(8,128)(2,1)S(1)}, bf16[2,3,4,128,128]{4,3,2,1,0:T(8,128)(2,1)S(1)}, bf16[2,3,4,128,128]{4,3,2,1,0:T(8,128)(2,1)S...) custom-call(s32[681]{0:T(1024)S(1)} %copy-done.18, bf16[4,2,256,2048]{3,2,1,0:T(8,128)(2,1)} %bitcast.285, ...), custom_call_target="tpu_custom_call" | custom-call | flops 1610612736 | bytes 25165824 | tf_op jit(solution)/shard_map/ffn_grads/pallas_call | solution.py:126
  255.5 4.7 %collective-permute-start.33 = (bf16[3,4,128,128]{3,2,1,0:T(8,128)(2,1)}, bf16[3,4,128,128]{3,2,1,0:T(8,128)(2,1)S(1)}, u32[]{:S(2)}, u32[]{:S(2)}) collective-permute-start(bf16[3,4,128,128]{3,2,1,0:T(8,128)(2,1)} %get-tuple-element.138), channel_id=1, source_target_pairs={{0,8},{4,12},{8,16},{12,20},{16,24},{20,28},{1,9},{5,13},{9,17},{1... | collective-permute-start | bytes 1179656 | tf_op jit(solution)/shard_map/ppermute | solution.py:350
  262.2 5.1 %collective-permute-start.31 = (bf16[3,4,128,128]{3,2,1,0:T(8,128)(2,1)S(1)}, bf16[3,4,128,128]{3,2,1,0:T(8,128)(2,1)S(1)}, u32[]{:S(2)}, u32[]{:S(2)}) collective-permute-start(bf16[3,4,128,128]{3,2,1,0:T(8,128)(2,1)S(1)} %get-tuple-element.140), channel_id=1, source_target_pairs={{0,8},{4,12},{8,16},{12,20},{16,24},{20,28},{1,9},{5,13},{9,17},{1... | collective-permute-start | bytes 1179656 | tf_op jit(solution)/shard_map/ppermute | solution.py:350
  267.3 12.5 %ffn_grads.8 = (bf16[2,3,8,128,128]{4,3,2,1,0:T(8,128)(2,1)S(1)}, bf16[2,3,8,128,128]{4,3,2,1,0:T(8,128)(2,1)S(1)}, bf16[2,3,8,128,128]{4,3,2,1,0:T(8,128)(2,1)S...) custom-call(s32[681]{0:T(1024)S(1)} %copy-done.18, bf16[4,2,256,2048]{3,2,1,0:T(8,128)(2,1)} %bitcast.286, ...), custom_call_target="tpu_custom_call" | custom-call | flops 3221225472 | bytes 50331648 | tf_op jit(solution)/shard_map/ffn_grads/pallas_call | solution.py:126
  281.7 4.6 collective-permute-start.38
  286.6 7.4 %collective-permute-done.37 = bf16[3,4,128,128]{3,2,1,0:T(8,128)(2,1)S(1)} collective-permute-done((bf16[3,4,128,128]{3,2,1,0:T(8,128)(2,1)S(1)}, bf16[3,4,128,128]{3,2,1,0:T(8,128)(2,1)S(1)}, u32[]{:S(2)}, u32[]{:S(2)}) %collective-permute-start.37) | collective-permute-done | bytes 393248 | tf_op jit(solution)/shard_map/ppermute | solution.py:351
  302.9 8.8 %ffn_grads.9 = (bf16[2,3,4,128,128]{4,3,2,1,0:T(8,128)(2,1)S(1)}, bf16[2,3,4,128,128]{4,3,2,1,0:T(8,128)(2,1)S(1)}, bf16[2,3,4,128,128]{4,3,2,1,0:T(8,128)(2,1)S...) custom-call(s32[681]{0:T(1024)S(1)} %copy-done.18, bf16[4,2,256,2048]{3,2,1,0:T(8,128)(2,1)} %bitcast.287, ...), custom_call_target="tpu_custom_call" | custom-call | flops 1610612736 | bytes 25165824 | tf_op jit(solution)/shard_map/ffn_grads/pallas_call | solution.py:126
  320.5 23.3 %ffn_adds.3 = (bf16[2,16,128,256]{3,2,1,0:T(8,128)(2,1)}, bf16[2,16,128,256]{3,2,1,0:T(8,128)(2,1)}, bf16[2,16,128,256]{3,2,1,0:T(8,128)(2,1)}, bf16[2,8,128,256]{3,2,1,0:T(8,128)(2,1)}, bf16[2,8,128,256]{3,2,1,0:T(8,128)(2,1)}) custom-call(s32[681]{0:T(1024)} %copy-done.17, bf16[2,3,4,128,128]{4,3,2,1,0:T(8,128)(2,1)} %collective-permute-done.41.refs_0_, ...), custom_call_target="tpu_custom_call" | custom-call | flops 3221225472 | bytes 50331648 | tf_op jit(solution)/shard_map/ffn_adds/pallas_call | solution.py:261
  345.4 5.8 %collective-permute-start.49 = (bf16[3,4,128,128]{3,2,1,0:T(8,128)(2,1)}, bf16[3,4,128,128]{3,2,1,0:T(8,128)(2,1)S(1)}, u32[]{:S(2)}, u32[]{:S(2)}) collective-permute-start(bf16[3,4,128,128]{3,2,1,0:T(8,128)(2,1)} %get-tuple-element.133), channel_id=1, source_target_pairs={{0,8},{4,12},{8,16},{12,20},{16,24},{20,28},{1,9},{5,13},{9,17},{1... | collective-permute-start | bytes 1179656 | tf_op jit(solution)/shard_map/ppermute | solution.py:350
  361.2 7.8 %collective-permute-done.43 = bf16[2,8,128,256]{3,2,1,0:T(8,128)(2,1)S(1)} collective-permute-done((bf16[2,8,128,256]{3,2,1,0:T(8,128)(2,1)}, bf16[2,8,128,256]{3,2,1,0:T(8,128)(2,1)S(1)}, u32[]{:S(2)}, u32[]{:S(2)}) %collective-permute-start.43) | collective-permute-done | bytes 1048608 | tf_op jit(solution)/shard_map/ppermute | solution.py:300
  368.9 4.2 collective-permute-start.54
  385.9 5.7 %collective-permute-done.54 = bf16[2,3,4,128,128]{4,3,2,1,0:T(8,128)(2,1)S(1)} collective-permute-done((bf16[2,3,4,128,128]{4,3,2,1,0:T(8,128)(2,1)S(1)}, bf16[2,3,4,128,128]{4,3,2,1,0:T(8,128)(2,1)S(1)}, u32[]{:S(2)}, u32[]{:S(2)}) %collective-permute-start.54) | collective-permute-done | bytes 786464 | tf_op jit(solution)/shard_map/ppermute | solution.py:374
  395.0 11.7 %collective-permute-done.50 = bf16[3,4,128,128]{3,2,1,0:T(8,128)(2,1)S(1)} collective-permute-done((bf16[3,4,128,128]{3,2,1,0:T(8,128)(2,1)S(1)}, bf16[3,4,128,128]{3,2,1,0:T(8,128)(2,1)S(1)}, u32[]{:S(2)}, u32[]{:S(2)}) %collective-permute-start.50) | collective-permute-done | bytes 393248 | tf_op jit(solution)/shard_map/ppermute | solution.py:351
  407.0 35.8 %collective-permute-done.55 = bf16[3,4,128,128]{3,2,1,0:T(8,128)(2,1)S(1)} collective-permute-done((bf16[3,4,128,128]{3,2,1,0:T(8,128)(2,1)S(1)}, bf16[3,4,128,128]{3,2,1,0:T(8,128)(2,1)S(1)}, u32[]{:S(2)}, u32[]{:S(2)}) %collective-permute-start.55) | collective-permute-done | bytes 393248 | tf_op jit(solution)/shard_map/ppermute | solution.py:380
  451.0 3.9 add_convert_fusion.1
  (274 shorter events, 127.6 us)
Async XLA Ops:
  7.2 109.5 %all-gather.3.cloned.1.call-start = ((), (), s32[]{:S(2)}) async-start(), calls=%async_computation | async-start | bytes 10485760 | tf_op jit(solution)/shard_map/all_gather | solution.py:397
  12.7 30.1 %collective-permute-start.1 = (bf16[3,12,128,128]{3,2,1,0:T(8,128)(2,1)S(1)}, bf16[3,12,128,128]{3,2,1,0:T(8,128)(2,1)S(1)}, u32[]{:S(2)}, u32[]{:S(2)}) collective-permute-start(bf16[3,12,128,128]{3,2,1,0:T(8,128)(2,1)S(1)} %get-tuple-element.146), channel_id=1, source_target_pairs={{0,8},{4,12},{8,16},{12,20},{16,24},{20,28},{1,9},{5,13},{9,17},{1... | collective-permute-start | bytes 3538952 | tf_op jit(solution)/shard_map/ppermute | solution.py:350
  17.7 29.3 %collective-permute-start.3 = (bf16[3,12,128,128]{3,2,1,0:T(8,128)(2,1)S(1)}, bf16[3,12,128,128]{3,2,1,0:T(8,128)(2,1)S(1)}, u32[]{:S(2)}, u32[]{:S(2)}) collective-permute-start(bf16[3,12,128,128]{3,2,1,0:T(8,128)(2,1)S(1)} %get-tuple-element.146), channel_id=1, source_target_pairs={{8,0},{12,4},{16,8},{20,12},{24,16},{28,20},{9,1},{13,5},{17,9},{2... | collective-permute-start | bytes 3538952 | tf_op jit(solution)/shard_map/ppermute | solution.py:351
  47.0 29.7 %collective-permute-start.4 = (bf16[3,12,128,128]{3,2,1,0:T(8,128)(2,1)S(1)}, bf16[3,12,128,128]{3,2,1,0:T(8,128)(2,1)}, u32[]{:S(2)}, u32[]{:S(2)}) collective-permute-start(bf16[3,12,128,128]{3,2,1,0:T(8,128)(2,1)S(1)} %collective-permute-done.3), channel_id=1, source_target_pairs={{8,0},{12,4},{16,8},{20,12},{9,1},{13,5},{17,9},{21,13},{10,2},{14... | collective-permute-start | bytes 3538952 | tf_op jit(solution)/shard_map/ppermute | solution.py:351
  48.3 31.5 %collective-permute-start.6 = (bf16[3,12,128,128]{3,2,1,0:T(8,128)(2,1)}, bf16[3,12,128,128]{3,2,1,0:T(8,128)(2,1)}, u32[]{:S(2)}, u32[]{:S(2)}) collective-permute-start(bf16[3,12,128,128]{3,2,1,0:T(8,128)(2,1)} %collective-permute-done.2), channel_id=1, source_target_pairs={{16,24},{20,28},{17,25},{21,29},{18,26},{22,30},{19,27},{23,31}} | collective-permute-start | bytes 3538952 | tf_op jit(solution)/shard_map/ppermute | solution.py:350
  76.8 28.2 %collective-permute-start.5 = (bf16[3,12,128,128]{3,2,1,0:T(8,128)(2,1)}, bf16[3,12,128,128]{3,2,1,0:T(8,128)(2,1)}, u32[]{:S(2)}, u32[]{:S(2)}) collective-permute-start(bf16[3,12,128,128]{3,2,1,0:T(8,128)(2,1)} %collective-permute-done.4), channel_id=1, source_target_pairs={{8,0},{12,4},{9,1},{13,5},{10,2},{14,6},{11,3},{15,7}} | collective-permute-start | bytes 3538952 | tf_op jit(solution)/shard_map/ppermute | solution.py:351
  79.7 36.9 %collective-permute-start.7 = (bf16[2,3,12,128,128]{4,3,2,1,0:T(8,128)(2,1)S(1)}, bf16[2,3,12,128,128]{4,3,2,1,0:T(8,128)(2,1)}, u32[]{:S(2)}, u32[]{:S(2)}) collective-permute-start(bf16[2,3,12,128,128]{4,3,2,1,0:T(8,128)(2,1)S(1)} %pad_maximum_fusion.refs_1_.refs_2_.refs_6_), channel_id=1, source_target_pairs={{0,4},{4,0},{8,12},{12,8},{16,20},{20,16},{24,28},{28,24},{1,5},{5... | collective-permute-start | bytes 7077896 | tf_op jit(solution)/shard_map/ppermute | solution.py:303
  131.7 27.3 %collective-permute-start.21 = (bf16[3,8,128,128]{3,2,1,0:T(8,128)(2,1)}, bf16[3,8,128,128]{3,2,1,0:T(8,128)(2,1)}, u32[]{:S(2)}, u32[]{:S(2)}) collective-permute-start(bf16[3,8,128,128]{3,2,1,0:T(8,128)(2,1)} %get-tuple-element.164), channel_id=1, source_target_pairs={{8,0},{12,4},{16,8},{20,12},{24,16},{28,20},{9,1},{13,5},{17,9},{2... | collective-permute-start | bytes 2359304 | tf_op jit(solution)/shard_map/ppermute | solution.py:351
  133.0 26.0 %collective-permute-start.20 = (bf16[3,8,128,128]{3,2,1,0:T(8,128)(2,1)}, bf16[3,8,128,128]{3,2,1,0:T(8,128)(2,1)}, u32[]{:S(2)}, u32[]{:S(2)}) collective-permute-start(bf16[3,8,128,128]{3,2,1,0:T(8,128)(2,1)} %get-tuple-element.164), channel_id=1, source_target_pairs={{0,8},{4,12},{8,16},{12,20},{16,24},{20,28},{1,9},{5,13},{9,17},{1... | collective-permute-start | bytes 2359304 | tf_op jit(solution)/shard_map/ppermute | solution.py:350
  163.3 25.7 %collective-permute-start.26 = (bf16[2,3,8,128,128]{4,3,2,1,0:T(8,128)(2,1)}, bf16[2,3,8,128,128]{4,3,2,1,0:T(8,128)(2,1)}, u32[]{:S(2)}, u32[]{:S(2)}) collective-permute-start(bf16[2,3,8,128,128]{4,3,2,1,0:T(8,128)(2,1)} %get-tuple-element.77), channel_id=1, source_target_pairs={{0,4},{4,0},{8,12},{12,8},{16,20},{20,16},{24,28},{28,24},{1,5},{5... | collective-permute-start | bytes 4718600 | tf_op jit(solution)/shard_map/ppermute | solution.py:303
  175.5 23.2 %collective-permute-start.23 = (bf16[3,8,128,128]{3,2,1,0:T(8,128)(2,1)}, bf16[3,8,128,128]{3,2,1,0:T(8,128)(2,1)}, u32[]{:S(2)}, u32[]{:S(2)}) collective-permute-start(bf16[3,8,128,128]{3,2,1,0:T(8,128)(2,1)} %get-tuple-element.131), channel_id=1, source_target_pairs={{0,8},{4,12},{8,16},{12,20},{16,24},{20,28},{1,9},{5,13},{9,17},{1... | collective-permute-start | bytes 2359304 | tf_op jit(solution)/shard_map/ppermute | solution.py:350
  183.2 44.5 %collective-permute-start.15 = (bf16[3,4,128,128]{3,2,1,0:T(8,128)(2,1)S(1)}, bf16[3,4,128,128]{3,2,1,0:T(8,128)(2,1)S(1)}, u32[]{:S(2)}, u32[]{:S(2)}) collective-permute-start(bf16[3,4,128,128]{3,2,1,0:T(8,128)(2,1)S(1)} %get-tuple-element.141), channel_id=1, source_target_pairs={{8,0},{12,4},{16,8},{20,12},{24,16},{28,20},{9,1},{13,5},{17,9},{2... | collective-permute-start | bytes 1179656 | tf_op jit(solution)/shard_map/ppermute | solution.py:351
  184.5 43.2 %collective-permute-start.14 = (bf16[3,4,128,128]{3,2,1,0:T(8,128)(2,1)S(1)}, bf16[3,4,128,128]{3,2,1,0:T(8,128)(2,1)S(1)}, u32[]{:S(2)}, u32[]{:S(2)}) collective-permute-start(bf16[3,4,128,128]{3,2,1,0:T(8,128)(2,1)S(1)} %get-tuple-element.142), channel_id=1, source_target_pairs={{0,8},{4,12},{8,16},{12,20},{16,24},{20,28},{1,9},{5,13},{9,17},{1... | collective-permute-start | bytes 1179656 | tf_op jit(solution)/shard_map/ppermute | solution.py:350
  203.3 28.9 %collective-permute-start.27 = (bf16[3,8,128,128]{3,2,1,0:T(8,128)(2,1)}, bf16[3,8,128,128]{3,2,1,0:T(8,128)(2,1)S(1)}, u32[]{:S(2)}, u32[]{:S(2)}) collective-permute-start(bf16[3,8,128,128]{3,2,1,0:T(8,128)(2,1)} %get-tuple-element.128), channel_id=1, source_target_pairs={{8,0},{12,4},{16,8},{20,12},{24,16},{28,20},{9,1},{13,5},{17,9},{2... | collective-permute-start | bytes 2359304 | tf_op jit(solution)/shard_map/ppermute | solution.py:351
  204.6 27.6 %collective-permute-start.28 = (bf16[3,8,128,128]{3,2,1,0:T(8,128)(2,1)}, bf16[3,8,128,128]{3,2,1,0:T(8,128)(2,1)S(1)}, u32[]{:S(2)}, u32[]{:S(2)}) collective-permute-start(bf16[3,8,128,128]{3,2,1,0:T(8,128)(2,1)} %get-tuple-element.129), channel_id=1, source_target_pairs={{0,8},{4,12},{8,16},{12,20},{16,24},{20,28},{1,9},{5,13},{9,17},{1... | collective-permute-start | bytes 2359304 | tf_op jit(solution)/shard_map/ppermute | solution.py:350
  231.8 29.0 %collective-permute-start.29 = (bf16[2,3,8,128,128]{4,3,2,1,0:T(8,128)(2,1)S(1)}, bf16[2,3,8,128,128]{4,3,2,1,0:T(8,128)(2,1)S(1)}, u32[]{:S(2)}, u32[]{:S(2)}) collective-permute-start(bf16[2,3,8,128,128]{4,3,2,1,0:T(8,128)(2,1)S(1)} %pad_maximum_fusion.5.refs_2_.refs_9_), channel_id=1, source_target_pairs={{0,4},{4,0},{8,12},{12,8},{16,20},{20,16},{24,28},{28,24},{1,5},{5... | collective-permute-start | bytes 4718600 | tf_op jit(solution)/shard_map/ppermute | solution.py:303
  237.9 24.3 %collective-permute-start.30 = (bf16[2,3,8,128,128]{4,3,2,1,0:T(8,128)(2,1)S(1)}, bf16[2,3,8,128,128]{4,3,2,1,0:T(8,128)(2,1)S(1)}, u32[]{:S(2)}, u32[]{:S(2)}) collective-permute-start(bf16[2,3,8,128,128]{4,3,2,1,0:T(8,128)(2,1)S(1)} %pad_maximum_fusion.6.refs_3_.refs_10_), channel_id=1, source_target_pairs={{0,4},{4,0},{8,12},{12,8},{16,20},{20,16},{24,28},{28,24},{1,5},{5... | collective-permute-start | bytes 4718600 | tf_op jit(solution)/shard_map/ppermute | solution.py:303
  254.2 25.6 %collective-permute-start.34 = (bf16[3,4,128,128]{3,2,1,0:T(8,128)(2,1)}, bf16[3,4,128,128]{3,2,1,0:T(8,128)(2,1)S(1)}, u32[]{:S(2)}, u32[]{:S(2)}) collective-permute-start(bf16[3,4,128,128]{3,2,1,0:T(8,128)(2,1)} %get-tuple-element.137), channel_id=1, source_target_pairs={{8,0},{12,4},{16,8},{20,12},{24,16},{28,20},{9,1},{13,5},{17,9},{2... | collective-permute-start | bytes 1179656 | tf_op jit(solution)/shard_map/ppermute | solution.py:351
  255.5 24.3 %collective-permute-start.33 = (bf16[3,4,128,128]{3,2,1,0:T(8,128)(2,1)}, bf16[3,4,128,128]{3,2,1,0:T(8,128)(2,1)S(1)}, u32[]{:S(2)}, u32[]{:S(2)}) collective-permute-start(bf16[3,4,128,128]{3,2,1,0:T(8,128)(2,1)} %get-tuple-element.138), channel_id=1, source_target_pairs={{0,8},{4,12},{8,16},{12,20},{16,24},{20,28},{1,9},{5,13},{9,17},{1... | collective-permute-start | bytes 1179656 | tf_op jit(solution)/shard_map/ppermute | solution.py:350
  298.6 45.2 %collective-permute-start.42 = (bf16[2,3,8,128,128]{4,3,2,1,0:T(8,128)(2,1)}, bf16[2,3,8,128,128]{4,3,2,1,0:T(8,128)(2,1)}, u32[]{:S(2)}, u32[]{:S(2)}) collective-permute-start(bf16[2,3,8,128,128]{4,3,2,1,0:T(8,128)(2,1)} %add_convert_fusion), channel_id=1, source_target_pairs={{0,8},{4,12},{8,0},{12,4},{16,24},{20,28},{24,16},{28,20},{1,9},{5... | collective-permute-start | bytes 4718600 | tf_op jit(solution)/shard_map/ppermute | solution.py:374
  315.4 37.6 %collective-permute-start.47 = (bf16[3,8,128,128]{3,2,1,0:T(8,128)(2,1)}, bf16[3,8,128,128]{3,2,1,0:T(8,128)(2,1)S(1)}, u32[]{:S(2)}, u32[]{:S(2)}) collective-permute-start(bf16[3,8,128,128]{3,2,1,0:T(8,128)(2,1)} %get-tuple-element.126), channel_id=1, source_target_pairs={{0,8},{4,12},{8,16},{12,20},{16,24},{20,28},{1,9},{5,13},{9,17},{1... | collective-permute-start | bytes 2359304 | tf_op jit(solution)/shard_map/ppermute | solution.py:350
  317.6 36.9 %collective-permute-start.48 = (bf16[3,8,128,128]{3,2,1,0:T(8,128)(2,1)}, bf16[3,8,128,128]{3,2,1,0:T(8,128)(2,1)}, u32[]{:S(2)}, u32[]{:S(2)}) collective-permute-start(bf16[3,8,128,128]{3,2,1,0:T(8,128)(2,1)} %get-tuple-element.127), channel_id=1, source_target_pairs={{8,0},{12,4},{16,8},{20,12},{24,16},{28,20},{9,1},{13,5},{17,9},{2... | collective-permute-start | bytes 2359304 | tf_op jit(solution)/shard_map/ppermute | solution.py:351
  343.8 25.1 %collective-permute-start.43 = (bf16[2,8,128,256]{3,2,1,0:T(8,128)(2,1)}, bf16[2,8,128,256]{3,2,1,0:T(8,128)(2,1)S(1)}, u32[]{:S(2)}, u32[]{:S(2)}) collective-permute-start(bf16[2,8,128,256]{3,2,1,0:T(8,128)(2,1)} %get-tuple-element.99), channel_id=1, source_target_pairs={{0,2},{1,3},{2,0},{3,1},{4,6},{5,7},{6,4},{7,5},{8,10},{9,11},{10,... | collective-permute-start | bytes 3145736 | tf_op jit(solution)/shard_map/ppermute | solution.py:300
  345.4 49.5 %collective-permute-start.49 = (bf16[3,4,128,128]{3,2,1,0:T(8,128)(2,1)}, bf16[3,4,128,128]{3,2,1,0:T(8,128)(2,1)S(1)}, u32[]{:S(2)}, u32[]{:S(2)}) collective-permute-start(bf16[3,4,128,128]{3,2,1,0:T(8,128)(2,1)} %get-tuple-element.133), channel_id=1, source_target_pairs={{0,8},{4,12},{8,16},{12,20},{16,24},{20,28},{1,9},{5,13},{9,17},{1... | collective-permute-start | bytes 1179656 | tf_op jit(solution)/shard_map/ppermute | solution.py:350
  351.2 29.7 %collective-permute-start.51 = (bf16[2,3,8,128,128]{4,3,2,1,0:T(8,128)(2,1)S(1)}, bf16[2,3,8,128,128]{4,3,2,1,0:T(8,128)(2,1)S(1)}, u32[]{:S(2)}, u32[]{:S(2)}) collective-permute-start(bf16[2,3,8,128,128]{4,3,2,1,0:T(8,128)(2,1)S(1)} %copy-done.20), channel_id=1, source_target_pairs={{0,4},{4,0},{8,12},{12,8},{16,20},{20,16},{24,28},{28,24},{1,5},{5... | collective-permute-start | bytes 4718600 | tf_op jit(solution)/shard_map/ppermute | solution.py:303
  353.0 24.5 %collective-permute-start.45 = (bf16[2,8,128,256]{3,2,1,0:T(8,128)(2,1)}, bf16[2,8,128,256]{3,2,1,0:T(8,128)(2,1)S(1)}, u32[]{:S(2)}, u32[]{:S(2)}) collective-permute-start(bf16[2,8,128,256]{3,2,1,0:T(8,128)(2,1)} %get-tuple-element.101), channel_id=1, source_target_pairs={{0,1},{1,0},{2,3},{3,2},{4,5},{5,4},{6,7},{7,6},{8,9},{9,8},{10,11... | collective-permute-start | bytes 3145736 | tf_op jit(solution)/shard_map/ppermute | solution.py:300
  357.6 24.9 %collective-permute-start.53 = (bf16[2,3,4,128,128]{4,3,2,1,0:T(8,128)(2,1)S(1)}, bf16[2,3,4,128,128]{4,3,2,1,0:T(8,128)(2,1)S(1)}, u32[]{:S(2)}, u32[]{:S(2)}) collective-permute-start(bf16[2,3,4,128,128]{4,3,2,1,0:T(8,128)(2,1)S(1)} %copy-done.22), channel_id=1, source_target_pairs={{0,4},{4,0},{8,12},{12,8},{16,20},{20,16},{24,28},{28,24},{1,5},{5... | collective-permute-start | bytes 2359304 | tf_op jit(solution)/shard_map/ppermute | solution.py:303
  377.5 29.3 %collective-permute-start.50 = (bf16[3,4,128,128]{3,2,1,0:T(8,128)(2,1)S(1)}, bf16[3,4,128,128]{3,2,1,0:T(8,128)(2,1)S(1)}, u32[]{:S(2)}, u32[]{:S(2)}) collective-permute-start(bf16[3,4,128,128]{3,2,1,0:T(8,128)(2,1)S(1)} %copy-done.54), channel_id=1, source_target_pairs={{8,0},{12,4},{16,8},{20,12},{24,16},{28,20},{9,1},{13,5},{17,9},{2... | collective-permute-start | bytes 1179656 | tf_op jit(solution)/shard_map/ppermute | solution.py:351
  380.9 70.1 %collective-permute-start.46 = (bf16[2,16,128,256]{3,2,1,0:T(8,128)(2,1)}, bf16[2,16,128,256]{3,2,1,0:T(8,128)(2,1)}, u32[]{:S(2)}, u32[]{:S(2)}) collective-permute-start(bf16[2,16,128,256]{3,2,1,0:T(8,128)(2,1)} %pad_maximum_fusion.4), channel_id=1, source_target_pairs={{0,2},{1,3},{2,0},{3,1},{4,6},{5,7},{6,4},{7,5},{8,10},{9,11},{10,... | collective-permute-start | bytes 6291464 | tf_op jit(solution)/shard_map/ppermute | solution.py:300
  382.5 68.5 %collective-permute-start.44 = (bf16[2,16,128,256]{3,2,1,0:T(8,128)(2,1)}, bf16[2,16,128,256]{3,2,1,0:T(8,128)(2,1)}, u32[]{:S(2)}, u32[]{:S(2)}) collective-permute-start(bf16[2,16,128,256]{3,2,1,0:T(8,128)(2,1)} %pad_maximum_fusion.3), channel_id=1, source_target_pairs={{0,1},{1,0},{2,3},{3,2},{4,5},{5,4},{6,7},{7,6},{8,9},{9,8},{10,11... | collective-permute-start | bytes 6291464 | tf_op jit(solution)/shard_map/ppermute | solution.py:300
  391.6 51.6 %collective-permute-start.52 = (bf16[3,8,128,128]{3,2,1,0:T(8,128)(2,1)S(1)}, bf16[3,8,128,128]{3,2,1,0:T(8,128)(2,1)S(1)}, u32[]{:S(2)}, u32[]{:S(2)}) collective-permute-start(bf16[3,8,128,128]{3,2,1,0:T(8,128)(2,1)S(1)} %fusion.15), channel_id=1, source_target_pairs={{0,16},{4,20},{8,24},{12,28},{16,0},{20,4},{24,8},{28,12},{1,17},{... | collective-permute-start | bytes 2359304 | tf_op jit(solution)/shard_map/ppermute | solution.py:380
  395.0 47.9 %collective-permute-start.55 = (bf16[3,4,128,128]{3,2,1,0:T(8,128)(2,1)S(1)}, bf16[3,4,128,128]{3,2,1,0:T(8,128)(2,1)S(1)}, u32[]{:S(2)}, u32[]{:S(2)}) collective-permute-start(bf16[3,4,128,128]{3,2,1,0:T(8,128)(2,1)S(1)} %fusion.45), channel_id=1, source_target_pairs={{0,16},{4,20},{8,24},{12,28},{16,0},{20,4},{24,8},{28,12},{1,17},{... | collective-permute-start | bytes 1179656 | tf_op jit(solution)/shard_map/ppermute | solution.py:380
  (84 other events, 820.9 us)
Sparse Core Ops, SparseCore 0:
  10.4 90.2 all-gather.2

commit v6 on v5

--- a/solution.py
+++ b/solution.py
@@ -373,12 +373,17 @@
             self.grads = grads
             self.near = lax.ppermute(total_of(grads[1], grads[3]), "row", [(r, r ^ 2) for r in range(n_row)])
 
+        def finish(self, after=()):
+            keep, _, got, _ = self.grads
+            near, _ = lax.optimization_barrier((self.near, after))
+            far = jnp.where(self.even_z, near[1], near[0])
+            self.mine = jnp.where(self.even_z, near[0], near[1])
+            self.rest = lax.ppermute(total_of(keep[1], got[1], far), "row", [(r, r ^ 4) for r in range(n_row)])
+            return self
+
         def total(self):
             keep, _, got, _ = self.grads
-            far = jnp.where(self.even_z, self.near[1], self.near[0])
-            mine = jnp.where(self.even_z, self.near[0], self.near[1])
-            rest = lax.ppermute(total_of(keep[1], got[1], far), "row", [(r, r ^ 4) for r in range(n_row)])
-            return total_of(keep[0], got[0], mine, rest)
+            return total_of(keep[0], got[0], self.mine, self.rest)
 
     def shards(tokens, out_grad, gate_weight, up_weight, down_weight, gate_rows, up_rows, down_columns):
         f_total, part = gate_weight.shape[:2]
@@ -466,7 +471,10 @@
             *accs, _ = lax.optimization_barrier((*accs, fourth.near))
             two.run(1)
             three.run(1)
-            sums = [one.total(), two.total(), three.total(), fourth.total(), Halves(z, last).total()]
+            fifth = Halves(z, last)
+            fourth.finish()
+            fifth.finish((fourth.rest,))
+            sums = [one.total(), two.total(), three.total(), fourth.total(), fifth.total()]
         else:
             gather = Chain(z, own_tiles(0, f_total)).run(nz - 1)
             grads, part_0 = compute(0, f_total, all_tiles(gather.slots()), 0)

time: 473 us -> 459 us (0.970)
  the two profiles are of different devices: /device:TPU:0 before, /device:TPU:24 now
where the time goes in v6:
time: 459 us; the launch traced here: 451 us
  waiting for transfers between devices  177 us (39%)
  Pallas kernels  91.9 us (20%)
  starting transfers between devices  86.3 us (19%)
  other arithmetic  51 us (11%)
  local copies, waits for them, and re-layouts  30 us (7%)
  between operations  15.5 us (3%)
    ppermute x15, waiting for transfers between devices, run(): self.from_left.append(lax.ppermute(to_right, 'row', right(start, stop)))  97.3 us
    ppermute x15, starting transfers between devices, run(): lax.ppermute(to_left, 'row', left(nz - stop, nz - start))  54.3 us
    pallas_call x5, Pallas kernels, run_grads(): pl.pallas_call(kernel, grid_spec=pltpu.PrefetchScalarGridSpec(num_scalar_...  51 us
    pallas_call x2, Pallas kernels, run_adds(): pl.pallas_call(kernel, grid_spec=pltpu.PrefetchScalarGridSpec(num_scalar_...  40.8 us
    ppermute x2, waiting for transfers between devices, finish(): lax.ppermute(total_of(keep[1], got[1], far), 'row', [(r, r ^ 4) for r in...  33.8 us
    ppermute x15, starting transfers between devices, run(): self.from_left.append(lax.ppermute(to_right, 'row', right(start, stop)))  20.2 us
    unnamed x122, local copies, waits for them, and re-layouts  18.7 us
    ppermute x15, waiting for transfers between devices, run(): lax.ppermute(to_left, 'row', left(nz - stop, nz - start))  18.3 us
  transfers between devices with their start and end apart: 57, of which 20 were waited for; matrix products, arithmetic and copies ran while one was open for 13% of the time, Pallas kernels for 20%

profile of v6, /device:TPU:24, one launch (start us, length us, event | category | flops | bytes accessed | tf_op | source)
XLA Modules:
  0.0 451.5 jit_solution(6546201322542229770)
XLA Ops:
  14.0 4.6 %collective-permute-start.3 = (bf16[3,12,128,128]{3,2,1,0:T(8,128)(2,1)S(1)}, bf16[3,12,128,128]{3,2,1,0:T(8,128)(2,1)S(1)}, u32[]{:S(2)}, u32[]{:S(2)}) collective-permute-start(bf16[3,12,128,128]{3,2,1,0:T(8,128)(2,1)S(1)} %get-tuple-element.148), channel_id=1, source_target_pairs={{8,0},{12,4},{16,8},{20,12},{24,16},{28,20},{9,1},{13,5},{17,9},{2... | collective-permute-start | bytes 3538952 | tf_op jit(solution)/shard_map/ppermute | solution.py:351
  18.6 23.7 %collective-permute-done.1 = bf16[3,12,128,128]{3,2,1,0:T(8,128)(2,1)S(1)} collective-permute-done((bf16[3,12,128,128]{3,2,1,0:T(8,128)(2,1)S(1)}, bf16[3,12,128,128]{3,2,1,0:T(8,128)(2,1)S(1)}, u32[]{:S(2)}, u32[]{:S(2)}) %collective-permute-start.1) | collective-permute-done | bytes 1179680 | tf_op jit(solution)/shard_map/ppermute | solution.py:350
  45.3 25.9 %collective-permute-done.2 = bf16[3,12,128,128]{3,2,1,0:T(8,128)(2,1)} collective-permute-done((bf16[3,12,128,128]{3,2,1,0:T(8,128)(2,1)S(1)}, bf16[3,12,128,128]{3,2,1,0:T(8,128)(2,1)}, u32[]{:S(2)}, u32[]{:S(2)}) %collective-permute-start.2) | collective-permute-done | bytes 1179680 | tf_op jit(solution)/shard_map/ppermute | solution.py:350
  76.0 23.5 %collective-permute-done.6 = bf16[3,12,128,128]{3,2,1,0:T(8,128)(2,1)} collective-permute-done((bf16[3,12,128,128]{3,2,1,0:T(8,128)(2,1)}, bf16[3,12,128,128]{3,2,1,0:T(8,128)(2,1)}, u32[]{:S(2)}, u32[]{:S(2)}) %collective-permute-start.6) | collective-permute-done | bytes 1179680 | tf_op jit(solution)/shard_map/ppermute | solution.py:350
  108.4 5.3 %collective-permute-start.9 = (bf16[3,4,128,128]{3,2,1,0:T(8,128)(2,1)}, bf16[3,4,128,128]{3,2,1,0:T(8,128)(2,1)}, u32[]{:S(2)}, u32[]{:S(2)}) collective-permute-start(bf16[3,4,128,128]{3,2,1,0:T(8,128)(2,1)} %get-tuple-element.183), channel_id=1, source_target_pairs={{8,0},{12,4},{16,8},{20,12},{24,16},{28,20},{9,1},{13,5},{17,9},{2... | collective-permute-start | bytes 1179656 | tf_op jit(solution)/shard_map/ppermute | solution.py:351
  114.5 9.0 %ffn_grads.5 = (bf16[2,3,4,128,128]{4,3,2,1,0:T(8,128)(2,1)S(1)}, bf16[2,3,4,128,128]{4,3,2,1,0:T(8,128)(2,1)S(1)}, bf16[2,3,4,128,128]{4,3,2,1,0:T(8,128)(2,1)}...) custom-call(s32[681]{0:T(1024)S(1)} %concatenate.18.scal, bf16[4,2,256,2048]{3,2,1,0:T(8,128)(2,1)} %bitcast.283, ...), custom_call_target="tpu_custom_call" | custom-call | flops 1610612736 | bytes 25165824 | tf_op jit(solution)/shard_map/ffn_grads/pallas_call | solution.py:126
  133.8 4.6 %collective-permute-start.12 = (bf16[3,4,128,128]{3,2,1,0:T(8,128)(2,1)S(1)}, bf16[3,4,128,128]{3,2,1,0:T(8,128)(2,1)S(1)}, u32[]{:S(2)}, u32[]{:S(2)}) collective-permute-start(bf16[3,4,128,128]{3,2,1,0:T(8,128)(2,1)S(1)} %get-tuple-element.145), channel_id=1, source_target_pairs={{8,0},{12,4},{16,8},{20,12},{24,16},{28,20},{9,1},{13,5},{17,9},{2... | collective-permute-start | bytes 1179656 | tf_op jit(solution)/shard_map/ppermute | solution.py:351
  139.9 12.6 %ffn_grads.6 = (bf16[2,3,8,128,128]{4,3,2,1,0:T(8,128)(2,1)S(1)}, bf16[2,3,8,128,128]{4,3,2,1,0:T(8,128)(2,1)S(1)}, bf16[2,3,8,128,128]{4,3,2,1,0:T(8,128)(2,1)}...) custom-call(s32[681]{0:T(1024)S(1)} %concatenate.18.scal, bf16[4,2,256,2048]{3,2,1,0:T(8,128)(2,1)} %bitcast.284, ...), custom_call_target="tpu_custom_call" | custom-call | flops 3221225472 | bytes 50331648 | tf_op jit(solution)/shard_map/ffn_grads/pallas_call | solution.py:126
  155.8 5.0 %collective-permute-done.11 = bf16[3,4,128,128]{3,2,1,0:T(8,128)(2,1)S(1)} collective-permute-done((bf16[3,4,128,128]{3,2,1,0:T(8,128)(2,1)S(1)}, bf16[3,4,128,128]{3,2,1,0:T(8,128)(2,1)S(1)}, u32[]{:S(2)}, u32[]{:S(2)}) %collective-permute-start.11) | collective-permute-done | bytes 393248 | tf_op jit(solution)/shard_map/ppermute | solution.py:350
  161.3 5.3 %collective-permute-done.22 = bf16[2,3,8,128,128]{4,3,2,1,0:T(8,128)(2,1)S(1)} collective-permute-done((bf16[2,3,8,128,128]{4,3,2,1,0:T(8,128)(2,1)}, bf16[2,3,8,128,128]{4,3,2,1,0:T(8,128)(2,1)S(1)}, u32[]{:S(2)}, u32[]{:S(2)}) %collective-permute-start.22) | collective-permute-done | bytes 1572896 | tf_op jit(solution)/shard_map/ppermute | solution.py:303
  166.7 5.0 %fusion.12 = (bf16[3,8,128,128]{3,2,1,0:T(8,128)(2,1)}, bf16[3,8,128,128]{3,2,1,0:T(8,128)(2,1)}) fusion(bf16[3,8,128,128]{3,2,1,0:T(8,128)(2,1)} %collective-permute-done.21, pred[]{:T(512)S(6)} %ge.15, bf16[2,3,8,128,128]{4,3,2,1,0:T(8,128)(2,1)S(1)} %collective-permute-done.22, bf16[2,3,8,128,128]{4,3,2,1,0:T(8,128)(2,1)S(1)} %get-tuple-element.73, ...), kind=kLoop, calls=%fused_computation.37 | loop fusion | flops 5505024 | bytes 6291458 | tf_op jit(solution)/shard_map/jit(_where)/select_n | solution.py:347
  178.6 4.6 %collective-permute-start.15 = (bf16[3,4,128,128]{3,2,1,0:T(8,128)(2,1)S(1)}, bf16[3,4,128,128]{3,2,1,0:T(8,128)(2,1)S(1)}, u32[]{:S(2)}, u32[]{:S(2)}) collective-permute-start(bf16[3,4,128,128]{3,2,1,0:T(8,128)(2,1)S(1)} %get-tuple-element.143), channel_id=1, source_target_pairs={{8,0},{12,4},{16,8},{20,12},{24,16},{28,20},{9,1},{13,5},{17,9},{2... | collective-permute-start | bytes 1179656 | tf_op jit(solution)/shard_map/ppermute | solution.py:351
  184.5 8.3 %collective-permute-done.24 = bf16[3,8,128,128]{3,2,1,0:T(8,128)(2,1)} collective-permute-done((bf16[3,8,128,128]{3,2,1,0:T(8,128)(2,1)}, bf16[3,8,128,128]{3,2,1,0:T(8,128)(2,1)}, u32[]{:S(2)}, u32[]{:S(2)}) %collective-permute-start.24) | collective-permute-done | bytes 786464 | tf_op jit(solution)/shard_map/ppermute | solution.py:351
  192.8 5.3 %collective-permute-done.23 = bf16[3,8,128,128]{3,2,1,0:T(8,128)(2,1)} collective-permute-done((bf16[3,8,128,128]{3,2,1,0:T(8,128)(2,1)}, bf16[3,8,128,128]{3,2,1,0:T(8,128)(2,1)}, u32[]{:S(2)}, u32[]{:S(2)}) %collective-permute-start.23) | collective-permute-done | bytes 786464 | tf_op jit(solution)/shard_map/ppermute | solution.py:350
  198.1 4.0 fusion.14
  206.5 17.6 %ffn_adds.2 = (f32[64,128,256]{2,1,0:T(8,128)}, f32[64,128,256]{2,1,0:T(8,128)}) custom-call(s32[681]{0:T(1024)} %copy-done.17, bf16[3,4,128,256]{3,2,1,0:T(8,128)(2,1)} %copy-done.8, bf16[2,3,12,128,128]{4,3,2,1,0:T(8,128)(2,1)} %copy-done.21, bf16[2,3,12,128,128]{4,3,2,1,0:T(8,128)(2,1)} %pad_maximum_fusion.1.refs_2_.refs_3_.refs_7_, ...), custom_call_target="tpu_custom_call" | custom-call | flops 2415919104 | bytes 50331648 | tf_op jit(solution)/shard_map/ffn_adds/pallas_call | solution.py:261
  235.3 4.9 %collective-permute-start.19 = (bf16[3,4,128,128]{3,2,1,0:T(8,128)(2,1)S(1)}, bf16[3,4,128,128]{3,2,1,0:T(8,128)(2,1)S(1)}, u32[]{:S(2)}, u32[]{:S(2)}) collective-permute-start(bf16[3,4,128,128]{3,2,1,0:T(8,128)(2,1)S(1)} %get-tuple-element.180), channel_id=1, source_target_pairs={{8,0},{12,4},{16,8},{20,12},{24,16},{28,20},{9,1},{13,5},{17,9},{2... | collective-permute-start | bytes 1179656 | tf_op jit(solution)/shard_map/ppermute | solution.py:351
  242.5 8.1 %ffn_grads.7 = (bf16[2,3,4,128,128]{4,3,2,1,0:T(8,128)(2,1)S(1)}, bf16[2,3,4,128,128]{4,3,2,1,0:T(8,128)(2,1)S(1)}, bf16[2,3,4,128,128]{4,3,2,1,0:T(8,128)(2,1)S...) custom-call(s32[681]{0:T(1024)S(1)} %copy-done.18, bf16[4,2,256,2048]{3,2,1,0:T(8,128)(2,1)} %bitcast.285, ...), custom_call_target="tpu_custom_call" | custom-call | flops 1610612736 | bytes 25165824 | tf_op jit(solution)/shard_map/ffn_grads/pallas_call | solution.py:126
  257.5 4.4 collective-permute-start.32
  263.7 12.6 %ffn_grads.8 = (bf16[2,3,8,128,128]{4,3,2,1,0:T(8,128)(2,1)S(1)}, bf16[2,3,8,128,128]{4,3,2,1,0:T(8,128)(2,1)S(1)}, bf16[2,3,8,128,128]{4,3,2,1,0:T(8,128)(2,1)}...) custom-call(s32[681]{0:T(1024)S(1)} %copy-done.18, bf16[4,2,256,2048]{3,2,1,0:T(8,128)(2,1)} %bitcast.286, ...), custom_call_target="tpu_custom_call" | custom-call | flops 3221225472 | bytes 50331648 | tf_op jit(solution)/shard_map/ffn_grads/pallas_call | solution.py:126
  283.1 7.3 %collective-permute-done.37 = bf16[3,4,128,128]{3,2,1,0:T(8,128)(2,1)S(1)} collective-permute-done((bf16[3,4,128,128]{3,2,1,0:T(8,128)(2,1)S(1)}, bf16[3,4,128,128]{3,2,1,0:T(8,128)(2,1)S(1)}, u32[]{:S(2)}, u32[]{:S(2)}) %collective-permute-start.37) | collective-permute-done | bytes 393248 | tf_op jit(solution)/shard_map/ppermute | solution.py:351
  290.4 4.1 collective-permute-done.38
  300.1 8.8 %ffn_grads.9 = (bf16[2,3,4,128,128]{4,3,2,1,0:T(8,128)(2,1)S(1)}, bf16[2,3,4,128,128]{4,3,2,1,0:T(8,128)(2,1)S(1)}, bf16[2,3,4,128,128]{4,3,2,1,0:T(8,128)(2,1)S...) custom-call(s32[681]{0:T(1024)S(1)} %copy-done.18, bf16[4,2,256,2048]{3,2,1,0:T(8,128)(2,1)} %bitcast.287, ...), custom_call_target="tpu_custom_call" | custom-call | flops 1610612736 | bytes 25165824 | tf_op jit(solution)/shard_map/ffn_grads/pallas_call | solution.py:126
  314.3 4.8 %collective-permute-start.48 = (bf16[3,8,128,128]{3,2,1,0:T(8,128)(2,1)}, bf16[3,8,128,128]{3,2,1,0:T(8,128)(2,1)S(1)}, u32[]{:S(2)}, u32[]{:S(2)}) collective-permute-start(bf16[3,8,128,128]{3,2,1,0:T(8,128)(2,1)} %get-tuple-element.129), channel_id=1, source_target_pairs={{8,0},{12,4},{16,8},{20,12},{24,16},{28,20},{9,1},{13,5},{17,9},{2... | collective-permute-start | bytes 2359304 | tf_op jit(solution)/shard_map/ppermute | solution.py:351
  320.5 23.3 %ffn_adds.3 = (bf16[2,16,128,256]{3,2,1,0:T(8,128)(2,1)}, bf16[2,16,128,256]{3,2,1,0:T(8,128)(2,1)}, bf16[2,16,128,256]{3,2,1,0:T(8,128)(2,1)}, bf16[2,8,128,256]{3,2,1,0:T(8,128)(2,1)}, bf16[2,8,128,256]{3,2,1,0:T(8,128)(2,1)}) custom-call(s32[681]{0:T(1024)} %copy-done.17, bf16[2,3,4,128,128]{4,3,2,1,0:T(8,128)(2,1)} %collective-permute-done.41.refs_0_, ...), custom_call_target="tpu_custom_call" | custom-call | flops 3221225472 | bytes 50331648 | tf_op jit(solution)/shard_map/ffn_adds/pallas_call | solution.py:261
  346.6 5.6 %collective-permute-done.47 = bf16[3,8,128,128]{3,2,1,0:T(8,128)(2,1)S(1)} collective-permute-done((bf16[3,8,128,128]{3,2,1,0:T(8,128)(2,1)}, bf16[3,8,128,128]{3,2,1,0:T(8,128)(2,1)S(1)}, u32[]{:S(2)}, u32[]{:S(2)}) %collective-permute-start.47) | collective-permute-done | bytes 786464 | tf_op jit(solution)/shard_map/ppermute | solution.py:350
  363.8 4.8 %collective-permute-done.43 = bf16[2,8,128,256]{3,2,1,0:T(8,128)(2,1)S(1)} collective-permute-done((bf16[2,8,128,256]{3,2,1,0:T(8,128)(2,1)}, bf16[2,8,128,256]{3,2,1,0:T(8,128)(2,1)S(1)}, u32[]{:S(2)}, u32[]{:S(2)}) %collective-permute-start.43) | collective-permute-done | bytes 1048608 | tf_op jit(solution)/shard_map/ppermute | solution.py:300
  370.7 7.5 %collective-permute-done.45 = bf16[2,8,128,256]{3,2,1,0:T(8,128)(2,1)S(1)} collective-permute-done((bf16[2,8,128,256]{3,2,1,0:T(8,128)(2,1)}, bf16[2,8,128,256]{3,2,1,0:T(8,128)(2,1)S(1)}, u32[]{:S(2)}, u32[]{:S(2)}) %collective-permute-start.45) | collective-permute-done | bytes 1048608 | tf_op jit(solution)/shard_map/ppermute | solution.py:300
  385.6 9.6 %collective-permute-done.54 = bf16[2,3,4,128,128]{4,3,2,1,0:T(8,128)(2,1)S(1)} collective-permute-done((bf16[2,3,4,128,128]{4,3,2,1,0:T(8,128)(2,1)S(1)}, bf16[2,3,4,128,128]{4,3,2,1,0:T(8,128)(2,1)S(1)}, u32[]{:S(2)}, u32[]{:S(2)}) %collective-permute-start.54) | collective-permute-done | bytes 786464 | tf_op jit(solution)/shard_map/ppermute | solution.py:374
  395.2 27.5 %collective-permute-done.52 = bf16[3,8,128,128]{3,2,1,0:T(8,128)(2,1)S(1)} collective-permute-done((bf16[3,8,128,128]{3,2,1,0:T(8,128)(2,1)S(1)}, bf16[3,8,128,128]{3,2,1,0:T(8,128)(2,1)S(1)}, u32[]{:S(2)}, u32[]{:S(2)}) %collective-permute-start.52) | collective-permute-done | bytes 786464 | tf_op jit(solution)/shard_map/ppermute | solution.py:381
  425.4 6.3 %collective-permute-done.55 = bf16[3,4,128,128]{3,2,1,0:T(8,128)(2,1)S(1)} collective-permute-done((bf16[3,4,128,128]{3,2,1,0:T(8,128)(2,1)S(1)}, bf16[3,4,128,128]{3,2,1,0:T(8,128)(2,1)S(1)}, u32[]{:S(2)}, u32[]{:S(2)}) %collective-permute-start.55) | collective-permute-done | bytes 393248 | tf_op jit(solution)/shard_map/ppermute | solution.py:381
  437.7 3.9 add_convert_fusion.1
  (268 shorter events, 128.3 us)
Async XLA Ops:
  7.2 107.3 %all-gather.3.cloned.1.call-start = ((), (), s32[]{:S(2)}) async-start(), calls=%async_computation | async-start | bytes 10485760 | tf_op jit(solution)/shard_map/all_gather | solution.py:402
  12.7 29.6 %collective-permute-start.1 = (bf16[3,12,128,128]{3,2,1,0:T(8,128)(2,1)S(1)}, bf16[3,12,128,128]{3,2,1,0:T(8,128)(2,1)S(1)}, u32[]{:S(2)}, u32[]{:S(2)}) collective-permute-start(bf16[3,12,128,128]{3,2,1,0:T(8,128)(2,1)S(1)} %get-tuple-element.148), channel_id=1, source_target_pairs={{0,8},{4,12},{8,16},{12,20},{16,24},{20,28},{1,9},{5,13},{9,17},{1... | collective-permute-start | bytes 3538952 | tf_op jit(solution)/shard_map/ppermute | solution.py:350
  14.0 29.6 %collective-permute-start.3 = (bf16[3,12,128,128]{3,2,1,0:T(8,128)(2,1)S(1)}, bf16[3,12,128,128]{3,2,1,0:T(8,128)(2,1)S(1)}, u32[]{:S(2)}, u32[]{:S(2)}) collective-permute-start(bf16[3,12,128,128]{3,2,1,0:T(8,128)(2,1)S(1)} %get-tuple-element.148), channel_id=1, source_target_pairs={{8,0},{12,4},{16,8},{20,12},{24,16},{28,20},{9,1},{13,5},{17,9},{2... | collective-permute-start | bytes 3538952 | tf_op jit(solution)/shard_map/ppermute | solution.py:351
  42.3 28.9 %collective-permute-start.2 = (bf16[3,12,128,128]{3,2,1,0:T(8,128)(2,1)S(1)}, bf16[3,12,128,128]{3,2,1,0:T(8,128)(2,1)}, u32[]{:S(2)}, u32[]{:S(2)}) collective-permute-start(bf16[3,12,128,128]{3,2,1,0:T(8,128)(2,1)S(1)} %collective-permute-done.1), channel_id=1, source_target_pairs={{8,16},{12,20},{16,24},{20,28},{9,17},{13,21},{17,25},{21,29},{10,... | collective-permute-start | bytes 3538952 | tf_op jit(solution)/shard_map/ppermute | solution.py:350
  43.6 28.9 %collective-permute-start.4 = (bf16[3,12,128,128]{3,2,1,0:T(8,128)(2,1)S(1)}, bf16[3,12,128,128]{3,2,1,0:T(8,128)(2,1)}, u32[]{:S(2)}, u32[]{:S(2)}) collective-permute-start(bf16[3,12,128,128]{3,2,1,0:T(8,128)(2,1)S(1)} %collective-permute-done.3), channel_id=1, source_target_pairs={{8,0},{12,4},{16,8},{20,12},{9,1},{13,5},{17,9},{21,13},{10,2},{14... | collective-permute-start | bytes 3538952 | tf_op jit(solution)/shard_map/ppermute | solution.py:351
  71.2 28.2 %collective-permute-start.6 = (bf16[3,12,128,128]{3,2,1,0:T(8,128)(2,1)}, bf16[3,12,128,128]{3,2,1,0:T(8,128)(2,1)}, u32[]{:S(2)}, u32[]{:S(2)}) collective-permute-start(bf16[3,12,128,128]{3,2,1,0:T(8,128)(2,1)} %collective-permute-done.2), channel_id=1, source_target_pairs={{16,24},{20,28},{17,25},{21,29},{18,26},{22,30},{19,27},{23,31}} | collective-permute-start | bytes 3538952 | tf_op jit(solution)/shard_map/ppermute | solution.py:350
  72.5 28.4 %collective-permute-start.5 = (bf16[3,12,128,128]{3,2,1,0:T(8,128)(2,1)}, bf16[3,12,128,128]{3,2,1,0:T(8,128)(2,1)}, u32[]{:S(2)}, u32[]{:S(2)}) collective-permute-start(bf16[3,12,128,128]{3,2,1,0:T(8,128)(2,1)} %collective-permute-done.4), channel_id=1, source_target_pairs={{8,0},{12,4},{9,1},{13,5},{10,2},{14,6},{11,3},{15,7}} | collective-permute-start | bytes 3538952 | tf_op jit(solution)/shard_map/ppermute | solution.py:351
  75.9 38.5 %collective-permute-start.7 = (bf16[2,3,12,128,128]{4,3,2,1,0:T(8,128)(2,1)S(1)}, bf16[2,3,12,128,128]{4,3,2,1,0:T(8,128)(2,1)}, u32[]{:S(2)}, u32[]{:S(2)}) collective-permute-start(bf16[2,3,12,128,128]{4,3,2,1,0:T(8,128)(2,1)S(1)} %pad_maximum_fusion.refs_1_.refs_2_.refs_6_), channel_id=1, source_target_pairs={{0,4},{4,0},{8,12},{12,8},{16,20},{20,16},{24,28},{28,24},{1,5},{5... | collective-permute-start | bytes 7077896 | tf_op jit(solution)/shard_map/ppermute | solution.py:303
  127.1 25.4 %collective-permute-start.21 = (bf16[3,8,128,128]{3,2,1,0:T(8,128)(2,1)}, bf16[3,8,128,128]{3,2,1,0:T(8,128)(2,1)}, u32[]{:S(2)}, u32[]{:S(2)}) collective-permute-start(bf16[3,8,128,128]{3,2,1,0:T(8,128)(2,1)} %get-tuple-element.166), channel_id=1, source_target_pairs={{8,0},{12,4},{16,8},{20,12},{24,16},{28,20},{9,1},{13,5},{17,9},{2... | collective-permute-start | bytes 2359304 | tf_op jit(solution)/shard_map/ppermute | solution.py:351
  130.6 22.6 %collective-permute-start.20 = (bf16[3,8,128,128]{3,2,1,0:T(8,128)(2,1)}, bf16[3,8,128,128]{3,2,1,0:T(8,128)(2,1)}, u32[]{:S(2)}, u32[]{:S(2)}) collective-permute-start(bf16[3,8,128,128]{3,2,1,0:T(8,128)(2,1)} %get-tuple-element.166), channel_id=1, source_target_pairs={{0,8},{4,12},{8,16},{12,20},{16,24},{20,28},{1,9},{5,13},{9,17},{1... | collective-permute-start | bytes 2359304 | tf_op jit(solution)/shard_map/ppermute | solution.py:350
  160.8 23.6 %collective-permute-start.26 = (bf16[2,3,8,128,128]{4,3,2,1,0:T(8,128)(2,1)}, bf16[2,3,8,128,128]{4,3,2,1,0:T(8,128)(2,1)}, u32[]{:S(2)}, u32[]{:S(2)}) collective-permute-start(bf16[2,3,8,128,128]{4,3,2,1,0:T(8,128)(2,1)} %get-tuple-element.78), channel_id=1, source_target_pairs={{0,4},{4,0},{8,12},{12,8},{16,20},{20,16},{24,28},{28,24},{1,5},{5... | collective-permute-start | bytes 4718600 | tf_op jit(solution)/shard_map/ppermute | solution.py:303
  175.5 22.6 %collective-permute-start.23 = (bf16[3,8,128,128]{3,2,1,0:T(8,128)(2,1)}, bf16[3,8,128,128]{3,2,1,0:T(8,128)(2,1)}, u32[]{:S(2)}, u32[]{:S(2)}) collective-permute-start(bf16[3,8,128,128]{3,2,1,0:T(8,128)(2,1)} %get-tuple-element.133), channel_id=1, source_target_pairs={{0,8},{4,12},{8,16},{12,20},{16,24},{20,28},{1,9},{5,13},{9,17},{1... | collective-permute-start | bytes 2359304 | tf_op jit(solution)/shard_map/ppermute | solution.py:350
  178.6 45.6 %collective-permute-start.15 = (bf16[3,4,128,128]{3,2,1,0:T(8,128)(2,1)S(1)}, bf16[3,4,128,128]{3,2,1,0:T(8,128)(2,1)S(1)}, u32[]{:S(2)}, u32[]{:S(2)}) collective-permute-start(bf16[3,4,128,128]{3,2,1,0:T(8,128)(2,1)S(1)} %get-tuple-element.143), channel_id=1, source_target_pairs={{8,0},{12,4},{16,8},{20,12},{24,16},{28,20},{9,1},{13,5},{17,9},{2... | collective-permute-start | bytes 1179656 | tf_op jit(solution)/shard_map/ppermute | solution.py:351
  183.2 41.1 %collective-permute-start.14 = (bf16[3,4,128,128]{3,2,1,0:T(8,128)(2,1)S(1)}, bf16[3,4,128,128]{3,2,1,0:T(8,128)(2,1)S(1)}, u32[]{:S(2)}, u32[]{:S(2)}) collective-permute-start(bf16[3,4,128,128]{3,2,1,0:T(8,128)(2,1)S(1)} %get-tuple-element.144), channel_id=1, source_target_pairs={{0,8},{4,12},{8,16},{12,20},{16,24},{20,28},{1,9},{5,13},{9,17},{1... | collective-permute-start | bytes 1179656 | tf_op jit(solution)/shard_map/ppermute | solution.py:350
  202.1 26.7 %collective-permute-start.27 = (bf16[3,8,128,128]{3,2,1,0:T(8,128)(2,1)}, bf16[3,8,128,128]{3,2,1,0:T(8,128)(2,1)S(1)}, u32[]{:S(2)}, u32[]{:S(2)}) collective-permute-start(bf16[3,8,128,128]{3,2,1,0:T(8,128)(2,1)} %get-tuple-element.130), channel_id=1, source_target_pairs={{8,0},{12,4},{16,8},{20,12},{24,16},{28,20},{9,1},{13,5},{17,9},{2... | collective-permute-start | bytes 2359304 | tf_op jit(solution)/shard_map/ppermute | solution.py:351
  204.9 23.9 %collective-permute-start.28 = (bf16[3,8,128,128]{3,2,1,0:T(8,128)(2,1)S(1)}, bf16[3,8,128,128]{3,2,1,0:T(8,128)(2,1)S(1)}, u32[]{:S(2)}, u32[]{:S(2)}) collective-permute-start(bf16[3,8,128,128]{3,2,1,0:T(8,128)(2,1)S(1)} %get-tuple-element.131), channel_id=1, source_target_pairs={{0,8},{4,12},{8,16},{12,20},{16,24},{20,28},{1,9},{5,13},{9,17},{1... | collective-permute-start | bytes 2359304 | tf_op jit(solution)/shard_map/ppermute | solution.py:350
  228.4 29.1 %collective-permute-start.29 = (bf16[2,3,8,128,128]{4,3,2,1,0:T(8,128)(2,1)S(1)}, bf16[2,3,8,128,128]{4,3,2,1,0:T(8,128)(2,1)S(1)}, u32[]{:S(2)}, u32[]{:S(2)}) collective-permute-start(bf16[2,3,8,128,128]{4,3,2,1,0:T(8,128)(2,1)S(1)} %pad_maximum_fusion.5.refs_2_.refs_9_), channel_id=1, source_target_pairs={{0,4},{4,0},{8,12},{12,8},{16,20},{20,16},{24,28},{28,24},{1,5},{5... | collective-permute-start | bytes 4718600 | tf_op jit(solution)/shard_map/ppermute | solution.py:303
  234.4 27.4 %collective-permute-start.30 = (bf16[2,3,8,128,128]{4,3,2,1,0:T(8,128)(2,1)S(1)}, bf16[2,3,8,128,128]{4,3,2,1,0:T(8,128)(2,1)S(1)}, u32[]{:S(2)}, u32[]{:S(2)}) collective-permute-start(bf16[2,3,8,128,128]{4,3,2,1,0:T(8,128)(2,1)S(1)} %pad_maximum_fusion.6.refs_3_.refs_10_), channel_id=1, source_target_pairs={{0,4},{4,0},{8,12},{12,8},{16,20},{20,16},{24,28},{28,24},{1,5},{5... | collective-permute-start | bytes 4718600 | tf_op jit(solution)/shard_map/ppermute | solution.py:303
  253.2 23.0 %collective-permute-start.34 = (bf16[3,4,128,128]{3,2,1,0:T(8,128)(2,1)}, bf16[3,4,128,128]{3,2,1,0:T(8,128)(2,1)S(1)}, u32[]{:S(2)}, u32[]{:S(2)}) collective-permute-start(bf16[3,4,128,128]{3,2,1,0:T(8,128)(2,1)} %get-tuple-element.139), channel_id=1, source_target_pairs={{8,0},{12,4},{16,8},{20,12},{24,16},{28,20},{9,1},{13,5},{17,9},{2... | collective-permute-start | bytes 1179656 | tf_op jit(solution)/shard_map/ppermute | solution.py:351
  298.0 45.7 %collective-permute-start.42 = (bf16[2,3,8,128,128]{4,3,2,1,0:T(8,128)(2,1)}, bf16[2,3,8,128,128]{4,3,2,1,0:T(8,128)(2,1)}, u32[]{:S(2)}, u32[]{:S(2)}) collective-permute-start(bf16[2,3,8,128,128]{4,3,2,1,0:T(8,128)(2,1)} %add_convert_fusion), channel_id=1, source_target_pairs={{0,8},{4,12},{8,0},{12,4},{16,24},{20,28},{24,16},{28,20},{1,9},{5... | collective-permute-start | bytes 4718600 | tf_op jit(solution)/shard_map/ppermute | solution.py:374
  312.6 48.1 %collective-permute-start.51 = (bf16[2,3,8,128,128]{4,3,2,1,0:T(8,128)(2,1)}, bf16[2,3,8,128,128]{4,3,2,1,0:T(8,128)(2,1)}, u32[]{:S(2)}, u32[]{:S(2)}) collective-permute-start(bf16[2,3,8,128,128]{4,3,2,1,0:T(8,128)(2,1)} %get-tuple-element.104), channel_id=1, source_target_pairs={{0,4},{4,0},{8,12},{12,8},{16,20},{20,16},{24,28},{28,24},{1,5},{5... | collective-permute-start | bytes 4718600 | tf_op jit(solution)/shard_map/ppermute | solution.py:303
  313.0 39.2 %collective-permute-start.47 = (bf16[3,8,128,128]{3,2,1,0:T(8,128)(2,1)}, bf16[3,8,128,128]{3,2,1,0:T(8,128)(2,1)S(1)}, u32[]{:S(2)}, u32[]{:S(2)}) collective-permute-start(bf16[3,8,128,128]{3,2,1,0:T(8,128)(2,1)} %get-tuple-element.128), channel_id=1, source_target_pairs={{0,8},{4,12},{8,16},{12,20},{16,24},{20,28},{1,9},{5,13},{9,17},{1... | collective-permute-start | bytes 2359304 | tf_op jit(solution)/shard_map/ppermute | solution.py:350
  314.3 39.7 %collective-permute-start.48 = (bf16[3,8,128,128]{3,2,1,0:T(8,128)(2,1)}, bf16[3,8,128,128]{3,2,1,0:T(8,128)(2,1)S(1)}, u32[]{:S(2)}, u32[]{:S(2)}) collective-permute-start(bf16[3,8,128,128]{3,2,1,0:T(8,128)(2,1)} %get-tuple-element.129), channel_id=1, source_target_pairs={{8,0},{12,4},{16,8},{20,12},{24,16},{28,20},{9,1},{13,5},{17,9},{2... | collective-permute-start | bytes 2359304 | tf_op jit(solution)/shard_map/ppermute | solution.py:351
  343.7 25.0 %collective-permute-start.43 = (bf16[2,8,128,256]{3,2,1,0:T(8,128)(2,1)}, bf16[2,8,128,256]{3,2,1,0:T(8,128)(2,1)S(1)}, u32[]{:S(2)}, u32[]{:S(2)}) collective-permute-start(bf16[2,8,128,256]{3,2,1,0:T(8,128)(2,1)} %get-tuple-element.100), channel_id=1, source_target_pairs={{0,2},{1,3},{2,0},{3,1},{4,6},{5,7},{6,4},{7,5},{8,10},{9,11},{10,... | collective-permute-start | bytes 3145736 | tf_op jit(solution)/shard_map/ppermute | solution.py:300
  345.3 36.8 %collective-permute-start.49 = (bf16[3,4,128,128]{3,2,1,0:T(8,128)(2,1)}, bf16[3,4,128,128]{3,2,1,0:T(8,128)(2,1)S(1)}, u32[]{:S(2)}, u32[]{:S(2)}) collective-permute-start(bf16[3,4,128,128]{3,2,1,0:T(8,128)(2,1)} %get-tuple-element.135), channel_id=1, source_target_pairs={{0,8},{4,12},{8,16},{12,20},{16,24},{20,28},{1,9},{5,13},{9,17},{1... | collective-permute-start | bytes 1179656 | tf_op jit(solution)/shard_map/ppermute | solution.py:350
  352.3 31.4 %collective-permute-start.50 = (bf16[3,4,128,128]{3,2,1,0:T(8,128)(2,1)}, bf16[3,4,128,128]{3,2,1,0:T(8,128)(2,1)S(1)}, u32[]{:S(2)}, u32[]{:S(2)}) collective-permute-start(bf16[3,4,128,128]{3,2,1,0:T(8,128)(2,1)} %get-tuple-element.136), channel_id=1, source_target_pairs={{8,0},{12,4},{16,8},{20,12},{24,16},{28,20},{9,1},{13,5},{17,9},{2... | collective-permute-start | bytes 1179656 | tf_op jit(solution)/shard_map/ppermute | solution.py:351
  354.0 24.2 %collective-permute-start.45 = (bf16[2,8,128,256]{3,2,1,0:T(8,128)(2,1)}, bf16[2,8,128,256]{3,2,1,0:T(8,128)(2,1)S(1)}, u32[]{:S(2)}, u32[]{:S(2)}) collective-permute-start(bf16[2,8,128,256]{3,2,1,0:T(8,128)(2,1)} %get-tuple-element.102), channel_id=1, source_target_pairs={{0,1},{1,0},{2,3},{3,2},{4,5},{5,4},{6,7},{7,6},{8,9},{9,8},{10,11... | collective-permute-start | bytes 3145736 | tf_op jit(solution)/shard_map/ppermute | solution.py:300
  361.7 61.0 %collective-permute-start.53 = (bf16[2,3,4,128,128]{4,3,2,1,0:T(8,128)(2,1)S(1)}, bf16[2,3,4,128,128]{4,3,2,1,0:T(8,128)(2,1)S(1)}, u32[]{:S(2)}, u32[]{:S(2)}) collective-permute-start(bf16[2,3,4,128,128]{4,3,2,1,0:T(8,128)(2,1)S(1)} %copy-done.20), channel_id=1, source_target_pairs={{0,4},{4,0},{8,12},{12,8},{16,20},{20,16},{24,28},{28,24},{1,5},{5... | collective-permute-start | bytes 2359304 | tf_op jit(solution)/shard_map/ppermute | solution.py:303
  368.7 26.5 %collective-permute-start.54 = (bf16[2,3,4,128,128]{4,3,2,1,0:T(8,128)(2,1)S(1)}, bf16[2,3,4,128,128]{4,3,2,1,0:T(8,128)(2,1)S(1)}, u32[]{:S(2)}, u32[]{:S(2)}) collective-permute-start(bf16[2,3,4,128,128]{4,3,2,1,0:T(8,128)(2,1)S(1)} %add_convert_fusion.5), channel_id=1, source_target_pairs={{0,8},{4,12},{8,0},{12,4},{16,24},{20,28},{24,16},{28,20},{1,9},{5... | collective-permute-start | bytes 2359304 | tf_op jit(solution)/shard_map/ppermute | solution.py:374
  378.2 44.5 %collective-permute-start.52 = (bf16[3,8,128,128]{3,2,1,0:T(8,128)(2,1)S(1)}, bf16[3,8,128,128]{3,2,1,0:T(8,128)(2,1)S(1)}, u32[]{:S(2)}, u32[]{:S(2)}) collective-permute-start(bf16[3,8,128,128]{3,2,1,0:T(8,128)(2,1)S(1)} %fusion.15), channel_id=1, source_target_pairs={{0,16},{4,20},{8,24},{12,28},{16,0},{20,4},{24,8},{28,12},{1,17},{... | collective-permute-start | bytes 2359304 | tf_op jit(solution)/shard_map/ppermute | solution.py:381
  382.2 55.6 %collective-permute-start.46 = (bf16[2,16,128,256]{3,2,1,0:T(8,128)(2,1)}, bf16[2,16,128,256]{3,2,1,0:T(8,128)(2,1)}, u32[]{:S(2)}, u32[]{:S(2)}) collective-permute-start(bf16[2,16,128,256]{3,2,1,0:T(8,128)(2,1)} %pad_maximum_fusion.4), channel_id=1, source_target_pairs={{0,2},{1,3},{2,0},{3,1},{4,6},{5,7},{6,4},{7,5},{8,10},{9,11},{10,... | collective-permute-start | bytes 6291464 | tf_op jit(solution)/shard_map/ppermute | solution.py:300
  383.7 54.0 %collective-permute-start.44 = (bf16[2,16,128,256]{3,2,1,0:T(8,128)(2,1)}, bf16[2,16,128,256]{3,2,1,0:T(8,128)(2,1)}, u32[]{:S(2)}, u32[]{:S(2)}) collective-permute-start(bf16[2,16,128,256]{3,2,1,0:T(8,128)(2,1)} %pad_maximum_fusion.3), channel_id=1, source_target_pairs={{0,1},{1,0},{2,3},{3,2},{4,5},{5,4},{6,7},{7,6},{8,9},{9,8},{10,11... | collective-permute-start | bytes 6291464 | tf_op jit(solution)/shard_map/ppermute | solution.py:300
  (81 other events, 872.2 us)
Sparse Core Ops, SparseCore 0:
  10.4 88.5 all-gather.2

commit v7 on v6

--- a/solution.py
+++ b/solution.py
@@ -470,9 +470,10 @@
             accs = add_up(accs, [part_2, part_3, part_4], True, (last[3],))
             *accs, _ = lax.optimization_barrier((*accs, fourth.near))
             two.run(1)
-            three.run(1)
             fifth = Halves(z, last)
             fourth.finish()
+            three.tie(2, fifth.near)
+            three.run(1)
             fifth.finish((fourth.rest,))
             sums = [one.total(), two.total(), three.total(), fourth.total(), fifth.total()]
         else:

time: 459 us -> 472 us (1.028)
  the two profiles are of different devices: /device:TPU:24 before, /device:TPU:0 now
where the time goes in v7:
time: 472 us; the launch traced here: 464 us
  waiting for transfers between devices  169 us (36%)
  starting transfers between devices  101 us (21%)
  Pallas kernels  91.9 us (19%)
  other arithmetic  51.9 us (11%)
  local copies, waits for them, and re-layouts  34.4 us (7%)
  between operations  15.6 us (3%)
    ppermute x15, waiting for transfers between devices, run(): lax.ppermute(to_left, 'row', left(nz - stop, nz - start))  73 us
    ppermute x15, starting transfers between devices, run(): self.from_left.append(lax.ppermute(to_right, 'row', right(start, stop)))  62.2 us
    pallas_call x5, Pallas kernels, run_grads(): pl.pallas_call(kernel, grid_spec=pltpu.PrefetchScalarGridSpec(num_scalar_...  51.1 us
    pallas_call x2, Pallas kernels, run_adds(): pl.pallas_call(kernel, grid_spec=pltpu.PrefetchScalarGridSpec(num_scalar_...  40.8 us
    ppermute x2, waiting for transfers between devices, finish(): lax.ppermute(total_of(keep[1], got[1], far), 'row', [(r, r ^ 4) for r in...  36.6 us
    ppermute x15, waiting for transfers between devices, run(): self.from_left.append(lax.ppermute(to_right, 'row', right(start, stop)))  29.6 us
    unnamed x146, local copies, waits for them, and re-layouts  22.7 us
    ppermute x15, starting transfers between devices, run(): lax.ppermute(to_left, 'row', left(nz - stop, nz - start))  19.9 us
  transfers between devices with their start and end apart: 57, of which 19 were waited for; matrix products, arithmetic and copies ran while one was open for 13% of the time, Pallas kernels for 20%

profile of v7, /device:TPU:0, one launch (start us, length us, event | category | flops | bytes accessed | tf_op | source)
XLA Modules:
  0.0 464.1 jit_solution(9241210943301882522)
XLA Ops:
  12.7 5.0 %collective-permute-start.1 = (bf16[3,12,128,128]{3,2,1,0:T(8,128)(2,1)S(1)}, bf16[3,12,128,128]{3,2,1,0:T(8,128)(2,1)S(1)}, u32[]{:S(2)}, u32[]{:S(2)}) collective-permute-start(bf16[3,12,128,128]{3,2,1,0:T(8,128)(2,1)S(1)} %get-tuple-element.152), channel_id=1, source_target_pairs={{0,8},{4,12},{8,16},{12,20},{16,24},{20,28},{1,9},{5,13},{9,17},{1... | collective-permute-start | bytes 3538952 | tf_op jit(solution)/shard_map/ppermute | solution.py:350
  19.0 23.8 %collective-permute-done.1 = bf16[3,12,128,128]{3,2,1,0:T(8,128)(2,1)S(1)} collective-permute-done((bf16[3,12,128,128]{3,2,1,0:T(8,128)(2,1)S(1)}, bf16[3,12,128,128]{3,2,1,0:T(8,128)(2,1)S(1)}, u32[]{:S(2)}, u32[]{:S(2)}) %collective-permute-start.1) | collective-permute-done | bytes 1179680 | tf_op jit(solution)/shard_map/ppermute | solution.py:350
  50.0 26.8 %collective-permute-done.4 = bf16[3,12,128,128]{3,2,1,0:T(8,128)(2,1)} collective-permute-done((bf16[3,12,128,128]{3,2,1,0:T(8,128)(2,1)S(1)}, bf16[3,12,128,128]{3,2,1,0:T(8,128)(2,1)}, u32[]{:S(2)}, u32[]{:S(2)}) %collective-permute-start.4) | collective-permute-done | bytes 1179680 | tf_op jit(solution)/shard_map/ppermute | solution.py:351
  81.2 23.8 %collective-permute-done.5 = bf16[3,12,128,128]{3,2,1,0:T(8,128)(2,1)} collective-permute-done((bf16[3,12,128,128]{3,2,1,0:T(8,128)(2,1)}, bf16[3,12,128,128]{3,2,1,0:T(8,128)(2,1)}, u32[]{:S(2)}, u32[]{:S(2)}) %collective-permute-start.5) | collective-permute-done | bytes 1179680 | tf_op jit(solution)/shard_map/ppermute | solution.py:351
  116.6 9.1 %ffn_grads.5 = (bf16[2,3,4,128,128]{4,3,2,1,0:T(8,128)(2,1)S(1)}, bf16[2,3,4,128,128]{4,3,2,1,0:T(8,128)(2,1)S(1)}, bf16[2,3,4,128,128]{4,3,2,1,0:T(8,128)(2,1)}...) custom-call(s32[681]{0:T(1024)S(1)} %concatenate.18.scal, bf16[4,2,256,2048]{3,2,1,0:T(8,128)(2,1)} %bitcast.283, ...), custom_call_target="tpu_custom_call" | custom-call | flops 1610612736 | bytes 25165824 | tf_op jit(solution)/shard_map/ffn_grads/pallas_call | solution.py:126
  132.9 5.5 %collective-permute-start.20 = (bf16[3,8,128,128]{3,2,1,0:T(8,128)(2,1)}, bf16[3,8,128,128]{3,2,1,0:T(8,128)(2,1)}, u32[]{:S(2)}, u32[]{:S(2)}) collective-permute-start(bf16[3,8,128,128]{3,2,1,0:T(8,128)(2,1)} %get-tuple-element.170), channel_id=1, source_target_pairs={{0,8},{4,12},{8,16},{12,20},{16,24},{20,28},{1,9},{5,13},{9,17},{1... | collective-permute-start | bytes 2359304 | tf_op jit(solution)/shard_map/ppermute | solution.py:350
  141.5 4.8 %collective-permute-start.11 = (bf16[3,4,128,128]{3,2,1,0:T(8,128)(2,1)S(1)}, bf16[3,4,128,128]{3,2,1,0:T(8,128)(2,1)S(1)}, u32[]{:S(2)}, u32[]{:S(2)}) collective-permute-start(bf16[3,4,128,128]{3,2,1,0:T(8,128)(2,1)S(1)} %get-tuple-element.150), channel_id=1, source_target_pairs={{0,8},{4,12},{8,16},{12,20},{16,24},{20,28},{1,9},{5,13},{9,17},{1... | collective-permute-start | bytes 1179656 | tf_op jit(solution)/shard_map/ppermute | solution.py:350
  146.3 12.7 %ffn_grads.6 = (bf16[2,3,8,128,128]{4,3,2,1,0:T(8,128)(2,1)S(1)}, bf16[2,3,8,128,128]{4,3,2,1,0:T(8,128)(2,1)S(1)}, bf16[2,3,8,128,128]{4,3,2,1,0:T(8,128)(2,1)}...) custom-call(s32[681]{0:T(1024)S(1)} %concatenate.18.scal, bf16[4,2,256,2048]{3,2,1,0:T(8,128)(2,1)} %bitcast.284, ...), custom_call_target="tpu_custom_call" | custom-call | flops 3221225472 | bytes 50331648 | tf_op jit(solution)/shard_map/ffn_grads/pallas_call | solution.py:126
  163.8 5.3 %collective-permute-done.22 = bf16[2,3,8,128,128]{4,3,2,1,0:T(8,128)(2,1)S(1)} collective-permute-done((bf16[2,3,8,128,128]{4,3,2,1,0:T(8,128)(2,1)}, bf16[2,3,8,128,128]{4,3,2,1,0:T(8,128)(2,1)S(1)}, u32[]{:S(2)}, u32[]{:S(2)}) %collective-permute-start.22) | collective-permute-done | bytes 1572896 | tf_op jit(solution)/shard_map/ppermute | solution.py:303
  169.1 4.8 %fusion.12 = (bf16[3,8,128,128]{3,2,1,0:T(8,128)(2,1)}, bf16[3,8,128,128]{3,2,1,0:T(8,128)(2,1)}) fusion(bf16[3,8,128,128]{3,2,1,0:T(8,128)(2,1)} %collective-permute-done.21, pred[]{:T(512)S(6)} %ge.15, bf16[2,3,8,128,128]{4,3,2,1,0:T(8,128)(2,1)S(1)} %collective-permute-done.22, bf16[2,3,8,128,128]{4,3,2,1,0:T(8,128)(2,1)S(1)} %get-tuple-element.75, ...), kind=kLoop, calls=%fused_computation.37 | loop fusion | flops 5505024 | bytes 6291458 | tf_op jit(solution)/shard_map/jit(_where)/select_n | solution.py:347
  175.2 5.9 %collective-permute-start.23 = (bf16[3,8,128,128]{3,2,1,0:T(8,128)(2,1)}, bf16[3,8,128,128]{3,2,1,0:T(8,128)(2,1)}, u32[]{:S(2)}, u32[]{:S(2)}) collective-permute-start(bf16[3,8,128,128]{3,2,1,0:T(8,128)(2,1)} %get-tuple-element.137), channel_id=1, source_target_pairs={{0,8},{4,12},{8,16},{12,20},{16,24},{20,28},{1,9},{5,13},{9,17},{1... | collective-permute-start | bytes 2359304 | tf_op jit(solution)/shard_map/ppermute | solution.py:350
  184.9 5.3 %collective-permute-start.14 = (bf16[3,4,128,128]{3,2,1,0:T(8,128)(2,1)S(1)}, bf16[3,4,128,128]{3,2,1,0:T(8,128)(2,1)}, u32[]{:S(2)}, u32[]{:S(2)}) collective-permute-start(bf16[3,4,128,128]{3,2,1,0:T(8,128)(2,1)S(1)} %get-tuple-element.148), channel_id=1, source_target_pairs={{0,8},{4,12},{8,16},{12,20},{16,24},{20,28},{1,9},{5,13},{9,17},{1... | collective-permute-start | bytes 1179656 | tf_op jit(solution)/shard_map/ppermute | solution.py:350
  190.2 6.7 %collective-permute-done.24 = bf16[3,8,128,128]{3,2,1,0:T(8,128)(2,1)} collective-permute-done((bf16[3,8,128,128]{3,2,1,0:T(8,128)(2,1)}, bf16[3,8,128,128]{3,2,1,0:T(8,128)(2,1)}, u32[]{:S(2)}, u32[]{:S(2)}) %collective-permute-start.24) | collective-permute-done | bytes 786464 | tf_op jit(solution)/shard_map/ppermute | solution.py:351
  198.4 4.4 fusion.14
  204.1 6.1 %collective-permute-start.28 = (bf16[3,8,128,128]{3,2,1,0:T(8,128)(2,1)}, bf16[3,8,128,128]{3,2,1,0:T(8,128)(2,1)}, u32[]{:S(2)}, u32[]{:S(2)}) collective-permute-start(bf16[3,8,128,128]{3,2,1,0:T(8,128)(2,1)} %get-tuple-element.135), channel_id=1, source_target_pairs={{0,8},{4,12},{8,16},{12,20},{16,24},{20,28},{1,9},{5,13},{9,17},{1... | collective-permute-start | bytes 2359304 | tf_op jit(solution)/shard_map/ppermute | solution.py:350
  210.3 17.5 %ffn_adds.2 = (f32[64,128,256]{2,1,0:T(8,128)}, f32[64,128,256]{2,1,0:T(8,128)}) custom-call(s32[681]{0:T(1024)} %copy-done.18, bf16[3,4,128,256]{3,2,1,0:T(8,128)(2,1)} %copy-done.13, bf16[2,3,12,128,128]{4,3,2,1,0:T(8,128)(2,1)} %copy-done.23, bf16[2,3,12,128,128]{4,3,2,1,0:T(8,128)(2,1)} %pad_maximum_fusion.1.refs_2_.refs_3_.refs_7_, ...), custom_call_target="tpu_custom_call" | custom-call | flops 2415919104 | bytes 50331648 | tf_op jit(solution)/shard_map/ffn_adds/pallas_call | solution.py:261
  235.5 4.2 fusion.11
  242.1 4.6 collective-permute-start.18
  247.6 8.1 %ffn_grads.7 = (bf16[2,3,4,128,128]{4,3,2,1,0:T(8,128)(2,1)S(1)}, bf16[2,3,4,128,128]{4,3,2,1,0:T(8,128)(2,1)S(1)}, bf16[2,3,4,128,128]{4,3,2,1,0:T(8,128)(2,1)S...) custom-call(s32[681]{0:T(1024)S(1)} %copy-done.19, bf16[4,2,256,2048]{3,2,1,0:T(8,128)(2,1)} %bitcast.285, ...), custom_call_target="tpu_custom_call" | custom-call | flops 1610612736 | bytes 25165824 | tf_op jit(solution)/shard_map/ffn_grads/pallas_call | solution.py:126
  258.1 4.1 collective-permute-start.33
  264.0 5.0 %collective-permute-start.31 = (bf16[3,4,128,128]{3,2,1,0:T(8,128)(2,1)S(1)}, bf16[3,4,128,128]{3,2,1,0:T(8,128)(2,1)S(1)}, u32[]{:S(2)}, u32[]{:S(2)}) collective-permute-start(bf16[3,4,128,128]{3,2,1,0:T(8,128)(2,1)S(1)} %get-tuple-element.146), channel_id=1, source_target_pairs={{0,8},{4,12},{8,16},{12,20},{16,24},{20,28},{1,9},{5,13},{9,17},{1... | collective-permute-start | bytes 1179656 | tf_op jit(solution)/shard_map/ppermute | solution.py:350
  269.0 12.5 %ffn_grads.8 = (bf16[2,3,8,128,128]{4,3,2,1,0:T(8,128)(2,1)S(1)}, bf16[2,3,8,128,128]{4,3,2,1,0:T(8,128)(2,1)S(1)}, bf16[2,3,8,128,128]{4,3,2,1,0:T(8,128)(2,1)S...) custom-call(s32[681]{0:T(1024)S(1)} %copy-done.19, bf16[4,2,256,2048]{3,2,1,0:T(8,128)(2,1)} %bitcast.286, ...), custom_call_target="tpu_custom_call" | custom-call | flops 3221225472 | bytes 50331648 | tf_op jit(solution)/shard_map/ffn_grads/pallas_call | solution.py:126
  284.7 4.6 collective-permute-start.38
  289.5 7.2 %collective-permute-done.37 = bf16[3,4,128,128]{3,2,1,0:T(8,128)(2,1)S(1)} collective-permute-done((bf16[3,4,128,128]{3,2,1,0:T(8,128)(2,1)S(1)}, bf16[3,4,128,128]{3,2,1,0:T(8,128)(2,1)S(1)}, u32[]{:S(2)}, u32[]{:S(2)}) %collective-permute-start.37) | collective-permute-done | bytes 393248 | tf_op jit(solution)/shard_map/ppermute | solution.py:351
  304.1 8.8 %ffn_grads.9 = (bf16[2,3,4,128,128]{4,3,2,1,0:T(8,128)(2,1)S(1)}, bf16[2,3,4,128,128]{4,3,2,1,0:T(8,128)(2,1)S(1)}, bf16[2,3,4,128,128]{4,3,2,1,0:T(8,128)(2,1)S...) custom-call(s32[681]{0:T(1024)S(1)} %copy-done.19, bf16[4,2,256,2048]{3,2,1,0:T(8,128)(2,1)} %bitcast.287, ...), custom_call_target="tpu_custom_call" | custom-call | flops 1610612736 | bytes 25165824 | tf_op jit(solution)/shard_map/ffn_grads/pallas_call | solution.py:126
  322.5 4.3 collective-permute-start.49
  326.8 23.3 %ffn_adds.3 = (bf16[2,16,128,256]{3,2,1,0:T(8,128)(2,1)}, bf16[2,16,128,256]{3,2,1,0:T(8,128)(2,1)}, bf16[2,16,128,256]{3,2,1,0:T(8,128)(2,1)}, bf16[2,8,128,256]{3,2,1,0:T(8,128)(2,1)}, bf16[2,8,128,256]{3,2,1,0:T(8,128)(2,1)}) custom-call(s32[681]{0:T(1024)} %copy-done.18, bf16[2,3,4,128,128]{4,3,2,1,0:T(8,128)(2,1)} %collective-permute-done.41.refs_0_, ...), custom_call_target="tpu_custom_call" | custom-call | flops 3221225472 | bytes 50331648 | tf_op jit(solution)/shard_map/ffn_adds/pallas_call | solution.py:261
  356.7 14.5 %collective-permute-done.49 = bf16[2,3,4,128,128]{4,3,2,1,0:T(8,128)(2,1)S(1)} collective-permute-done((bf16[2,3,4,128,128]{4,3,2,1,0:T(8,128)(2,1)S(1)}, bf16[2,3,4,128,128]{4,3,2,1,0:T(8,128)(2,1)S(1)}, u32[]{:S(2)}, u32[]{:S(2)}) %collective-permute-start.49) | collective-permute-done | bytes 786464 | tf_op jit(solution)/shard_map/ppermute | solution.py:374
  381.0 4.0 collective-permute-start.53
  386.8 9.3 %collective-permute-done.43 = bf16[2,8,128,256]{3,2,1,0:T(8,128)(2,1)S(1)} collective-permute-done((bf16[2,8,128,256]{3,2,1,0:T(8,128)(2,1)S(1)}, bf16[2,8,128,256]{3,2,1,0:T(8,128)(2,1)S(1)}, u32[]{:S(2)}, u32[]{:S(2)}) %collective-permute-start.43) | collective-permute-done | bytes 1048608 | tf_op jit(solution)/shard_map/ppermute | solution.py:300
  402.6 30.9 %collective-permute-done.53 = bf16[3,8,128,128]{3,2,1,0:T(8,128)(2,1)S(1)} collective-permute-done((bf16[3,8,128,128]{3,2,1,0:T(8,128)(2,1)S(1)}, bf16[3,8,128,128]{3,2,1,0:T(8,128)(2,1)S(1)}, u32[]{:S(2)}, u32[]{:S(2)}) %collective-permute-start.53) | collective-permute-done | bytes 786464 | tf_op jit(solution)/shard_map/ppermute | solution.py:381
  436.9 5.7 %collective-permute-done.55 = bf16[3,4,128,128]{3,2,1,0:T(8,128)(2,1)S(1)} collective-permute-done((bf16[3,4,128,128]{3,2,1,0:T(8,128)(2,1)S(1)}, bf16[3,4,128,128]{3,2,1,0:T(8,128)(2,1)S(1)}, u32[]{:S(2)}, u32[]{:S(2)}) %collective-permute-start.55) | collective-permute-done | bytes 393248 | tf_op jit(solution)/shard_map/ppermute | solution.py:381
  (294 shorter events, 130.1 us)
Async XLA Ops:
  7.2 109.5 %all-gather.3.cloned.1.call-start = ((), (), s32[]{:S(2)}) async-start(), calls=%async_computation | async-start | bytes 10485760 | tf_op jit(solution)/shard_map/all_gather | solution.py:402
  12.7 30.1 %collective-permute-start.1 = (bf16[3,12,128,128]{3,2,1,0:T(8,128)(2,1)S(1)}, bf16[3,12,128,128]{3,2,1,0:T(8,128)(2,1)S(1)}, u32[]{:S(2)}, u32[]{:S(2)}) collective-permute-start(bf16[3,12,128,128]{3,2,1,0:T(8,128)(2,1)S(1)} %get-tuple-element.152), channel_id=1, source_target_pairs={{0,8},{4,12},{8,16},{12,20},{16,24},{20,28},{1,9},{5,13},{9,17},{1... | collective-permute-start | bytes 3538952 | tf_op jit(solution)/shard_map/ppermute | solution.py:350
  17.7 29.3 %collective-permute-start.3 = (bf16[3,12,128,128]{3,2,1,0:T(8,128)(2,1)S(1)}, bf16[3,12,128,128]{3,2,1,0:T(8,128)(2,1)S(1)}, u32[]{:S(2)}, u32[]{:S(2)}) collective-permute-start(bf16[3,12,128,128]{3,2,1,0:T(8,128)(2,1)S(1)} %get-tuple-element.152), channel_id=1, source_target_pairs={{8,0},{12,4},{16,8},{20,12},{24,16},{28,20},{9,1},{13,5},{17,9},{2... | collective-permute-start | bytes 3538952 | tf_op jit(solution)/shard_map/ppermute | solution.py:351
  47.0 29.8 %collective-permute-start.4 = (bf16[3,12,128,128]{3,2,1,0:T(8,128)(2,1)S(1)}, bf16[3,12,128,128]{3,2,1,0:T(8,128)(2,1)}, u32[]{:S(2)}, u32[]{:S(2)}) collective-permute-start(bf16[3,12,128,128]{3,2,1,0:T(8,128)(2,1)S(1)} %collective-permute-done.3), channel_id=1, source_target_pairs={{8,0},{12,4},{16,8},{20,12},{9,1},{13,5},{17,9},{21,13},{10,2},{14... | collective-permute-start | bytes 3538952 | tf_op jit(solution)/shard_map/ppermute | solution.py:351
  48.3 31.5 %collective-permute-start.6 = (bf16[3,12,128,128]{3,2,1,0:T(8,128)(2,1)}, bf16[3,12,128,128]{3,2,1,0:T(8,128)(2,1)}, u32[]{:S(2)}, u32[]{:S(2)}) collective-permute-start(bf16[3,12,128,128]{3,2,1,0:T(8,128)(2,1)} %collective-permute-done.2), channel_id=1, source_target_pairs={{16,24},{20,28},{17,25},{21,29},{18,26},{22,30},{19,27},{23,31}} | collective-permute-start | bytes 3538952 | tf_op jit(solution)/shard_map/ppermute | solution.py:350
  76.8 28.2 %collective-permute-start.5 = (bf16[3,12,128,128]{3,2,1,0:T(8,128)(2,1)}, bf16[3,12,128,128]{3,2,1,0:T(8,128)(2,1)}, u32[]{:S(2)}, u32[]{:S(2)}) collective-permute-start(bf16[3,12,128,128]{3,2,1,0:T(8,128)(2,1)} %collective-permute-done.4), channel_id=1, source_target_pairs={{8,0},{12,4},{9,1},{13,5},{10,2},{14,6},{11,3},{15,7}} | collective-permute-start | bytes 3538952 | tf_op jit(solution)/shard_map/ppermute | solution.py:351
  79.7 36.8 %collective-permute-start.7 = (bf16[2,3,12,128,128]{4,3,2,1,0:T(8,128)(2,1)S(1)}, bf16[2,3,12,128,128]{4,3,2,1,0:T(8,128)(2,1)}, u32[]{:S(2)}, u32[]{:S(2)}) collective-permute-start(bf16[2,3,12,128,128]{4,3,2,1,0:T(8,128)(2,1)S(1)} %pad_maximum_fusion.refs_1_.refs_2_.refs_6_), channel_id=1, source_target_pairs={{0,4},{4,0},{8,12},{12,8},{16,20},{20,16},{24,28},{28,24},{1,5},{5... | collective-permute-start | bytes 7077896 | tf_op jit(solution)/shard_map/ppermute | solution.py:303
  131.6 27.4 %collective-permute-start.21 = (bf16[3,8,128,128]{3,2,1,0:T(8,128)(2,1)}, bf16[3,8,128,128]{3,2,1,0:T(8,128)(2,1)}, u32[]{:S(2)}, u32[]{:S(2)}) collective-permute-start(bf16[3,8,128,128]{3,2,1,0:T(8,128)(2,1)} %get-tuple-element.170), channel_id=1, source_target_pairs={{8,0},{12,4},{16,8},{20,12},{24,16},{28,20},{9,1},{13,5},{17,9},{2... | collective-permute-start | bytes 2359304 | tf_op jit(solution)/shard_map/ppermute | solution.py:351
  132.9 26.2 %collective-permute-start.20 = (bf16[3,8,128,128]{3,2,1,0:T(8,128)(2,1)}, bf16[3,8,128,128]{3,2,1,0:T(8,128)(2,1)}, u32[]{:S(2)}, u32[]{:S(2)}) collective-permute-start(bf16[3,8,128,128]{3,2,1,0:T(8,128)(2,1)} %get-tuple-element.170), channel_id=1, source_target_pairs={{0,8},{4,12},{8,16},{12,20},{16,24},{20,28},{1,9},{5,13},{9,17},{1... | collective-permute-start | bytes 2359304 | tf_op jit(solution)/shard_map/ppermute | solution.py:350
  163.3 26.9 %collective-permute-start.26 = (bf16[2,3,8,128,128]{4,3,2,1,0:T(8,128)(2,1)}, bf16[2,3,8,128,128]{4,3,2,1,0:T(8,128)(2,1)}, u32[]{:S(2)}, u32[]{:S(2)}) collective-permute-start(bf16[2,3,8,128,128]{4,3,2,1,0:T(8,128)(2,1)} %get-tuple-element.80), channel_id=1, source_target_pairs={{0,4},{4,0},{8,12},{12,8},{16,20},{20,16},{24,28},{28,24},{1,5},{5... | collective-permute-start | bytes 4718600 | tf_op jit(solution)/shard_map/ppermute | solution.py:303
  183.6 44.4 %collective-permute-start.15 = (bf16[3,4,128,128]{3,2,1,0:T(8,128)(2,1)}, bf16[3,4,128,128]{3,2,1,0:T(8,128)(2,1)S(1)}, u32[]{:S(2)}, u32[]{:S(2)}) collective-permute-start(bf16[3,4,128,128]{3,2,1,0:T(8,128)(2,1)} %get-tuple-element.147), channel_id=1, source_target_pairs={{8,0},{12,4},{16,8},{20,12},{24,16},{28,20},{9,1},{13,5},{17,9},{2... | collective-permute-start | bytes 1179656 | tf_op jit(solution)/shard_map/ppermute | solution.py:351
  184.9 43.1 %collective-permute-start.14 = (bf16[3,4,128,128]{3,2,1,0:T(8,128)(2,1)S(1)}, bf16[3,4,128,128]{3,2,1,0:T(8,128)(2,1)}, u32[]{:S(2)}, u32[]{:S(2)}) collective-permute-start(bf16[3,4,128,128]{3,2,1,0:T(8,128)(2,1)S(1)} %get-tuple-element.148), channel_id=1, source_target_pairs={{0,8},{4,12},{8,16},{12,20},{16,24},{20,28},{1,9},{5,13},{9,17},{1... | collective-permute-start | bytes 1179656 | tf_op jit(solution)/shard_map/ppermute | solution.py:350
  202.8 30.9 %collective-permute-start.27 = (bf16[3,8,128,128]{3,2,1,0:T(8,128)(2,1)}, bf16[3,8,128,128]{3,2,1,0:T(8,128)(2,1)S(1)}, u32[]{:S(2)}, u32[]{:S(2)}) collective-permute-start(bf16[3,8,128,128]{3,2,1,0:T(8,128)(2,1)} %get-tuple-element.134), channel_id=1, source_target_pairs={{8,0},{12,4},{16,8},{20,12},{24,16},{28,20},{9,1},{13,5},{17,9},{2... | collective-permute-start | bytes 2359304 | tf_op jit(solution)/shard_map/ppermute | solution.py:351
  204.1 29.6 %collective-permute-start.28 = (bf16[3,8,128,128]{3,2,1,0:T(8,128)(2,1)}, bf16[3,8,128,128]{3,2,1,0:T(8,128)(2,1)}, u32[]{:S(2)}, u32[]{:S(2)}) collective-permute-start(bf16[3,8,128,128]{3,2,1,0:T(8,128)(2,1)} %get-tuple-element.135), channel_id=1, source_target_pairs={{0,8},{4,12},{8,16},{12,20},{16,24},{20,28},{1,9},{5,13},{9,17},{1... | collective-permute-start | bytes 2359304 | tf_op jit(solution)/shard_map/ppermute | solution.py:350
  233.6 29.0 %collective-permute-start.29 = (bf16[2,3,8,128,128]{4,3,2,1,0:T(8,128)(2,1)S(1)}, bf16[2,3,8,128,128]{4,3,2,1,0:T(8,128)(2,1)S(1)}, u32[]{:S(2)}, u32[]{:S(2)}) collective-permute-start(bf16[2,3,8,128,128]{4,3,2,1,0:T(8,128)(2,1)S(1)} %pad_maximum_fusion.5.refs_2_.refs_9_), channel_id=1, source_target_pairs={{0,4},{4,0},{8,12},{12,8},{16,20},{20,16},{24,28},{28,24},{1,5},{5... | collective-permute-start | bytes 4718600 | tf_op jit(solution)/shard_map/ppermute | solution.py:303
  239.9 24.1 %collective-permute-start.30 = (bf16[2,3,8,128,128]{4,3,2,1,0:T(8,128)(2,1)S(1)}, bf16[2,3,8,128,128]{4,3,2,1,0:T(8,128)(2,1)S(1)}, u32[]{:S(2)}, u32[]{:S(2)}) collective-permute-start(bf16[2,3,8,128,128]{4,3,2,1,0:T(8,128)(2,1)S(1)} %pad_maximum_fusion.6.refs_3_.refs_10_), channel_id=1, source_target_pairs={{0,4},{4,0},{8,12},{12,8},{16,20},{20,16},{24,28},{28,24},{1,5},{5... | collective-permute-start | bytes 4718600 | tf_op jit(solution)/shard_map/ppermute | solution.py:303
  255.8 27.0 %collective-permute-start.36 = (bf16[2,3,4,128,128]{4,3,2,1,0:T(8,128)(2,1)S(1)}, bf16[2,3,4,128,128]{4,3,2,1,0:T(8,128)(2,1)S(1)}, u32[]{:S(2)}, u32[]{:S(2)}) collective-permute-start(bf16[2,3,4,128,128]{4,3,2,1,0:T(8,128)(2,1)S(1)} %get-tuple-element.86), channel_id=1, source_target_pairs={{0,4},{4,0},{8,12},{12,8},{16,20},{20,16},{24,28},{28,24},{1,5},{5... | collective-permute-start | bytes 2359304 | tf_op jit(solution)/shard_map/ppermute | solution.py:303
  256.3 26.4 %collective-permute-start.34 = (bf16[3,4,128,128]{3,2,1,0:T(8,128)(2,1)}, bf16[3,4,128,128]{3,2,1,0:T(8,128)(2,1)S(1)}, u32[]{:S(2)}, u32[]{:S(2)}) collective-permute-start(bf16[3,4,128,128]{3,2,1,0:T(8,128)(2,1)} %get-tuple-element.143), channel_id=1, source_target_pairs={{8,0},{12,4},{16,8},{20,12},{24,16},{28,20},{9,1},{13,5},{17,9},{2... | collective-permute-start | bytes 1179656 | tf_op jit(solution)/shard_map/ppermute | solution.py:351
  258.1 24.6 %collective-permute-start.33 = (bf16[3,4,128,128]{3,2,1,0:T(8,128)(2,1)S(1)}, bf16[3,4,128,128]{3,2,1,0:T(8,128)(2,1)S(1)}, u32[]{:S(2)}, u32[]{:S(2)}) collective-permute-start(bf16[3,4,128,128]{3,2,1,0:T(8,128)(2,1)S(1)} %get-tuple-element.144), channel_id=1, source_target_pairs={{0,8},{4,12},{8,16},{12,20},{16,24},{20,28},{1,9},{5,13},{9,17},{1... | collective-permute-start | bytes 1179656 | tf_op jit(solution)/shard_map/ppermute | solution.py:350
  299.8 50.2 %collective-permute-start.42 = (bf16[2,3,8,128,128]{4,3,2,1,0:T(8,128)(2,1)}, bf16[2,3,8,128,128]{4,3,2,1,0:T(8,128)(2,1)}, u32[]{:S(2)}, u32[]{:S(2)}) collective-permute-start(bf16[2,3,8,128,128]{4,3,2,1,0:T(8,128)(2,1)} %add_convert_fusion), channel_id=1, source_target_pairs={{0,8},{4,12},{8,0},{12,4},{16,24},{20,28},{24,16},{28,20},{1,9},{5... | collective-permute-start | bytes 4718600 | tf_op jit(solution)/shard_map/ppermute | solution.py:374
  315.8 61.5 %collective-permute-start.52 = (bf16[2,3,8,128,128]{4,3,2,1,0:T(8,128)(2,1)}, bf16[2,3,8,128,128]{4,3,2,1,0:T(8,128)(2,1)}, u32[]{:S(2)}, u32[]{:S(2)}) collective-permute-start(bf16[2,3,8,128,128]{4,3,2,1,0:T(8,128)(2,1)} %copy-done.20), channel_id=1, source_target_pairs={{0,4},{4,0},{8,12},{12,8},{16,20},{20,16},{24,28},{28,24},{1,5},{5... | collective-permute-start | bytes 4718600 | tf_op jit(solution)/shard_map/ppermute | solution.py:303
  317.7 36.5 %collective-permute-start.47 = (bf16[3,8,128,128]{3,2,1,0:T(8,128)(2,1)}, bf16[3,8,128,128]{3,2,1,0:T(8,128)(2,1)S(1)}, u32[]{:S(2)}, u32[]{:S(2)}) collective-permute-start(bf16[3,8,128,128]{3,2,1,0:T(8,128)(2,1)} %get-tuple-element.132), channel_id=1, source_target_pairs={{0,8},{4,12},{8,16},{12,20},{16,24},{20,28},{1,9},{5,13},{9,17},{1... | collective-permute-start | bytes 2359304 | tf_op jit(solution)/shard_map/ppermute | solution.py:350
  319.7 35.1 %collective-permute-start.48 = (bf16[3,8,128,128]{3,2,1,0:T(8,128)(2,1)S(1)}, bf16[3,8,128,128]{3,2,1,0:T(8,128)(2,1)}, u32[]{:S(2)}, u32[]{:S(2)}) collective-permute-start(bf16[3,8,128,128]{3,2,1,0:T(8,128)(2,1)S(1)} %copy-done.53), channel_id=1, source_target_pairs={{8,0},{12,4},{16,8},{20,12},{24,16},{28,20},{9,1},{13,5},{17,9},{2... | collective-permute-start | bytes 2359304 | tf_op jit(solution)/shard_map/ppermute | solution.py:351
  322.5 48.7 %collective-permute-start.49 = (bf16[2,3,4,128,128]{4,3,2,1,0:T(8,128)(2,1)S(1)}, bf16[2,3,4,128,128]{4,3,2,1,0:T(8,128)(2,1)S(1)}, u32[]{:S(2)}, u32[]{:S(2)}) collective-permute-start(bf16[2,3,4,128,128]{4,3,2,1,0:T(8,128)(2,1)S(1)} %add_convert_fusion.6), channel_id=1, source_target_pairs={{0,8},{4,12},{8,0},{12,4},{16,24},{20,28},{24,16},{28,20},{1,9},{5... | collective-permute-start | bytes 2359304 | tf_op jit(solution)/shard_map/ppermute | solution.py:374
  350.1 30.9 %collective-permute-start.45 = (bf16[2,8,128,256]{3,2,1,0:T(8,128)(2,1)}, bf16[2,8,128,256]{3,2,1,0:T(8,128)(2,1)S(1)}, u32[]{:S(2)}, u32[]{:S(2)}) collective-permute-start(bf16[2,8,128,256]{3,2,1,0:T(8,128)(2,1)} %get-tuple-element.104), channel_id=1, source_target_pairs={{0,1},{1,0},{2,3},{3,2},{4,5},{5,4},{6,7},{7,6},{8,9},{9,8},{10,11... | collective-permute-start | bytes 3145736 | tf_op jit(solution)/shard_map/ppermute | solution.py:300
  356.7 76.9 %collective-permute-start.54 = (bf16[2,3,4,128,128]{4,3,2,1,0:T(8,128)(2,1)S(1)}, bf16[2,3,4,128,128]{4,3,2,1,0:T(8,128)(2,1)S(1)}, u32[]{:S(2)}, u32[]{:S(2)}) collective-permute-start(bf16[2,3,4,128,128]{4,3,2,1,0:T(8,128)(2,1)S(1)} %copy-done.22), channel_id=1, source_target_pairs={{0,4},{4,0},{8,12},{12,8},{16,20},{20,16},{24,28},{28,24},{1,5},{5... | collective-permute-start | bytes 2359304 | tf_op jit(solution)/shard_map/ppermute | solution.py:303
  371.2 24.9 %collective-permute-start.43 = (bf16[2,8,128,256]{3,2,1,0:T(8,128)(2,1)S(1)}, bf16[2,8,128,256]{3,2,1,0:T(8,128)(2,1)S(1)}, u32[]{:S(2)}, u32[]{:S(2)}) collective-permute-start(bf16[2,8,128,256]{3,2,1,0:T(8,128)(2,1)S(1)} %copy-done.67), channel_id=1, source_target_pairs={{0,2},{1,3},{2,0},{3,1},{4,6},{5,7},{6,4},{7,5},{8,10},{9,11},{10,... | collective-permute-start | bytes 3145736 | tf_op jit(solution)/shard_map/ppermute | solution.py:300
  373.2 26.3 %collective-permute-start.50 = (bf16[3,4,128,128]{3,2,1,0:T(8,128)(2,1)S(1)}, bf16[3,4,128,128]{3,2,1,0:T(8,128)(2,1)S(1)}, u32[]{:S(2)}, u32[]{:S(2)}) collective-permute-start(bf16[3,4,128,128]{3,2,1,0:T(8,128)(2,1)S(1)} %get-tuple-element.139), channel_id=1, source_target_pairs={{0,8},{4,12},{8,16},{12,20},{16,24},{20,28},{1,9},{5,13},{9,17},{1... | collective-permute-start | bytes 1179656 | tf_op jit(solution)/shard_map/ppermute | solution.py:350
  377.2 24.5 %collective-permute-start.51 = (bf16[3,4,128,128]{3,2,1,0:T(8,128)(2,1)S(1)}, bf16[3,4,128,128]{3,2,1,0:T(8,128)(2,1)S(1)}, u32[]{:S(2)}, u32[]{:S(2)}) collective-permute-start(bf16[3,4,128,128]{3,2,1,0:T(8,128)(2,1)S(1)} %get-tuple-element.140), channel_id=1, source_target_pairs={{8,0},{12,4},{16,8},{20,12},{24,16},{28,20},{9,1},{13,5},{17,9},{2... | collective-permute-start | bytes 1179656 | tf_op jit(solution)/shard_map/ppermute | solution.py:351
  381.0 52.6 %collective-permute-start.53 = (bf16[3,8,128,128]{3,2,1,0:T(8,128)(2,1)S(1)}, bf16[3,8,128,128]{3,2,1,0:T(8,128)(2,1)S(1)}, u32[]{:S(2)}, u32[]{:S(2)}) collective-permute-start(bf16[3,8,128,128]{3,2,1,0:T(8,128)(2,1)S(1)} %fusion.15), channel_id=1, source_target_pairs={{0,16},{4,20},{8,24},{12,28},{16,0},{20,4},{24,8},{28,12},{1,17},{... | collective-permute-start | bytes 2359304 | tf_op jit(solution)/shard_map/ppermute | solution.py:381
  396.1 54.1 %collective-permute-start.46 = (bf16[2,16,128,256]{3,2,1,0:T(8,128)(2,1)}, bf16[2,16,128,256]{3,2,1,0:T(8,128)(2,1)}, u32[]{:S(2)}, u32[]{:S(2)}) collective-permute-start(bf16[2,16,128,256]{3,2,1,0:T(8,128)(2,1)} %pad_maximum_fusion.4), channel_id=1, source_target_pairs={{0,2},{1,3},{2,0},{3,1},{4,6},{5,7},{6,4},{7,5},{8,10},{9,11},{10,... | collective-permute-start | bytes 6291464 | tf_op jit(solution)/shard_map/ppermute | solution.py:300
  399.5 50.8 %collective-permute-start.44 = (bf16[2,16,128,256]{3,2,1,0:T(8,128)(2,1)}, bf16[2,16,128,256]{3,2,1,0:T(8,128)(2,1)}, u32[]{:S(2)}, u32[]{:S(2)}) collective-permute-start(bf16[2,16,128,256]{3,2,1,0:T(8,128)(2,1)} %pad_maximum_fusion.3), channel_id=1, source_target_pairs={{0,1},{1,0},{2,3},{3,2},{4,5},{5,4},{6,7},{7,6},{8,9},{9,8},{10,11... | collective-permute-start | bytes 6291464 | tf_op jit(solution)/shard_map/ppermute | solution.py:300
  (93 other events, 862.5 us)
Sparse Core Ops, SparseCore 0:
  10.4 90.2 all-gather.2
